TPU v7x, 256 devices: a whole 4x4x8 slice. The times are simulated.
256 devices in a mesh: blk: 32 (over z, y), zero: 8 (over x, core).
Axes of the slice: x: 4, y: 4, z: 8, core: 2. Of those that a mesh axis runs over, the one named last changes fastest.
Arguments:
- grads: bfloat16 [16, 512, 6144], P('zero', 'blk'), may hold values from -4200 to 4200
- owners: int32 [8, 24, 1], P('zero'), may hold values from 0 to 31; in each aligned block of 24 rows (0 to 23, 24 to 47, ..., all dimensions but the last counted through in order) at most 2 rows name the same one
- left_stats: float32 [8, 24, 512, 512], P('zero', None, 'blk'), may hold values from -1.5 to 50, as said below
- right_stats: float32 [8, 24, 512, 512], P('zero', None, 'blk'), may hold values from -1.5 to 50, as said below
- second_moment: float32 [16, 512, 6144], P('zero', 'blk'), may hold values from 0.01 to 0.2
- roots: bfloat16 [8, 2, 64, 512, 512], P('zero', None, 'blk'), may hold values from -0.02 to 0.45, as said below
Outputs:
- update: bfloat16 [16, 512, 6144], P('zero', 'blk')
- new_second: float32 [16, 512, 6144], P('zero', 'blk')
- new_left: float32 [8, 24, 512, 512], P('zero', None, 'blk')
- new_right: float32 [8, 24, 512, 512], P('zero', None, 'blk')
- new_roots: bfloat16 [8, 2, 64, 512, 512], P('zero', None, 'blk')
Inputs may be any that keep to these rules, and one draw needn't show every extreme that they name: `owners`: within the 24 blocks of one index of zero no owner is named by more than 2 blocks, and in some index of zero an owner is named by exactly 2. `left_stats`: each block is symmetric. `right_stats`: each block is symmetric. `roots`: each block is symmetric.
All inputs are finite; a program needn't handle non-finite values.
Results may differ from a plain program's by a relative error of at most 0.0068.
Values may be sent and summed in bfloat16 or wider, within the bound.
No kernel may reach another device: no remote copies, remote signals or barrier semaphores. Data moves between devices by JAX's collectives and lax.ppermute only.
A program may use at most 64 MiB of HBM per device.

v0:
```python
import math

import jax
import jax.numpy as jnp
from jax import lax
from jax.sharding import PartitionSpec as P

BETA = 0.95
HIGHEST = lax.Precision.HIGHEST


def batched(former, latter):
    return jnp.einsum(
        "sij,sjk->sik", former, latter, precision=HIGHEST, preferred_element_type=jnp.float32
    )


def inverse_root(previous, statistic):
    seed_wide = previous.astype(jnp.float32)
    seed_square = batched(seed_wide, seed_wide)
    seed_fourth = batched(seed_square, seed_square)
    product = batched(seed_fourth, statistic)
    identity = jnp.eye(statistic.shape[-1], dtype=jnp.float32)
    newton_step = (5.0 * identity - product) * 0.25
    return batched(seed_wide, newton_step).astype(jnp.bfloat16)


def precondition(blocks, left_old, right_old, weight, left_seed, right_seed, factor):
    gram_left = jnp.einsum("sij,skj->sik", blocks, blocks, preferred_element_type=jnp.float32)
    gram_right = jnp.einsum("sji,sjk->sik", blocks, blocks, preferred_element_type=jnp.float32)
    left_new = BETA * left_old + factor * gram_left
    right_new = BETA * right_old + factor * gram_right
    left_root = inverse_root(left_seed, left_new)
    right_root = inverse_root(right_seed, right_new)
    left_applied = jnp.einsum(
        "sij,sjk->sik", left_root, blocks, preferred_element_type=jnp.float32
    ).astype(jnp.bfloat16)
    direction = jnp.einsum(
        "sij,sjk->sik", left_applied, right_root, preferred_element_type=jnp.float32
    ).astype(jnp.bfloat16)
    direction_wide = direction.astype(jnp.float32)
    square_sum = jnp.sum(direction_wide * direction_wide, axis=(1, 2))
    graft_ratio = jnp.sqrt(weight) / (jnp.sqrt(square_sum) + 1e-06)
    update = (direction_wide * graft_ratio[:, None, None]).astype(jnp.bfloat16)
    return (left_new, right_new, left_root, right_root, update)


def by_slot(values, source, filled):
    taken = jnp.take(values, source, axis=0)
    keeper = filled.reshape((-1,) + (1,) * (values.ndim - 1))
    return jnp.where(keeper, taken, jnp.zeros_like(taken))


def local(grads, owners, left_stats, right_stats, second_moment, roots):
    devices = lax.axis_size("blk")
    rows_dev, piece_rows, width = grads.shape
    block_order = left_stats.shape[-1]
    col_blocks = width // block_order
    block_count = rows_dev * col_blocks
    slot_count = roots.shape[2]
    widened = grads.astype(jnp.float32)
    grand_total = lax.psum(jnp.sum(widened * widened), ("blk", "zero"))
    entries = rows_dev * lax.axis_size("zero") * block_order * width
    clip_scale = jnp.minimum(1.0, math.sqrt(entries) / (jnp.sqrt(grand_total) + 1e-06))
    clipped = widened * clip_scale
    new_second = 0.95 * second_moment + 0.05 * clipped * clipped
    adam_step = clipped / (jnp.sqrt(new_second) + 1e-08)
    adam_part = jnp.sum(
        (adam_step * adam_step).reshape(rows_dev, piece_rows, col_blocks, block_order), axis=(1, 3)
    ).reshape(block_count)
    pieces = (
        grads.reshape(rows_dev, piece_rows, col_blocks, block_order)
        .transpose(0, 2, 1, 3)
        .reshape(block_count, piece_rows, block_order)
    )
    left_pieces = left_stats[0]
    right_pieces = right_stats[0]
    factor = 0.05 * clip_scale * clip_scale
    owner_of = owners[0, :, 0]
    positions = jnp.arange(block_count, dtype=jnp.int32)
    same_owner = (owner_of[:, None] == owner_of[None, :]) & (
        positions[None, :] < positions[:, None]
    )
    slot_of = jnp.sum(same_owner.astype(jnp.int32), axis=1)
    position = slot_of * devices + owner_of
    slot_grid = jnp.arange(slot_count * devices, dtype=jnp.int32)
    matches = position[None, :] == slot_grid[:, None]
    filled = jnp.any(matches, axis=1)
    source = jnp.sum(jnp.where(matches, positions[None, :], 0), axis=1)
    owner_load = jnp.sum((owner_of == lax.axis_index("blk")).astype(jnp.int32))
    live_slots = jnp.arange(slot_count) < owner_load
    home_roots = roots[0]
    split_shape = (slot_count, devices, piece_rows, block_order)
    square_shape = (slot_count, block_order, block_order)
    flat_shape = (slot_count * devices, piece_rows, block_order)
    grad_out = by_slot(pieces, source, filled).reshape(split_shape)
    left_out = by_slot(left_pieces, source, filled).reshape(split_shape)
    right_out = by_slot(right_pieces, source, filled).reshape(split_shape)
    adam_out = by_slot(adam_part, source, filled).reshape(slot_count, devices)
    grad_in = lax.all_to_all(grad_out, "blk", split_axis=1, concat_axis=1, tiled=True)
    left_in, right_in, adam_in = (
        lax.all_to_all(left_out, "blk", split_axis=1, concat_axis=1, tiled=True),
        lax.all_to_all(right_out, "blk", split_axis=1, concat_axis=1, tiled=True),
        lax.all_to_all(adam_out, "blk", split_axis=1, concat_axis=1, tiled=True),
    )
    left_new, right_new, left_root, right_root, update = precondition(
        grad_in.reshape(square_shape),
        left_in.reshape(square_shape),
        right_in.reshape(square_shape),
        jnp.sum(adam_in, axis=1),
        home_roots[0],
        home_roots[1],
        factor,
    )
    fresh_roots = jnp.stack([left_root, right_root])
    kept_roots = jnp.where(live_slots[None, :, None, None], fresh_roots, home_roots)
    returned = lax.all_to_all(
        update.reshape(split_shape), "blk", split_axis=1, concat_axis=1, tiled=True
    )
    left_back, right_back = (
        lax.all_to_all(
            left_new.reshape(split_shape).astype(jnp.bfloat16),
            "blk",
            split_axis=1,
            concat_axis=1,
            tiled=True,
        ).astype(jnp.float32),
        lax.all_to_all(
            right_new.reshape(split_shape).astype(jnp.bfloat16),
            "blk",
            split_axis=1,
            concat_axis=1,
            tiled=True,
        ).astype(jnp.float32),
    )
    update_pieces = jnp.take(returned.reshape(flat_shape), position, axis=0)
    left_final = jnp.take(left_back.reshape(flat_shape), position, axis=0)
    right_final = jnp.take(right_back.reshape(flat_shape), position, axis=0)
    update_out = (
        update_pieces.reshape(rows_dev, col_blocks, piece_rows, block_order)
        .transpose(0, 2, 1, 3)
        .reshape(rows_dev, piece_rows, width)
    )
    return (update_out, new_second, left_final[None], right_final[None], kept_roots[None])


def solution(mesh):
    placed = (
        P("zero", "blk", None),
        P("zero", None, None),
        P("zero", None, "blk", None),
        P("zero", None, "blk", None),
        P("zero", "blk", None),
        P("zero", None, "blk", None, None),
    )
    return jax.shard_map(
        local,
        mesh=mesh,
        in_specs=placed,
        out_specs=(
            P("zero", "blk", None),
            P("zero", "blk", None),
            P("zero", None, "blk", None),
            P("zero", None, "blk", None),
            P("zero", None, "blk", None, None),
        ),
        check_vma=False,
    )
```

profile of v0, /device:TPU:4, one launch (start us, length us, event | category | flops | bytes accessed | tf_op | source)
XLA Modules:
  0.0 344.6 jit_solution(16998052873343620706)
XLA Ops:
  2.5 1.8 fusion.32
  4.4 79.0 %psum.7 = f32[]{:T(128)} all-reduce(f32[]{:T(128)} %fusion.32), channel_id=1, replica_groups=mesh['blk'=32,'zero'=8] {'blk','zero'}, use_global_device_ids=true, to_apply=%region_4.6 | all-reduce | flops 1 | bytes 8 | tf_op jit(solution)/shard_map/psum | solution.py:62
  84.1 2.6 fusion.34
  88.6 5.3 %all-to-all-start.3 = ((f32[2,32,1]{0,2,1:T(1,128)}), f32[2,32,1]{0,2,1:T(1,128)S(1)}, u32[]{:S(2)}, u32[]{:S(2)}) async-start(f32[2,32,1]{0,2,1:T(1,128)} %copy.73), calls=%async_computation.3 | async-start | bytes 32768 | tf_op jit(solution)/shard_map/all_to_all | solution.py:104
  95.4 1.2 fusion.20
  96.6 6.9 %all-to-all-done.3 = f32[2,32,1]{0,2,1:T(1,128)S(1)} async-done(((f32[2,32,1]{0,2,1:T(1,128)}), f32[2,32,1]{0,2,1:T(1,128)S(1)}, u32[]{:S(2)}, u32[]{:S(2)}) %all-to-all-start.3) | async-done | bytes 288 | tf_op jit(solution)/shard_map/all_to_all | solution.py:104
  103.5 3.9 %all-to-all-start.1 = ((bf16[2,32,16,512]{3,2,0,1:T(8,128)(2,1)}), bf16[2,32,16,512]{3,2,0,1:T(8,128)(2,1)S(1)}, u32[]{:S(2)}, u32[]{:S(2)}) async-start(bf16[2,32,16,512]{3,2,0,1:T(8,128)(2,1)} %fusion.20), calls=%async_computation.1 | async-start | bytes 2097152 | tf_op jit(solution)/shard_map/all_to_all | solution.py:100
  107.5 2.0 gather_fusion.3
  109.5 2.0 gather_fusion.4
  111.6 2.7 select_select_fusion.1
  114.3 1.5 copy.69
  115.8 18.9 %all-to-all-done.1 = bf16[2,32,16,512]{3,2,0,1:T(8,128)(2,1)S(1)} async-done(((bf16[2,32,16,512]{3,2,0,1:T(8,128)(2,1)}), bf16[2,32,16,512]{3,2,0,1:T(8,128)(2,1)S(1)}, u32[]{:S(2)}, u32[]{:S(2)}) %all-to-all-start.1) | async-done | bytes 1048608 | tf_op jit(solution)/shard_map/all_to_all | solution.py:100
  135.7 5.4 %all-to-all-start.2 = ((f32[2,32,16,512]{3,2,0,1:T(8,128)}), f32[2,32,16,512]{3,2,0,1:T(8,128)}, u32[]{:S(2)}, u32[]{:S(2)}) async-start(f32[2,32,16,512]{3,2,0,1:T(8,128)} %copy.69), calls=%async_computation.2 | async-start | bytes 4194304 | tf_op jit(solution)/shard_map/all_to_all | solution.py:103
  141.1 1.5 copy.60
  142.6 47.1 %all-to-all-done.2 = f32[2,32,16,512]{3,2,0,1:T(8,128)} async-done(((f32[2,32,16,512]{3,2,0,1:T(8,128)}), f32[2,32,16,512]{3,2,0,1:T(8,128)}, u32[]{:S(2)}, u32[]{:S(2)}) %all-to-all-start.2) | async-done | bytes 2097184 | tf_op jit(solution)/shard_map/all_to_all | solution.py:103
  189.6 6.1 %all-to-all-start = ((f32[2,32,16,512]{3,2,0,1:T(8,128)}), f32[2,32,16,512]{3,2,0,1:T(8,128)}, u32[]{:S(2)}, u32[]{:S(2)}) async-start(f32[2,32,16,512]{3,2,0,1:T(8,128)} %copy.60), calls=%async_computation | async-start | bytes 4194304 | tf_op jit(solution)/shard_map/all_to_all | solution.py:102
  195.7 2.0 fusion.18
  197.8 1.3 copy.66
  199.1 1.8 broadcast_multiply_fusion
  201.2 2.1 fusion.44
  204.4 38.9 %all-to-all-done = f32[2,32,16,512]{3,2,0,1:T(8,128)} async-done(((f32[2,32,16,512]{3,2,0,1:T(8,128)}), f32[2,32,16,512]{3,2,0,1:T(8,128)}, u32[]{:S(2)}, u32[]{:S(2)}) %all-to-all-start) | async-done | bytes 2097184 | tf_op jit(solution)/shard_map/all_to_all | solution.py:102
  243.3 6.2 %all-to-all-start.6 = ((bf16[2,32,16,512]{3,2,0,1:T(8,128)(2,1)}), bf16[2,32,16,512]{3,2,0,1:T(8,128)(2,1)}, u32[]{:S(2)}, u32[]{:S(2)}) async-start(bf16[2,32,16,512]{3,2,0,1:T(8,128)(2,1)} %copy.79), calls=%async_computation.6 | async-start | bytes 2097152 | tf_op jit(solution)/shard_map/all_to_all | solution.py:128
  249.5 2.4 copy.81
  253.3 1.1 fusion.25
  255.2 4.9 %fusion.46 = f32[2,512,512]{2,1,0:T(8,128)} fusion(f32[2,512,512]{2,1,0:T(8,128)S(1)} %copy-done.3), kind=kOutput, calls=%fused_computation.95 | convolution fusion | flops 3221225472 | bytes 4194304 | tf_op jit(solution)/shard_map/sij,sjk->sik/dot_general | solution.py:13
  260.1 4.8 %fusion.48 = f32[2,512,512]{2,1,0:T(8,128)} fusion(f32[2,512,512]{2,1,0:T(8,128)S(1)} %fusion.15), kind=kOutput, calls=%fused_computation.97 | convolution fusion | flops 3221225472 | bytes 4194304 | tf_op jit(solution)/shard_map/sij,sjk->sik/dot_general | solution.py:13
  265.0 1.8 broadcast_multiply_fusion.1
  267.2 2.1 fusion.45
  269.2 1.0 copy.77
  270.3 4.5 %all-to-all-done.6 = bf16[2,32,16,512]{3,2,0,1:T(8,128)(2,1)} async-done(((bf16[2,32,16,512]{3,2,0,1:T(8,128)(2,1)}), bf16[2,32,16,512]{3,2,0,1:T(8,128)(2,1)}, u32[]{:S(2)}, u32[]{:S(2)}) %all-to-all-start.6) | async-done | bytes 1048608 | tf_op jit(solution)/shard_map/all_to_all | solution.py:128
  274.8 5.7 %all-to-all-start.5 = ((bf16[2,32,16,512]{3,2,0,1:T(8,128)(2,1)}), bf16[2,32,16,512]{3,2,0,1:T(8,128)(2,1)}, u32[]{:S(2)}, u32[]{:S(2)}) async-start(bf16[2,32,16,512]{3,2,0,1:T(8,128)(2,1)} %copy.77), calls=%async_computation.5 | async-start | bytes 2097152 | tf_op jit(solution)/shard_map/all_to_all | solution.py:121
  280.6 5.8 %fusion.47 = f32[2,512,512]{2,1,0:T(8,128)S(1)} fusion(f32[2,512,512]{2,1,0:T(8,128)} %fusion.46, f32[2,512,512]{2,1,0:T(8,128)} %get-tuple-element.45), kind=kOutput, calls=%fused_computation.96 | convolution fusion | flops 3221225472 | bytes 6291456 | tf_op jit(solution)/shard_map/sij,sjk->sik/dot_general | solution.py:13
  286.4 4.5 %fusion.8 = bf16[2,512,512]{2,1,0:T(8,128)(2,1)} fusion(f32[2,512,512]{2,1,0:T(8,128)S(1)} %fusion.47, f32[512,512]{1,0:T(8,128)S(1)} %copy-done.4, bf16[1,2,2,512,512]{4,3,2,1,0:T(8,128)(2,1)S(1)} %copy-done.2), kind=kOutput, calls=%fused_computation.22 | convolution fusion | flops 3222798336 | bytes 5242880 | tf_op jit(solution)/shard_map/sij,sjk->sik/dot_general | solution.py:13
  290.9 3.5 %fusion.49 = f32[2,512,512]{2,1,0:T(8,128)S(1)} fusion(f32[2,512,512]{2,1,0:T(8,128)S(1)} %copy-done.5, f32[2,512,512]{2,1,0:T(8,128)S(1)} %copy-done.7), kind=kOutput, calls=%fused_computation.98 | convolution fusion | flops 3221225472 | bytes 6291456 | tf_op jit(solution)/shard_map/sij,sjk->sik/dot_general | solution.py:13
  294.5 4.8 %fusion.11 = bf16[2,512,512]{2,1,0:T(8,128)(2,1)} fusion(f32[2,512,512]{2,1,0:T(8,128)S(1)} %fusion.49, f32[512,512]{1,0:T(8,128)S(1)} %copy-done.4, bf16[1,2,2,512,512]{4,3,2,1,0:T(8,128)(2,1)S(1)} %copy-done.2), kind=kOutput, calls=%fused_computation.23 | convolution fusion | flops 3222798336 | bytes 5242880 | tf_op jit(solution)/shard_map/sij,sjk->sik/dot_general | solution.py:13
  299.3 3.1 fusion
  302.8 1.1 copy.74
  303.9 1.4 all-to-all-done.5
  305.3 8.5 %all-to-all-start.4 = ((bf16[2,32,16,512]{3,2,0,1:T(8,128)(2,1)}), bf16[2,32,16,512]{3,2,0,1:T(8,128)(2,1)}, u32[]{:S(2)}, u32[]{:S(2)}) async-start(bf16[2,32,16,512]{3,2,0,1:T(8,128)(2,1)} %copy.74), calls=%async_computation.4 | async-start | bytes 2097152 | tf_op jit(solution)/shard_map/all_to_all | solution.py:117
  315.2 2.9 maximum_select_fusion
  318.1 4.1 %copy.82 = bf16[1,2,2,512,512]{4,3,2,1,0:T(8,128)(2,1)} copy(bf16[1,2,2,512,512]{3,4,2,1,0:T(8,128)(2,1)} %maximum_select_fusion) | data formatting | bytes 4194304
  322.3 1.3 copy.80
  324.5 1.3 copy.78
  326.2 1.5 gather_fusion.5
  327.7 10.6 %all-to-all-done.4 = bf16[2,32,16,512]{3,2,0,1:T(8,128)(2,1)} async-done(((bf16[2,32,16,512]{3,2,0,1:T(8,128)(2,1)}), bf16[2,32,16,512]{3,2,0,1:T(8,128)(2,1)}, u32[]{:S(2)}, u32[]{:S(2)}) %all-to-all-start.4) | async-done | bytes 1048608 | tf_op jit(solution)/shard_map/all_to_all | solution.py:117
  338.3 2.3 copy.75
  340.5 1.8 gather_fusion.2
  343.3 1.3 select_bitcast_fusion
  (78 shorter events, 14.2 us)
Async XLA Ops:
  0.6 106.9 %copy-start = (f32[1,24,16,512]{3,2,1,0:T(8,128)S(1)}, f32[1,24,16,512]{3,2,1,0:T(8,128)}, u32[]{:S(2)}) copy-start(f32[1,24,16,512]{3,2,1,0:T(8,128)} %param.12) | copy-start | bytes 2359300
  0.6 93.2 %copy-start.11 = (bf16[2,16,6144]{2,1,0:T(8,128)(2,1)S(1)}, bf16[2,16,6144]{2,1,0:T(8,128)(2,1)}, u32[]{:S(2)}) copy-start(bf16[2,16,6144]{2,1,0:T(8,128)(2,1)} %param.10) | copy-start | bytes 1179652
  88.6 15.0 %all-to-all-start.3 = ((f32[2,32,1]{0,2,1:T(1,128)}), f32[2,32,1]{0,2,1:T(1,128)S(1)}, u32[]{:S(2)}, u32[]{:S(2)}) async-start(f32[2,32,1]{0,2,1:T(1,128)} %copy.73), calls=%async_computation.3 | async-start | bytes 32768 | tf_op jit(solution)/shard_map/all_to_all | solution.py:104
  103.5 31.2 %all-to-all-start.1 = ((bf16[2,32,16,512]{3,2,0,1:T(8,128)(2,1)}), bf16[2,32,16,512]{3,2,0,1:T(8,128)(2,1)S(1)}, u32[]{:S(2)}, u32[]{:S(2)}) async-start(bf16[2,32,16,512]{3,2,0,1:T(8,128)(2,1)} %fusion.20), calls=%async_computation.1 | async-start | bytes 2097152 | tf_op jit(solution)/shard_map/all_to_all | solution.py:100
  107.5 2.0 copy-start.8
  134.7 1.0 copy-start.10
  135.7 53.9 %all-to-all-start.2 = ((f32[2,32,16,512]{3,2,0,1:T(8,128)}), f32[2,32,16,512]{3,2,0,1:T(8,128)}, u32[]{:S(2)}, u32[]{:S(2)}) async-start(f32[2,32,16,512]{3,2,0,1:T(8,128)} %copy.69), calls=%async_computation.2 | async-start | bytes 4194304 | tf_op jit(solution)/shard_map/all_to_all | solution.py:103
  142.6 53.1 %copy-start.2 = (bf16[1,2,2,512,512]{4,3,2,1,0:T(8,128)(2,1)S(1)}, bf16[1,2,2,512,512]{4,3,2,1,0:T(8,128)(2,1)}, u32[]{:S(2)}) copy-start(bf16[1,2,2,512,512]{4,3,2,1,0:T(8,128)(2,1)} %param.15) | copy-start | bytes 6291460
  189.6 53.6 %all-to-all-start = ((f32[2,32,16,512]{3,2,0,1:T(8,128)}), f32[2,32,16,512]{3,2,0,1:T(8,128)}, u32[]{:S(2)}, u32[]{:S(2)}) async-start(f32[2,32,16,512]{3,2,0,1:T(8,128)} %copy.60), calls=%async_computation | async-start | bytes 4194304 | tf_op jit(solution)/shard_map/all_to_all | solution.py:102
  243.3 31.5 %all-to-all-start.6 = ((bf16[2,32,16,512]{3,2,0,1:T(8,128)(2,1)}), bf16[2,32,16,512]{3,2,0,1:T(8,128)(2,1)}, u32[]{:S(2)}, u32[]{:S(2)}) async-start(bf16[2,32,16,512]{3,2,0,1:T(8,128)(2,1)} %copy.79), calls=%async_computation.6 | async-start | bytes 2097152 | tf_op jit(solution)/shard_map/all_to_all | solution.py:128
  249.5 3.0 copy-start.13
  253.3 2.0 copy-start.3
  274.8 30.5 %all-to-all-start.5 = ((bf16[2,32,16,512]{3,2,0,1:T(8,128)(2,1)}), bf16[2,32,16,512]{3,2,0,1:T(8,128)(2,1)}, u32[]{:S(2)}, u32[]{:S(2)}) async-start(bf16[2,32,16,512]{3,2,0,1:T(8,128)(2,1)} %copy.77), calls=%async_computation.5 | async-start | bytes 2097152 | tf_op jit(solution)/shard_map/all_to_all | solution.py:121
  280.6 5.9 %copy-start.4 = (f32[512,512]{1,0:T(8,128)S(1)}, f32[512,512]{1,0:T(8,128)}, u32[]{:S(2)}) copy-start(f32[512,512]{1,0:T(8,128)} %fusion.25) | copy-start | bytes 3145732
  286.4 4.5 %copy-start.5 = (f32[2,512,512]{2,1,0:T(8,128)S(1)}, f32[2,512,512]{2,1,0:T(8,128)}, u32[]{:S(2)}) copy-start(f32[2,512,512]{2,1,0:T(8,128)} %fusion.48) | copy-start | bytes 6291460
  286.4 4.5 %copy-start.7 = (f32[2,512,512]{2,1,0:T(8,128)S(1)}, f32[2,512,512]{2,1,0:T(8,128)}, u32[]{:S(2)}) copy-start(f32[2,512,512]{2,1,0:T(8,128)} %get-tuple-element.43) | copy-start | bytes 6291460
  302.8 12.5 %copy-start.6 = (bf16[1,2,2,512,512]{3,4,2,1,0:T(8,128)(2,1)S(1)}, bf16[1,2,2,512,512]{3,4,2,1,0:T(8,128)(2,1)}, u32[]{:S(2)}) copy-start(bf16[1,2,2,512,512]{3,4,2,1,0:T(8,128)(2,1)} %copy.81) | copy-start | bytes 6291460
  302.8 12.5 %copy-start.9 = (bf16[2,512,512]{2,1,0:T(8,128)(2,1)S(1)}, bf16[2,512,512]{2,1,0:T(8,128)(2,1)}, u32[]{:S(2)}) copy-start(bf16[2,512,512]{2,1,0:T(8,128)(2,1)} %fusion.8) | copy-start | bytes 3145732
  305.3 32.9 %all-to-all-start.4 = ((bf16[2,32,16,512]{3,2,0,1:T(8,128)(2,1)}), bf16[2,32,16,512]{3,2,0,1:T(8,128)(2,1)}, u32[]{:S(2)}, u32[]{:S(2)}) async-start(bf16[2,32,16,512]{3,2,0,1:T(8,128)(2,1)} %copy.74), calls=%async_computation.4 | async-start | bytes 2097152 | tf_op jit(solution)/shard_map/all_to_all | solution.py:117
  327.7 15.6 %copy-start.12 = (f32[24,16,512]{2,1,0:T(8,128)S(1)}, f32[24,16,512]{2,1,0:T(8,128)}, u32[]{:S(2)}) copy-start(f32[24,16,512]{2,1,0:T(8,128)} %gather_fusion.5) | copy-start | bytes 2359300
  342.3 2.2 copy-start.1
where the time goes:
time: 348 us; the launch traced here: 345 us
  waiting for transfers between devices  128 us (37%)
  blocking collectives  79 us (23%)
  starting transfers between devices  41.2 us (12%)
  matrix products  38.4 us (11%)
  local copies, waits for them, and re-layouts  33.4 us (10%)
  other arithmetic  22.5 us (6%)
    psum x1, blocking collectives, local(): grand_total = lax.psum(jnp.sum(widened * widened), ('blk', 'zero'))  79 us
    all_to_all x1, waiting for transfers between devices, local(): lax.all_to_all(right_out, 'blk', split_axis=1, concat_axis=1, tiled=True)  47.1 us
    all_to_all x1, waiting for transfers between devices, local(): lax.all_to_all(left_out, 'blk', split_axis=1, concat_axis=1, tiled=True)  38.9 us
    dot_general x8, matrix products, batched(): jnp.einsum('sij,sjk->sik', former, latter, precision=HIGHEST, preferred_e...  31.1 us
    all_to_all x1, waiting for transfers between devices, local(): lax.all_to_all(grad_out, 'blk', split_axis=1, concat_axis=1, tiled=True)  18.9 us
    all_to_all x1, waiting for transfers between devices, local(): lax.all_to_all(update.reshape(split_shape), 'blk', split_axis=1, concat_a...  10.6 us
    all_to_all x1, starting transfers between devices, local(): lax.all_to_all(update.reshape(split_shape), 'blk', split_axis=1, concat_a...  8.53 us
    unnamed x31, local copies, waits for them, and re-layouts  8.27 us
  transfers between devices with their start and end apart: 7, of which 7 were waited for; matrix products, arithmetic and copies ran while one was open for 23% of the time, Pallas kernels for 0%

commit v1 on v0

v1 whole, which is shorter than its diff:
```python
import functools
import math

import jax
import jax.numpy as jnp
from jax import lax
from jax.experimental import pallas as pl
from jax.experimental.pallas import tpu as pltpu
from jax.sharding import PartitionSpec as P

BETA = 0.95
VMEM_LIMIT = 56 * 1024 * 1024
VMEM = pl.BlockSpec(memory_space=pltpu.VMEM)
SMEM = pl.BlockSpec(memory_space=pltpu.SMEM)
PARAMS = pltpu.CompilerParams(vmem_limit_bytes=VMEM_LIMIT)


def dot(former, latter):
    return jnp.dot(former, latter, preferred_element_type=jnp.float32)


def split(wide):
    high = wide.astype(jnp.bfloat16)
    return high, (wide - high.astype(jnp.float32)).astype(jnp.bfloat16)


def grams_of(block):
    left = lax.dot_general(
        block, block, (((1,), (1,)), ((), ())), preferred_element_type=jnp.float32
    )
    right = lax.dot_general(
        block, block, (((0,), (0,)), ((), ())), preferred_element_type=jnp.float32
    )
    return left, right


def pack_kernel(slots, me_ref, owner_ref, grads_ref, left_ref, right_ref, out_ref, taken_ref):
    rows_dev, rows, width = grads_ref.shape
    order = left_ref.shape[-1]
    cols = width // order
    for owner in range(out_ref.shape[0]):
        taken_ref[owner] = 0
    row = me_ref[0] * rows + lax.broadcasted_iota(jnp.int32, (rows, order), 0)
    lower = lax.broadcasted_iota(jnp.int32, (rows, order), 1) <= row
    for k in range(rows_dev * cols):
        owner = owner_ref[k]
        slot = taken_ref[owner]
        taken_ref[owner] = slot + 1
        piece = grads_ref[k // cols, :, (k % cols) * order : (k % cols + 1) * order]
        out_ref[owner, slot] = piece
        out_ref[k, 2 * slots] = piece
        out_ref[owner, slots + slot] = jnp.where(lower, left_ref[k], right_ref[k]).astype(
            jnp.bfloat16
        )


def tally_kernel(me_ref, grads_ref, right_ref, _, square_ref, diagonal_ref):
    rows_dev, rows, width = grads_ref.shape
    blocks, _, order = right_ref.shape
    total = jnp.zeros((8, order), jnp.float32)
    for i in range(rows_dev):
        for half in range(width // order):
            wide = grads_ref[i, :, half * order : (half + 1) * order].astype(jnp.float32)
            wide = wide * wide
            total = total + wide[:8] + wide[8:]
    square_ref[...] = jnp.broadcast_to(jnp.sum(total, keepdims=True), square_ref.shape)
    row = me_ref[0] * rows + lax.broadcasted_iota(jnp.int32, (rows, order), 0)
    mine = lax.broadcasted_iota(jnp.int32, (rows, order), 1) == row
    for k in range(blocks):
        diagonal_ref[pl.ds(k, 1), :] = jnp.sum(
            jnp.where(mine, right_ref[k], 0.0), axis=0, keepdims=True
        )


def fifth_kernel(seed_ref, high_ref, low_ref):
    seed = seed_ref[0]
    high, low = split(dot(seed, seed))
    high, low = split(dot(high, high) + (dot(high, low) + dot(low, high)))
    high, low = split(dot(seed, high) + dot(seed, low))
    high_ref[0] = high
    low_ref[0] = low


def gram_kernel(block_ref, out_ref):
    devices, _, rows, order = block_ref.shape
    left, right = grams_of(block_ref[...].reshape(devices * rows, order))
    out_ref[:, 0] = left.reshape(devices, rows, order).astype(jnp.bfloat16)
    out_ref[:, 1] = right.reshape(devices, rows, order).astype(jnp.bfloat16)


def owner_kernel(
    me_ref,
    owner_ref,
    factor_ref,
    block_ref,
    mixed_ref,
    seed_ref,
    high_ref,
    low_ref,
    diagonal_ref,
    roots_ref,
    out_ref,
):
    slot = pl.program_id(0)
    devices, _, rows, order = block_ref.shape
    me = me_ref[0]
    load, chosen = jnp.int32(0), jnp.int32(0)
    for k in range(diagonal_ref.shape[0]):
        mine = owner_ref[k] == me
        chosen = jnp.where(mine & (load == slot), k, chosen)
        load = load + mine.astype(jnp.int32)
    live = slot < load
    factor = factor_ref[0]
    block = block_ref[...].reshape(order, order)
    mixed = mixed_ref[...].reshape(order, order).astype(jnp.float32)
    turned = mixed.T
    row = lax.broadcasted_iota(jnp.int32, (order, order), 0)
    col = lax.broadcasted_iota(jnp.int32, (order, order), 1)
    diagonal = diagonal_ref[pl.ds(chosen, 1), :]
    left_old = jnp.where(col <= row, mixed, turned)
    right_old = jnp.where(col > row, mixed, jnp.where(col == row, diagonal, turned))
    left_gram, right_gram = grams_of(block)

    def new_root(side, old, gram):
        high, low = split(BETA * old + factor * gram)
        fifth_high, fifth_low = high_ref[side, 0], low_ref[side, 0]
        moved = dot(fifth_high, high) + (dot(fifth_high, low) + dot(fifth_low, high))
        seed = seed_ref[side, 0]
        root = (1.25 * seed.astype(jnp.float32) - 0.25 * moved).astype(jnp.bfloat16)
        roots_ref[side, 0] = jnp.where(live, root, seed)
        return root

    left_root = new_root(0, left_old, left_gram)
    right_root = new_root(1, right_old, right_gram)
    applied = dot(left_root, block).astype(jnp.bfloat16)
    direction = dot(applied, right_root).astype(jnp.bfloat16).astype(jnp.float32)
    norm = jnp.sqrt(jnp.sum(direction * direction, keepdims=True)) + 1e-06
    out_ref[...] = (direction / norm).astype(jnp.bfloat16).reshape(out_ref.shape)


def place_kernel(owner_ref, norm_ref, back_ref, out_ref, taken_ref):
    rows_dev, rows, width = out_ref.shape
    order = back_ref.shape[-1]
    cols = width // order
    for owner in range(back_ref.shape[0]):
        taken_ref[owner] = 0
    for k in range(rows_dev * cols):
        owner = owner_ref[k]
        slot = taken_ref[owner]
        taken_ref[owner] = slot + 1
        out_ref[k // cols, :, (k % cols) * order : (k % cols + 1) * order] = (
            back_ref[owner, slot].astype(jnp.float32) * norm_ref[k]
        ).astype(jnp.bfloat16)


def butterfly(values, axis):
    size = lax.axis_size(axis)
    step = 1
    while step < size:
        values = values + lax.ppermute(values, axis, [(i, i ^ step) for i in range(size)])
        step *= 2
    return values


def exchange(values):
    return lax.all_to_all(values, "blk", split_axis=0, concat_axis=0, tiled=True)


def cost(passes, order, moved):
    return pl.CostEstimate(
        flops=2 * passes * order**3, bytes_accessed=moved, transcendentals=0
    )


def local(grads, owners, left_stats, right_stats, second_moment, roots):
    devices = lax.axis_size("blk")
    rows_dev, rows, width = grads.shape
    order = left_stats.shape[-1]
    cols = width // order
    blocks = rows_dev * cols
    slots = roots.shape[2]
    pieces = 2 * slots + 1
    me = lax.axis_index("blk").astype(jnp.int32).reshape(1)
    owner_of = owners.reshape(blocks)
    left_old, right_old = left_stats[0], right_stats[0]
    taken = [pltpu.SMEM((devices,), jnp.int32)]

    sent = pl.pallas_call(
        functools.partial(pack_kernel, slots),
        out_shape=jax.ShapeDtypeStruct((devices, pieces, rows, order), jnp.bfloat16),
        in_specs=[SMEM, SMEM, VMEM, VMEM, VMEM],
        out_specs=VMEM,
        scratch_shapes=taken,
        compiler_params=PARAMS,
        name="pack",
    )(me, owner_of, grads, left_old, right_old)
    arrived = exchange(sent)

    square, diagonal = pl.pallas_call(
        tally_kernel,
        out_shape=[
            jax.ShapeDtypeStruct((8, order), jnp.float32),
            jax.ShapeDtypeStruct((blocks, order), jnp.float32),
        ],
        in_specs=[SMEM, VMEM, VMEM, pl.BlockSpec(memory_space=pl.ANY)],
        out_specs=[VMEM, VMEM],
        compiler_params=PARAMS,
        name="tally",
    )(me, grads, right_old, sent)
    square = butterfly(square, "zero")
    gathered = butterfly(jnp.concatenate([diagonal, square]), "blk")
    diagonal, total = gathered[:blocks], gathered[blocks, 0]
    entries = rows_dev * lax.axis_size("zero") * order * width
    scale = jnp.minimum(1.0, math.sqrt(entries) / (jnp.sqrt(total) + 1e-06))
    factor = 0.05 * scale * scale

    seeds = roots[0]
    square_spec = pl.BlockSpec((1, order, order), lambda i: (i, 0, 0))
    fifth_shape = jax.ShapeDtypeStruct((2 * slots, order, order), jnp.bfloat16)
    high, low = pl.pallas_call(
        fifth_kernel,
        grid=(2 * slots,),
        out_shape=[fifth_shape, fifth_shape],
        in_specs=[square_spec],
        out_specs=[square_spec, square_spec],
        compiler_params=PARAMS,
        cost_estimate=cost(12 * slots, order, 12 * slots * order * order),
        name="fifth",
    )(seeds.reshape(2 * slots, order, order))
    high = high.reshape(2, slots, order, order)
    low = low.reshape(2, slots, order, order)

    clipped = grads.astype(jnp.float32) * scale
    new_second = 0.95 * second_moment + 0.05 * clipped * clipped
    adam_step = clipped / (jnp.sqrt(new_second) + 1e-08)
    adam_part = jnp.sum(
        (adam_step * adam_step).reshape(rows_dev, rows, cols, order), axis=(1, 3)
    ).reshape(blocks)
    adam_norm = jnp.sqrt(butterfly(adam_part, "blk"))

    grams = pl.pallas_call(
        gram_kernel,
        grid=(1,),
        out_shape=jax.ShapeDtypeStruct((devices, 2, rows, order), jnp.bfloat16),
        in_specs=[pl.BlockSpec((devices, 1, rows, order), lambda i: (0, 2 * slots, 0, 0))],
        out_specs=pl.BlockSpec((devices, 2, rows, order), lambda i: (0, 0, 0, 0)),
        compiler_params=PARAMS,
        cost_estimate=cost(2, order, 6 * order * order),
        name="grams",
    )(arrived)
    grams_back = exchange(grams)

    side_spec = pl.BlockSpec((2, 1, order, order), lambda s: (0, s, 0, 0))
    new_roots, update = pl.pallas_call(
        owner_kernel,
        grid=(slots,),
        out_shape=[
            jax.ShapeDtypeStruct((2, slots, order, order), jnp.bfloat16),
            jax.ShapeDtypeStruct((devices, slots, rows, order), jnp.bfloat16),
        ],
        in_specs=[
            SMEM,
            SMEM,
            SMEM,
            pl.BlockSpec((devices, 1, rows, order), lambda s: (0, s, 0, 0)),
            pl.BlockSpec((devices, 1, rows, order), lambda s: (0, slots + s, 0, 0)),
            side_spec,
            side_spec,
            side_spec,
            pl.BlockSpec((blocks, order), lambda s: (0, 0)),
        ],
        out_specs=[
            side_spec,
            pl.BlockSpec((devices, 1, rows, order), lambda s: (0, s, 0, 0)),
        ],
        compiler_params=PARAMS,
        cost_estimate=cost(10 * slots, order, 24 * slots * order * order),
        name="owner",
    )(me, owner_of, factor.reshape(1), arrived, arrived, seeds, high, low, diagonal)
    update_back = exchange(update)

    new_left = BETA * left_old + factor * grams_back[:blocks, 0].astype(jnp.float32)
    new_right = BETA * right_old + factor * grams_back[:blocks, 1].astype(jnp.float32)

    placed = pl.pallas_call(
        place_kernel,
        out_shape=jax.ShapeDtypeStruct((rows_dev, rows, width), jnp.bfloat16),
        in_specs=[SMEM, SMEM, VMEM],
        out_specs=VMEM,
        scratch_shapes=taken,
        compiler_params=PARAMS,
        name="place",
    )(owner_of, adam_norm, update_back)
    return (placed, new_second, new_left[None], new_right[None], new_roots[None])


def solution(mesh):
    placed = (
        P("zero", "blk", None),
        P("zero", None, None),
        P("zero", None, "blk", None),
        P("zero", None, "blk", None),
        P("zero", "blk", None),
        P("zero", None, "blk", None, None),
    )
    return jax.shard_map(
        local,
        mesh=mesh,
        in_specs=placed,
        out_specs=(
            P("zero", "blk", None),
            P("zero", "blk", None),
            P("zero", None, "blk", None),
            P("zero", None, "blk", None),
            P("zero", None, "blk", None, None),
        ),
        check_vma=False,
    )
```

time: 348 us -> 193 us (0.55)
  waiting for transfers between devices: 128 us -> 37.2 us
  matrix products: 38.4 us -> 0 us
  local copies, waits for them, and re-layouts: 33.4 us -> 2.25 us
  Pallas kernels: 0 us -> 30.5 us
  other arithmetic: 22.5 us -> 8.1 us
  blocking collectives: 79 us -> 74.4 us
    all_to_all x7 -> x2, waiting for transfers between devices: 128 us -> 0.01 us  [exchange(): lax.all_to_all(values, 'blk', split_axis=0, concat_axis=0, tiled=True)]
    psum x1 -> x0, blocking collectives: 79 us -> none  [local(): grand_total = lax.psum(jnp.sum(widened * widened), ('blk', 'zero'))]
    all_to_all x0 -> x1, blocking collectives: none -> 74.4 us  [exchange(): lax.all_to_all(values, 'blk', split_axis=0, concat_axis=0, tiled=True)]
    dot_general x11 -> x0, matrix products: 38.4 us -> none  [the longest x8 31.1 us: batched(): jnp.einsum('sij,sjk->sik', former, latter, precision=HIGHEST, preferred_e...]
    ppermute x0 -> x13, waiting for transfers between devices: none -> 37.2 us  [butterfly(): lax.ppermute(values, axis, [(i, i ^ step) for i in range(size)])]
    all_to_all x7 -> x2, starting transfers between devices: 41.2 us -> 9.99 us  [exchange(): lax.all_to_all(values, 'blk', split_axis=0, concat_axis=0, tiled=True)]
    pallas_call x0 -> x6, Pallas kernels: none -> 30.5 us  [the longest x1 10.6 us: local(): pl.pallas_call(owner_kernel, grid=(slots,), out_shape=[jax.ShapeDtypeStru...]
    ppermute x0 -> x13, starting transfers between devices: none -> 28.6 us  [butterfly(): lax.ppermute(values, axis, [(i, i ^ step) for i in range(size)])]
  transfers between devices with their start and end apart: 7 -> 15, of which waited for: 7 -> 12; matrix products, arithmetic and copies ran while one was open for 23% -> 5% of each run, Pallas kernels for 0% -> 12%
where the time goes in v1:
time: 193 us
  blocking collectives  74.4 us (39%)
  starting transfers between devices  38.6 us (20%)
  waiting for transfers between devices  37.2 us (19%)
  Pallas kernels  30.5 us (16%)
  other arithmetic  8.1 us (4%)
  local copies, waits for them, and re-layouts  2.25 us (1%)
    all_to_all x1, blocking collectives, exchange(): lax.all_to_all(values, 'blk', split_axis=0, concat_axis=0, tiled=True)  74.4 us
    ppermute x13, waiting for transfers between devices, butterfly(): lax.ppermute(values, axis, [(i, i ^ step) for i in range(size)])  37.2 us
    ppermute x13, starting transfers between devices, butterfly(): lax.ppermute(values, axis, [(i, i ^ step) for i in range(size)])  28.6 us
    pallas_call x1, Pallas kernels, local(): pl.pallas_call(owner_kernel, grid=(slots,), out_shape=[jax.ShapeDtypeStru...  10.6 us
    all_to_all x2, starting transfers between devices, exchange(): lax.all_to_all(values, 'blk', split_axis=0, concat_axis=0, tiled=True)  9.99 us
    pallas_call x1, Pallas kernels, local(): pl.pallas_call(fifth_kernel, grid=(2 * slots,), out_shape=[fifth_shape, f...  9.82 us
  transfers between devices with their start and end apart: 15, of which 12 were waited for; matrix products, arithmetic and copies ran while one was open for 5% of the time, Pallas kernels for 12%

profile of v1, /device:TPU:4, one launch (start us, length us, event | category | flops | bytes accessed | tf_op | source)
XLA Modules:
  0.0 192.6 jit_solution(16336117132847308492)
XLA Ops:
  0.6 3.2 %pack.1._ = bf16[32,5,16,512]{3,2,1,0:T(8,128)(2,1)} custom-call(s32[1]{0:T(128)} %bitcast.1.me_ref, s32[24]{0:T(128)} %bitcast.26, bf16[2,16,6144]{2,1,0:T(8,128)(2,1)} %grads_ref.3, f32[24,16,512]{2,1,0:T(8,128)} %bitcast.25, f32[24,16,512]{2,1,0:T(8,128)} %bitcast.23), custom_call_target="tpu_custom_call" | custom-call | tf_op jit(solution)/shard_map/pack/pallas_call | solution.py:188
  3.8 74.4 %all_to_all.15.block_ref.mixed_ref = bf16[32,5,16,512]{3,2,1,0:T(8,128)(2,1)} all-to-all(bf16[32,5,16,512]{3,2,1,0:T(8,128)(2,1)} %pack.1._), channel_id=1, replica_groups=mesh['blk'=32,'zero'=8] {'blk'}, dimensions={0} | all-to-all | bytes 5242880 | tf_op jit(solution)/shard_map/all_to_all | solution.py:166
  78.2 2.8 %grams.1 = bf16[32,2,16,512]{3,2,1,0:T(8,128)(2,1)} custom-call(bf16[32,5,16,512]{3,2,1,0:T(8,128)(2,1)} %all_to_all.15.block_ref.mixed_ref), custom_call_target="tpu_custom_call" | custom-call | flops 536870912 | bytes 1572864 | tf_op jit(solution)/shard_map/grams/pallas_call | solution.py:241
  81.0 4.5 %all-to-all-start.2 = ((bf16[32,2,16,512]{3,2,1,0:T(8,128)(2,1)}), bf16[32,2,16,512]{3,2,1,0:T(8,128)(2,1)S(1)}, u32[]{:S(2)}, u32[]{:S(2)}) async-start(bf16[32,2,16,512]{3,2,1,0:T(8,128)(2,1)} %grams.1), calls=%async_computation.2 | async-start | bytes 2097152 | tf_op jit(solution)/shard_map/all_to_all | solution.py:166
  85.5 2.1 %tally.1 = (f32[8,512]{1,0:T(8,128)}, f32[24,512]{1,0:T(8,128)}) custom-call(s32[1]{0:T(128)} %bitcast.1.me_ref, bf16[2,16,6144]{2,1,0:T(8,128)(2,1)} %grads_ref.3, f32[24,16,512]{2,1,0:T(8,128)} %bitcast.24, bf16[32,5,16,512]{3,2,1,0:T(8,128)(2,1)} %pack.1._), custom_call_target="tpu_custom_call" | custom-call | tf_op jit(solution)/shard_map/tally/pallas_call | solution.py:199
  87.6 0.0 collective-permute-start
  87.6 1.4 collective-permute-done
  89.0 0.7 add.60
  89.7 1.2 collective-permute-start.1
  90.9 2.5 %collective-permute-done.1 = f32[8,512]{1,0:T(8,128)S(1)} collective-permute-done((f32[8,512]{1,0:T(8,128)S(1)}, f32[8,512]{1,0:T(8,128)S(1)}, u32[]{:S(2)}, u32[]{:S(2)}) %collective-permute-start.1) | collective-permute-done | bytes 16416 | tf_op jit(solution)/shard_map/ppermute | solution.py:160
  93.5 0.5 collective-permute-start.2
  94.0 4.7 %collective-permute-done.2 = f32[8,512]{1,0:T(8,128)S(1)} collective-permute-done((f32[8,512]{1,0:T(8,128)S(1)}, f32[8,512]{1,0:T(8,128)S(1)}, u32[]{:S(2)}, u32[]{:S(2)}) %collective-permute-start.2) | collective-permute-done | bytes 16416 | tf_op jit(solution)/shard_map/ppermute | solution.py:160
  98.7 0.8 pad_maximum_fusion
  99.5 1.8 collective-permute-start.3
  101.3 2.8 %collective-permute-done.3 = f32[32,512]{1,0:T(8,128)S(1)} collective-permute-done((f32[32,512]{1,0:T(8,128)S(1)}, f32[32,512]{1,0:T(8,128)S(1)}, u32[]{:S(2)}, u32[]{:S(2)}) %collective-permute-start.3) | collective-permute-done | bytes 65568 | tf_op jit(solution)/shard_map/ppermute | solution.py:160
  104.1 0.8 fusion.1
  104.9 4.3 %collective-permute-start.4 = (f32[32,512]{1,0:T(8,128)S(1)}, f32[32,512]{1,0:T(8,128)S(1)}, u32[]{:S(2)}, u32[]{:S(2)}) collective-permute-start(f32[32,512]{1,0:T(8,128)S(1)} %fusion.1), channel_id=1, source_target_pairs={{0,16},{8,24},{16,0},{24,8},{32,48},{40,56},{48,32},{56,40},{64,80... | collective-permute-start | bytes 196616 | tf_op jit(solution)/shard_map/ppermute | solution.py:160
  109.2 2.7 %collective-permute-done.4 = f32[32,512]{1,0:T(8,128)S(1)} collective-permute-done((f32[32,512]{1,0:T(8,128)S(1)}, f32[32,512]{1,0:T(8,128)S(1)}, u32[]{:S(2)}, u32[]{:S(2)}) %collective-permute-start.4) | collective-permute-done | bytes 65568 | tf_op jit(solution)/shard_map/ppermute | solution.py:160
  111.9 1.0 collective-permute-start.5
  112.9 4.0 %collective-permute-done.5 = f32[32,512]{1,0:T(8,128)S(1)} collective-permute-done((f32[32,512]{1,0:T(8,128)S(1)}, f32[32,512]{1,0:T(8,128)S(1)}, u32[]{:S(2)}, u32[]{:S(2)}) %collective-permute-start.5) | collective-permute-done | bytes 65568 | tf_op jit(solution)/shard_map/ppermute | solution.py:160
  117.0 2.1 %collective-permute-start.6 = (f32[32,512]{1,0:T(8,128)S(1)}, f32[32,512]{1,0:T(8,128)S(1)}, u32[]{:S(2)}, u32[]{:S(2)}) collective-permute-start(f32[32,512]{1,0:T(8,128)S(1)} %add.65), channel_id=1, source_target_pairs={{0,64},{8,72},{16,80},{24,88},{32,96},{40,104},{48,112},{56,120},{... | collective-permute-start | bytes 196616 | tf_op jit(solution)/shard_map/ppermute | solution.py:160
  119.1 3.7 %collective-permute-done.6 = f32[32,512]{1,0:T(8,128)S(1)} collective-permute-done((f32[32,512]{1,0:T(8,128)S(1)}, f32[32,512]{1,0:T(8,128)S(1)}, u32[]{:S(2)}, u32[]{:S(2)}) %collective-permute-start.6) | collective-permute-done | bytes 65568 | tf_op jit(solution)/shard_map/ppermute | solution.py:160
  122.8 5.5 %collective-permute-start.7 = (f32[32,512]{1,0:T(8,128)S(1)}, f32[32,512]{1,0:T(8,128)S(1)}, u32[]{:S(2)}, u32[]{:S(2)}) collective-permute-start(f32[32,512]{1,0:T(8,128)S(1)} %add.66), channel_id=1, source_target_pairs={{0,128},{8,136},{16,144},{24,152},{32,160},{40,168},{48,176},{56,1... | collective-permute-start | bytes 196616 | tf_op jit(solution)/shard_map/ppermute | solution.py:160
  128.3 9.8 %fifth.1 = (bf16[4,512,512]{2,1,0:T(8,128)(2,1)}, bf16[4,512,512]{2,1,0:T(8,128)(2,1)}) custom-call(bf16[4,512,512]{2,1,0:T(8,128)(2,1)} %bitcast.29), custom_call_target="tpu_custom_call" | custom-call | flops 6442450944 | bytes 6291456 | tf_op jit(solution)/shard_map/fifth/pallas_call | solution.py:220
  138.1 0.0 collective-permute-done.7
  138.1 0.5 slice.16
  138.6 0.6 slice.17.diagonal_ref
  140.0 10.6 %owner.1 = (bf16[2,2,512,512]{3,2,1,0:T(8,128)(2,1)}, bf16[32,2,16,512]{3,2,1,0:T(8,128)(2,1)}) custom-call(s32[1]{0:T(128)} %bitcast.1.me_ref, s32[24]{0:T(128)} %bitcast.27, f32[1]{0:T(128)} %bitcast.5.factor_ref, bf16[32,5,16,512]{3,2,1,0:T(8,128)(2,1)} %all_to_all.15.block_ref.mixed_ref, bf16[32,5,16,512]{3,2,1,0:T(8,128)(2,1)} %all_to_all.15.block_ref.mixed_ref, ...), custom_call_target="tpu_custom_call" | custom-call | flops 5368709120 | bytes 12582912 | tf_op jit(solution)/shard_map/owner/pallas_call | solution.py:254
  150.6 0.0 copy-start
  150.6 5.4 %all-to-all-start.1 = ((bf16[32,2,16,512]{3,2,1,0:T(8,128)(2,1)}), bf16[32,2,16,512]{3,2,1,0:T(8,128)(2,1)S(1)}, u32[]{:S(2)}, u32[]{:S(2)}) async-start(bf16[32,2,16,512]{3,2,1,0:T(8,128)(2,1)} %get-tuple-element.15), calls=%async_computation.1 | async-start | bytes 2097152 | tf_op jit(solution)/shard_map/all_to_all | solution.py:166
  156.1 2.5 %multiply_reduce_fusion = (f32[2,6144]{1,0:T(2,128)S(1)}, f32[2,16,6144]{2,1,0:T(8,128)}) fusion(bf16[2,16,6144]{2,1,0:T(8,128)(2,1)S(1)} %copy-done.2, f32[]{:T(128)} %bitcast.4, f32[2,16,6144]{2,1,0:T(8,128)} %param.10), kind=kLoop, calls=%fused_computation.5 | loop fusion | flops 1953792 | bytes 2015236 | tf_op jit(solution)/shard_map/reduce_sum | solution.py:236
  158.6 0.1 reduce_sum.18
  158.7 0.1 reshape.71
  158.8 2.0 %collective-permute-start.8 = (f32[24]{0:T(128)S(1)}, f32[24]{0:T(128)S(1)}, u32[]{:S(2)}, u32[]{:S(2)}) collective-permute-start(f32[24]{0:T(128)S(1)} %reshape.71), channel_id=1, source_target_pairs={{0,8},{8,0},{16,24},{24,16},{32,40},{40,32},{48,56},{56,48},{64,72... | collective-permute-start | bytes 296 | tf_op jit(solution)/shard_map/ppermute | solution.py:160
  160.8 1.8 collective-permute-done.8
  162.5 3.3 %collective-permute-start.9 = (f32[24]{0:T(128)S(1)}, f32[24]{0:T(128)S(1)}, u32[]{:S(2)}, u32[]{:S(2)}) collective-permute-start(f32[24]{0:T(128)S(1)} %add.72), channel_id=1, source_target_pairs={{0,16},{8,24},{16,0},{24,8},{32,48},{40,56},{48,32},{56,40},{64,80... | collective-permute-start | bytes 296 | tf_op jit(solution)/shard_map/ppermute | solution.py:160
  165.8 1.7 collective-permute-done.9
  167.6 1.9 collective-permute-start.10
  169.5 5.0 %collective-permute-done.10 = f32[24]{0:T(128)S(1)} collective-permute-done((f32[24]{0:T(128)S(1)}, f32[24]{0:T(128)S(1)}, u32[]{:S(2)}, u32[]{:S(2)}) %collective-permute-start.10) | collective-permute-done | bytes 128 | tf_op jit(solution)/shard_map/ppermute | solution.py:160
  174.5 0.6 collective-permute-start.11
  175.1 3.9 %collective-permute-done.11 = f32[24]{0:T(128)S(1)} collective-permute-done((f32[24]{0:T(128)S(1)}, f32[24]{0:T(128)S(1)}, u32[]{:S(2)}, u32[]{:S(2)}) %collective-permute-start.11) | collective-permute-done | bytes 128 | tf_op jit(solution)/shard_map/ppermute | solution.py:160
  178.9 4.5 %collective-permute-start.12 = (f32[24]{0:T(128)S(1)}, f32[24]{0:T(128)S(1)}, u32[]{:S(2)}, u32[]{:S(2)}) collective-permute-start(f32[24]{0:T(128)S(1)} %add.75), channel_id=1, source_target_pairs={{0,128},{8,136},{16,144},{24,152},{32,160},{40,168},{48,176},{56,1... | collective-permute-start | bytes 296 | tf_op jit(solution)/shard_map/ppermute | solution.py:160
  183.4 3.0 %collective-permute-done.12 = f32[24]{0:T(128)S(1)} collective-permute-done((f32[24]{0:T(128)S(1)}, f32[24]{0:T(128)S(1)}, u32[]{:S(2)}, u32[]{:S(2)}) %collective-permute-start.12) | collective-permute-done | bytes 128 | tf_op jit(solution)/shard_map/ppermute | solution.py:160
  186.4 0.5 add_sqrt_fusion.norm_ref
  186.9 2.6 %bitcast_add_fusion = (f32[1,24,16,512]{3,2,1,0:T(8,128)}, f32[1,24,16,512]{3,2,1,0:T(8,128)}) fusion(f32[1,24,16,512]{3,2,1,0:T(8,128)S(1)} %copy-done, bf16[32,2,16,512]{3,2,1,0:T(8,128)(2,1)S(1)} %all-to-all-done.2, f32[]{:T(128)} %mul.77, f32[1,24,16,512]{3,2,1,0:T(8,128)} %param.8), kind=kLoop, calls=%fused_computation.2 | loop fusion | flops 1572864 | bytes 3932164 | tf_op jit(solution)/shard_map/add | solution.py:283
  189.5 0.0 all-to-all-done.1.back_ref
  189.5 1.0 copy-done.1
  190.5 2.1 %place.1 = bf16[2,16,6144]{2,1,0:T(8,128)(2,1)} custom-call(s32[24]{0:T(128)} %bitcast.28, f32[24]{0:T(128)} %add_sqrt_fusion.norm_ref, bf16[32,2,16,512]{3,2,1,0:T(8,128)(2,1)} %copy-done.1), custom_call_target="tpu_custom_call" | custom-call | tf_op jit(solution)/shard_map/place/pallas_call | solution.py:285
  (16 shorter events, 0.1 us)
Async XLA Ops:
  81.0 69.6 %all-to-all-start.2 = ((bf16[32,2,16,512]{3,2,1,0:T(8,128)(2,1)}), bf16[32,2,16,512]{3,2,1,0:T(8,128)(2,1)S(1)}, u32[]{:S(2)}, u32[]{:S(2)}) async-start(bf16[32,2,16,512]{3,2,1,0:T(8,128)(2,1)} %grams.1), calls=%async_computation.2 | async-start | bytes 2097152 | tf_op jit(solution)/shard_map/all_to_all | solution.py:166
  87.6 1.4 collective-permute-start
  89.7 3.7 %collective-permute-start.1 = (f32[8,512]{1,0:T(8,128)S(1)}, f32[8,512]{1,0:T(8,128)S(1)}, u32[]{:S(2)}, u32[]{:S(2)}) collective-permute-start(f32[8,512]{1,0:T(8,128)S(1)} %add.60), channel_id=1, source_target_pairs={{0,2},{1,3},{2,0},{3,1},{4,6},{5,7},{6,4},{7,5},{8,10},{9,11},{10,... | collective-permute-start | bytes 49160 | tf_op jit(solution)/shard_map/ppermute | solution.py:160
  93.5 5.2 %collective-permute-start.2 = (f32[8,512]{1,0:T(8,128)S(1)}, f32[8,512]{1,0:T(8,128)S(1)}, u32[]{:S(2)}, u32[]{:S(2)}) collective-permute-start(f32[8,512]{1,0:T(8,128)S(1)} %add.61), channel_id=1, source_target_pairs={{0,4},{1,5},{2,6},{3,7},{4,0},{5,1},{6,2},{7,3},{8,12},{9,13},{10,... | collective-permute-start | bytes 49160 | tf_op jit(solution)/shard_map/ppermute | solution.py:160
  99.5 4.6 %collective-permute-start.3 = (f32[32,512]{1,0:T(8,128)S(1)}, f32[32,512]{1,0:T(8,128)S(1)}, u32[]{:S(2)}, u32[]{:S(2)}) collective-permute-start(f32[32,512]{1,0:T(8,128)S(1)} %pad_maximum_fusion), channel_id=1, source_target_pairs={{0,8},{8,0},{16,24},{24,16},{32,40},{40,32},{48,56},{56,48},{64,72... | collective-permute-start | bytes 196616 | tf_op jit(solution)/shard_map/ppermute | solution.py:160
  104.9 7.0 %collective-permute-start.4 = (f32[32,512]{1,0:T(8,128)S(1)}, f32[32,512]{1,0:T(8,128)S(1)}, u32[]{:S(2)}, u32[]{:S(2)}) collective-permute-start(f32[32,512]{1,0:T(8,128)S(1)} %fusion.1), channel_id=1, source_target_pairs={{0,16},{8,24},{16,0},{24,8},{32,48},{40,56},{48,32},{56,40},{64,80... | collective-permute-start | bytes 196616 | tf_op jit(solution)/shard_map/ppermute | solution.py:160
  111.9 5.1 %collective-permute-start.5 = (f32[32,512]{1,0:T(8,128)S(1)}, f32[32,512]{1,0:T(8,128)S(1)}, u32[]{:S(2)}, u32[]{:S(2)}) collective-permute-start(f32[32,512]{1,0:T(8,128)S(1)} %add.64), channel_id=1, source_target_pairs={{0,32},{8,40},{16,48},{24,56},{32,0},{40,8},{48,16},{56,24},{64,96... | collective-permute-start | bytes 196616 | tf_op jit(solution)/shard_map/ppermute | solution.py:160
  117.0 5.8 %collective-permute-start.6 = (f32[32,512]{1,0:T(8,128)S(1)}, f32[32,512]{1,0:T(8,128)S(1)}, u32[]{:S(2)}, u32[]{:S(2)}) collective-permute-start(f32[32,512]{1,0:T(8,128)S(1)} %add.65), channel_id=1, source_target_pairs={{0,64},{8,72},{16,80},{24,88},{32,96},{40,104},{48,112},{56,120},{... | collective-permute-start | bytes 196616 | tf_op jit(solution)/shard_map/ppermute | solution.py:160
  122.8 15.3 %collective-permute-start.7 = (f32[32,512]{1,0:T(8,128)S(1)}, f32[32,512]{1,0:T(8,128)S(1)}, u32[]{:S(2)}, u32[]{:S(2)}) collective-permute-start(f32[32,512]{1,0:T(8,128)S(1)} %add.66), channel_id=1, source_target_pairs={{0,128},{8,136},{16,144},{24,152},{32,160},{40,168},{48,176},{56,1... | collective-permute-start | bytes 196616 | tf_op jit(solution)/shard_map/ppermute | solution.py:160
  150.6 5.5 %copy-start.2 = (bf16[2,16,6144]{2,1,0:T(8,128)(2,1)S(1)}, bf16[2,16,6144]{2,1,0:T(8,128)(2,1)}, u32[]{:S(2)}) copy-start(bf16[2,16,6144]{2,1,0:T(8,128)(2,1)} %grads_ref.3) | copy-start | bytes 1179652
  150.6 36.3 %copy-start = (f32[1,24,16,512]{3,2,1,0:T(8,128)S(1)}, f32[1,24,16,512]{3,2,1,0:T(8,128)}, u32[]{:S(2)}) copy-start(f32[1,24,16,512]{3,2,1,0:T(8,128)} %param.9) | copy-start | bytes 2359300
  150.6 38.9 %all-to-all-start.1 = ((bf16[32,2,16,512]{3,2,1,0:T(8,128)(2,1)}), bf16[32,2,16,512]{3,2,1,0:T(8,128)(2,1)S(1)}, u32[]{:S(2)}, u32[]{:S(2)}) async-start(bf16[32,2,16,512]{3,2,1,0:T(8,128)(2,1)} %get-tuple-element.15), calls=%async_computation.1 | async-start | bytes 2097152 | tf_op jit(solution)/shard_map/all_to_all | solution.py:166
  158.8 3.7 %collective-permute-start.8 = (f32[24]{0:T(128)S(1)}, f32[24]{0:T(128)S(1)}, u32[]{:S(2)}, u32[]{:S(2)}) collective-permute-start(f32[24]{0:T(128)S(1)} %reshape.71), channel_id=1, source_target_pairs={{0,8},{8,0},{16,24},{24,16},{32,40},{40,32},{48,56},{56,48},{64,72... | collective-permute-start | bytes 296 | tf_op jit(solution)/shard_map/ppermute | solution.py:160
  162.5 5.0 %collective-permute-start.9 = (f32[24]{0:T(128)S(1)}, f32[24]{0:T(128)S(1)}, u32[]{:S(2)}, u32[]{:S(2)}) collective-permute-start(f32[24]{0:T(128)S(1)} %add.72), channel_id=1, source_target_pairs={{0,16},{8,24},{16,0},{24,8},{32,48},{40,56},{48,32},{56,40},{64,80... | collective-permute-start | bytes 296 | tf_op jit(solution)/shard_map/ppermute | solution.py:160
  167.6 6.9 %collective-permute-start.10 = (f32[24]{0:T(128)S(1)}, f32[24]{0:T(128)S(1)}, u32[]{:S(2)}, u32[]{:S(2)}) collective-permute-start(f32[24]{0:T(128)S(1)} %add.73), channel_id=1, source_target_pairs={{0,32},{8,40},{16,48},{24,56},{32,0},{40,8},{48,16},{56,24},{64,96... | collective-permute-start | bytes 296 | tf_op jit(solution)/shard_map/ppermute | solution.py:160
  174.5 4.4 %collective-permute-start.11 = (f32[24]{0:T(128)S(1)}, f32[24]{0:T(128)S(1)}, u32[]{:S(2)}, u32[]{:S(2)}) collective-permute-start(f32[24]{0:T(128)S(1)} %add.74), channel_id=1, source_target_pairs={{0,64},{8,72},{16,80},{24,88},{32,96},{40,104},{48,112},{56,120},{... | collective-permute-start | bytes 296 | tf_op jit(solution)/shard_map/ppermute | solution.py:160
  178.9 7.4 %collective-permute-start.12 = (f32[24]{0:T(128)S(1)}, f32[24]{0:T(128)S(1)}, u32[]{:S(2)}, u32[]{:S(2)}) collective-permute-start(f32[24]{0:T(128)S(1)} %add.75), channel_id=1, source_target_pairs={{0,128},{8,136},{16,144},{24,152},{32,160},{40,168},{48,176},{56,1... | collective-permute-start | bytes 296 | tf_op jit(solution)/shard_map/ppermute | solution.py:160
  189.5 1.0 copy-start.1

commit v2 on v1

v2 whole, which is shorter than its diff:
```python
import functools
import math

import jax
import jax.numpy as jnp
from jax import lax
from jax.experimental import pallas as pl
from jax.experimental.pallas import tpu as pltpu
from jax.sharding import PartitionSpec as P

BETA = 0.95
VMEM_LIMIT = 56 * 1024 * 1024
VMEM = pl.BlockSpec(memory_space=pltpu.VMEM)
SMEM = pl.BlockSpec(memory_space=pltpu.SMEM)
PARAMS = pltpu.CompilerParams(vmem_limit_bytes=VMEM_LIMIT)


def dot(former, latter):
    return jnp.dot(former, latter, preferred_element_type=jnp.float32)


def split(wide):
    high = wide.astype(jnp.bfloat16)
    return high, (wide - high.astype(jnp.float32)).astype(jnp.bfloat16)


def grams_of(block):
    left = lax.dot_general(
        block, block, (((1,), (1,)), ((), ())), preferred_element_type=jnp.float32
    )
    right = lax.dot_general(
        block, block, (((0,), (0,)), ((), ())), preferred_element_type=jnp.float32
    )
    return left, right


LANES = 128


def thirds(wide):
    first = wide.astype(jnp.bfloat16).astype(jnp.float32)
    second = (wide - first).astype(jnp.bfloat16).astype(jnp.float32)
    return first, second, wide - first - second


def sublanes(shape):
    return lax.broadcasted_iota(jnp.int32, shape, len(shape) - 2)


def lanes(shape):
    return lax.broadcasted_iota(jnp.int32, shape, len(shape) - 1)


def store_piece(ref, place, first, piece):
    for tile in range(piece.shape[-1] // LANES):
        ref[place, first + tile] = piece[:, tile * LANES : (tile + 1) * LANES]


def whole_block(ref):
    devices, tiles, rows, _ = ref.shape
    return jnp.concatenate(
        [ref[:, tile].reshape(devices * rows, LANES) for tile in range(tiles)], axis=1
    )


def pack_kernel(slots, me_ref, owner_ref, grads_ref, left_ref, right_ref, out_ref, taken_ref):
    rows_dev, rows, width = grads_ref.shape
    order = left_ref.shape[-1]
    cols = width // order
    tiles = order // LANES
    devices, extra = out_ref.shape[0], out_ref.shape[1] - 1
    total = jnp.zeros((8, order), jnp.float32)
    for i in range(rows_dev):
        for j in range(cols):
            wide = grads_ref[i, :, j * order : (j + 1) * order].astype(jnp.float32)
            wide = wide * wide
            for part in range(rows // 8):
                total = total + wide[8 * part : 8 * part + 8]
    terms = thirds(jnp.sum(total, keepdims=True))
    tile_row = sublanes((rows, LANES))
    base = jnp.zeros((rows, LANES), jnp.float32)
    for place, term in enumerate(terms):
        base = jnp.where(tile_row == slots + place, term, base)
    for owner in range(devices):
        taken_ref[owner] = 0
        out_ref[owner, extra] = base.astype(jnp.bfloat16)
    row = me_ref[0] * rows + sublanes((rows, order))
    lower = lanes((rows, order)) <= row
    mine = lanes((rows, order)) == row
    for k in range(rows_dev * cols):
        owner = owner_ref[k]
        slot = taken_ref[owner]
        taken_ref[owner] = slot + 1
        piece = grads_ref[k // cols, :, (k % cols) * order : (k % cols + 1) * order]
        store_piece(out_ref, owner, slot * tiles, piece)
        store_piece(out_ref, k, 2 * slots * tiles, piece)
        right = right_ref[k]
        mixed = jnp.where(lower, left_ref[k], right).astype(jnp.bfloat16)
        store_piece(out_ref, owner, (slots + slot) * tiles, mixed)
        marked = jnp.where(mine, right, 0.0)
        diagonal = marked[:, :LANES]
        for tile in range(1, tiles):
            diagonal = diagonal + marked[:, tile * LANES : (tile + 1) * LANES]
        diagonal = jnp.sum(diagonal, axis=0, keepdims=True)
        out_ref[owner, extra] = jnp.where(
            tile_row == slot, diagonal, out_ref[owner, extra].astype(jnp.float32)
        ).astype(jnp.bfloat16)


def fifth_kernel(seed_ref, high_ref, low_ref):
    seed = seed_ref[0]
    high, low = split(dot(seed, seed))
    high, low = split(dot(high, high) + (dot(high, low) + dot(low, high)))
    high, low = split(dot(seed, high) + dot(seed, low))
    high_ref[0] = high
    low_ref[0] = low


def gram_kernel(slots, block_ref, extra_ref, _, out_ref, square_ref, diagonal_ref):
    devices, tiles, rows, lane_count = block_ref.shape
    order = tiles * lane_count
    for side, gram in enumerate(grams_of(whole_block(block_ref))):
        gram = gram.astype(jnp.bfloat16)
        for tile in range(tiles):
            out_ref[:, side * tiles + tile] = gram[
                :, tile * lane_count : (tile + 1) * lane_count
            ].reshape(devices, rows, lane_count)
    sums = []
    for tile in range(tiles):
        total = jnp.zeros((rows, lane_count), jnp.float32)
        for source in range(tile * devices // tiles, (tile + 1) * devices // tiles):
            total = total + extra_ref[source, 0].astype(jnp.float32)
        sums.append(total)
    tile_row = sublanes((rows, lane_count))
    for slot in range(slots):
        diagonal_ref[slot : slot + 1, :] = jnp.concatenate(
            [
                jnp.sum(jnp.where(tile_row == slot, total, 0.0), axis=0, keepdims=True)
                for total in sums
            ],
            axis=1,
        )
    total = functools.reduce(jnp.add, sums)
    terms = (tile_row >= slots) & (tile_row < slots + 3)
    square = jnp.sum(jnp.where(terms, total, 0.0), axis=0, keepdims=True)
    square_ref[...] = jnp.broadcast_to(square, square_ref.shape)


def adam_kernel(order, scale_ref, grads_ref, second_ref, new_ref, tile_ref):
    rows_dev, rows, width = grads_ref.shape
    cols = width // order
    scale = scale_ref[0]
    sums = jnp.zeros((1, LANES), jnp.float32)
    lane = lanes((1, LANES))
    for k in range(rows_dev * cols):
        where = (k // cols, slice(None), slice((k % cols) * order, (k % cols + 1) * order))
        clipped = grads_ref[where].astype(jnp.float32) * scale
        second = 0.95 * second_ref[where] + 0.05 * clipped * clipped
        new_ref[where] = second
        step = clipped / (jnp.sqrt(second) + 1e-08)
        sums = jnp.where(lane == k, jnp.sum(step * step, keepdims=True), sums)
    tile_row = sublanes(tile_ref.shape)
    tile = jnp.zeros(tile_ref.shape, jnp.float32)
    for place, term in enumerate(thirds(sums)):
        tile = jnp.where(tile_row == place, term, tile)
    tile_ref[...] = tile.astype(jnp.bfloat16)


def owner_kernel(
    me_ref,
    owner_ref,
    factor_ref,
    block_ref,
    mixed_ref,
    seed_ref,
    high_ref,
    low_ref,
    diagonal_ref,
    adam_ref,
    roots_ref,
    out_ref,
):
    slot = pl.program_id(0)
    devices, tiles, rows, lane_count = block_ref.shape
    order = tiles * lane_count
    me = me_ref[0]
    load = jnp.int32(0)
    for k in range(owner_ref.shape[0]):
        load = load + (owner_ref[k] == me).astype(jnp.int32)
    live = slot < load
    factor = factor_ref[0]
    block = whole_block(block_ref)
    mixed = whole_block(mixed_ref).astype(jnp.float32)
    turned = mixed.T
    row, col = sublanes((order, order)), lanes((order, order))
    diagonal = diagonal_ref[pl.ds(slot, 1), :]
    left_old = jnp.where(col <= row, mixed, turned)
    right_old = jnp.where(col > row, mixed, jnp.where(col == row, diagonal, turned))
    left_gram, right_gram = grams_of(block)

    def new_root(side, old, gram):
        high, low = split(BETA * old + factor * gram)
        fifth_high, fifth_low = high_ref[side, 0], low_ref[side, 0]
        moved = dot(fifth_high, high) + (dot(fifth_high, low) + dot(fifth_low, high))
        seed = seed_ref[side, 0]
        root = (1.25 * seed.astype(jnp.float32) - 0.25 * moved).astype(jnp.bfloat16)
        roots_ref[side, 0] = jnp.where(live, root, seed)
        return root

    left_root = new_root(0, left_old, left_gram)
    right_root = new_root(1, right_old, right_gram)
    applied = dot(left_root, block).astype(jnp.bfloat16)
    direction = dot(applied, right_root).astype(jnp.bfloat16).astype(jnp.float32)
    norm = jnp.sqrt(jnp.sum(direction * direction, keepdims=True)) + 1e-06
    unit = (direction / norm).astype(jnp.bfloat16)
    for tile in range(tiles):
        out_ref[:, pl.ds(slot * tiles + tile, 1)] = unit[
            :, tile * lane_count : (tile + 1) * lane_count
        ].reshape(devices, 1, rows, lane_count)

    @pl.when(slot == 0)
    def _():
        out_ref[:, out_ref.shape[1] - 1] = jnp.broadcast_to(
            adam_ref[...][None], (devices, rows, lane_count)
        )


def stats_kernel(factor_ref, left_ref, right_ref, gram_ref, new_left_ref, new_right_ref):
    factor = factor_ref[0]
    tiles = gram_ref.shape[1] // 2
    for side, (old_ref, new_ref) in enumerate(
        ((left_ref, new_left_ref), (right_ref, new_right_ref))
    ):
        for tile in range(tiles):
            part = slice(tile * LANES, (tile + 1) * LANES)
            new_ref[:, :, part] = BETA * old_ref[:, :, part] + factor * gram_ref[
                :, side * tiles + tile
            ].astype(jnp.float32)


def place_kernel(order, owner_ref, back_ref, out_ref, taken_ref):
    rows_dev, rows, width = out_ref.shape
    cols = width // order
    tiles = order // LANES
    devices, extra = back_ref.shape[0], back_ref.shape[1] - 1
    total = jnp.zeros((rows, LANES), jnp.float32)
    for source in range(devices):
        taken_ref[source] = 0
        total = total + back_ref[source, extra].astype(jnp.float32)
    norms = jnp.sqrt(jnp.sum(total, axis=0, keepdims=True))
    lane = lanes((1, LANES))
    for k in range(rows_dev * cols):
        owner = owner_ref[k]
        slot = taken_ref[owner]
        taken_ref[owner] = slot + 1
        norm = jnp.sum(jnp.where(lane == k, norms, 0.0), axis=1, keepdims=True)
        for tile in range(tiles):
            first = (k % cols) * order + tile * LANES
            out_ref[k // cols, :, first : first + LANES] = (
                back_ref[owner, slot * tiles + tile].astype(jnp.float32) * norm
            ).astype(jnp.bfloat16)


def butterfly(values, axis):
    size = lax.axis_size(axis)
    step = 1
    while step < size:
        values = values + lax.ppermute(values, axis, [(i, i ^ step) for i in range(size)])
        step *= 2
    return values


def exchange(values):
    return lax.all_to_all(values, "blk", split_axis=0, concat_axis=0, tiled=True)


def cost(passes, order, moved):
    return pl.CostEstimate(
        flops=2 * passes * order**3, bytes_accessed=moved, transcendentals=0
    )


def local(grads, owners, left_stats, right_stats, second_moment, roots):
    devices = lax.axis_size("blk")
    rows_dev, rows, width = grads.shape
    order = left_stats.shape[-1]
    cols = width // order
    blocks = rows_dev * cols
    slots = roots.shape[2]
    tiles = order // LANES
    me = lax.axis_index("blk").astype(jnp.int32).reshape(1)
    owner_of = owners.reshape(blocks)
    left_old, right_old = left_stats[0], right_stats[0]
    taken = [pltpu.SMEM((devices,), jnp.int32)]

    sent = pl.pallas_call(
        functools.partial(pack_kernel, slots),
        out_shape=jax.ShapeDtypeStruct(
            (devices, (2 * slots + 1) * tiles + 1, rows, LANES), jnp.bfloat16
        ),
        in_specs=[SMEM, SMEM, VMEM, VMEM, VMEM],
        out_specs=VMEM,
        scratch_shapes=taken,
        compiler_params=PARAMS,
        name="pack",
    )(me, owner_of, grads, left_old, right_old)
    arrived = exchange(sent)

    seeds = roots[0]
    square_spec = pl.BlockSpec((1, order, order), lambda i: (i, 0, 0))
    fifth_shape = jax.ShapeDtypeStruct((2 * slots, order, order), jnp.bfloat16)
    high, low = pl.pallas_call(
        fifth_kernel,
        grid=(2 * slots,),
        out_shape=[fifth_shape, fifth_shape],
        in_specs=[square_spec],
        out_specs=[square_spec, square_spec],
        compiler_params=PARAMS,
        cost_estimate=cost(12 * slots, order, 12 * slots * order * order),
        name="fifth",
    )(seeds.reshape(2 * slots, order, order))

    grams, square, diagonal = pl.pallas_call(
        functools.partial(gram_kernel, slots),
        grid=(1,),
        out_shape=[
            jax.ShapeDtypeStruct((devices, 2 * tiles, rows, LANES), jnp.bfloat16),
            jax.ShapeDtypeStruct((8, LANES), jnp.float32),
            jax.ShapeDtypeStruct((slots, order), jnp.float32),
        ],
        in_specs=[
            pl.BlockSpec((devices, tiles, rows, LANES), lambda i: (0, 2 * slots, 0, 0)),
            pl.BlockSpec(
                (devices, 1, rows, LANES), lambda i: (0, (2 * slots + 1) * tiles, 0, 0)
            ),
            pl.BlockSpec(memory_space=pl.ANY),
        ],
        out_specs=[
            pl.BlockSpec((devices, 2 * tiles, rows, LANES), lambda i: (0, 0, 0, 0)),
            pl.BlockSpec((8, LANES), lambda i: (0, 0)),
            pl.BlockSpec((slots, order), lambda i: (0, 0)),
        ],
        compiler_params=PARAMS,
        cost_estimate=cost(2, order, 6 * order * order),
        name="grams",
    )(arrived, arrived, low)
    grams_back = exchange(grams)

    total = butterfly(square, "zero")[0, 0]
    entries = rows_dev * lax.axis_size("zero") * order * width
    scale = jnp.minimum(1.0, math.sqrt(entries) / (jnp.sqrt(total) + 1e-06))
    factor = 0.05 * scale * scale
    new_second, adam = pl.pallas_call(
        functools.partial(adam_kernel, order),
        out_shape=[
            jax.ShapeDtypeStruct(second_moment.shape, jnp.float32),
            jax.ShapeDtypeStruct((rows, LANES), jnp.bfloat16),
        ],
        in_specs=[SMEM, VMEM, VMEM],
        out_specs=[VMEM, VMEM],
        compiler_params=PARAMS,
        name="adam",
    )(scale.reshape(1), grads, second_moment)
    side_spec = pl.BlockSpec((2, 1, order, order), lambda s: (0, s, 0, 0))
    new_roots, update = pl.pallas_call(
        owner_kernel,
        grid=(slots,),
        out_shape=[
            jax.ShapeDtypeStruct((2, slots, order, order), jnp.bfloat16),
            jax.ShapeDtypeStruct((devices, slots * tiles + 1, rows, LANES), jnp.bfloat16),
        ],
        in_specs=[
            SMEM,
            SMEM,
            SMEM,
            pl.BlockSpec((devices, tiles, rows, LANES), lambda s: (0, s, 0, 0)),
            pl.BlockSpec((devices, tiles, rows, LANES), lambda s: (0, slots + s, 0, 0)),
            side_spec,
            side_spec,
            side_spec,
            pl.BlockSpec((slots, order), lambda s: (0, 0)),
            pl.BlockSpec((rows, LANES), lambda s: (0, 0)),
        ],
        out_specs=[
            side_spec,
            pl.BlockSpec((devices, slots * tiles + 1, rows, LANES), lambda s: (0, 0, 0, 0)),
        ],
        compiler_params=PARAMS,
        cost_estimate=cost(10 * slots, order, 24 * slots * order * order),
        name="owner",
    )(
        me,
        owner_of,
        factor.reshape(1),
        arrived,
        arrived,
        seeds,
        high.reshape(2, slots, order, order),
        low.reshape(2, slots, order, order),
        diagonal,
        adam,
    )
    update_back = exchange(update)

    new_left, new_right = pl.pallas_call(
        stats_kernel,
        grid=(blocks // 4,),
        out_shape=[jax.ShapeDtypeStruct(left_old.shape, jnp.float32)] * 2,
        in_specs=[
            SMEM,
            pl.BlockSpec((4, rows, order), lambda i: (i, 0, 0)),
            pl.BlockSpec((4, rows, order), lambda i: (i, 0, 0)),
            pl.BlockSpec((4, 2 * tiles, rows, LANES), lambda i: (i, 0, 0, 0)),
        ],
        out_specs=[pl.BlockSpec((4, rows, order), lambda i: (i, 0, 0))] * 2,
        compiler_params=PARAMS,
        name="stats",
    )(factor.reshape(1), left_old, right_old, grams_back)

    placed = pl.pallas_call(
        functools.partial(place_kernel, order),
        out_shape=jax.ShapeDtypeStruct((rows_dev, rows, width), jnp.bfloat16),
        in_specs=[SMEM, VMEM],
        out_specs=VMEM,
        scratch_shapes=taken,
        compiler_params=PARAMS,
        name="place",
    )(owner_of, update_back)
    return (placed, new_second, new_left[None], new_right[None], new_roots[None])


def solution(mesh):
    placed = (
        P("zero", "blk", None),
        P("zero", None, None),
        P("zero", None, "blk", None),
        P("zero", None, "blk", None),
        P("zero", "blk", None),
        P("zero", None, "blk", None, None),
    )
    return jax.shard_map(
        local,
        mesh=mesh,
        in_specs=placed,
        out_specs=(
            P("zero", "blk", None),
            P("zero", "blk", None),
            P("zero", None, "blk", None),
            P("zero", None, "blk", None),
            P("zero", None, "blk", None, None),
        ),
        check_vma=False,
    )
```

time: 193 us -> 158 us (0.82)
  blocking collectives: 74.4 us -> 0 us
  waiting for transfers between devices: 37.2 us -> 89.7 us
  starting transfers between devices: 38.6 us -> 26.7 us
  other arithmetic: 8.1 us -> 0.01 us
  Pallas kernels: 30.5 us -> 36.5 us
    all_to_all x2 -> x3, waiting for transfers between devices: 0.01 us -> 81.5 us  [exchange(): lax.all_to_all(values, 'blk', split_axis=0, concat_axis=0, tiled=True)]
    all_to_all x1 -> x0, blocking collectives: 74.4 us -> none  [exchange(): lax.all_to_all(values, 'blk', split_axis=0, concat_axis=0, tiled=True)]
    ppermute x13 -> x3, waiting for transfers between devices: 37.2 us -> 8.16 us  [butterfly(): lax.ppermute(values, axis, [(i, i ^ step) for i in range(size)])]
    ppermute x13 -> x3, starting transfers between devices: 28.6 us -> 1.81 us  [butterfly(): lax.ppermute(values, axis, [(i, i ^ step) for i in range(size)])]
    all_to_all x2 -> x3, starting transfers between devices: 9.99 us -> 24.9 us  [exchange(): lax.all_to_all(values, 'blk', split_axis=0, concat_axis=0, tiled=True)]
    pallas_call x3 -> x4, Pallas kernels: 6.93 us -> 12.5 us  [the longest x1 4.78 us: local(): pl.pallas_call(stats_kernel, grid=(blocks // 4,), out_shape=[jax.ShapeDty...]
    add x1 -> x0, other arithmetic: 2.58 us -> none  [local(): BETA * right_old + factor * grams_back[:blocks, 1].astype(jnp.float32)]
    reduce_sum x2 -> x0, other arithmetic: 2.57 us -> none  [local(): jnp.sum((adam_step * adam_step).reshape(rows_dev, rows, cols, order), axi...]
  transfers between devices with their start and end apart: 15 -> 6, of which waited for: 12 -> 6; matrix products, arithmetic and copies ran while one was open for 5% -> 0% of each run, Pallas kernels for 12% -> 18%
where the time goes in v2:
time: 158 us; the launch traced here: 157 us
  waiting for transfers between devices  89.7 us (57%)
  Pallas kernels  36.5 us (23%)
  starting transfers between devices  26.7 us (17%)
  local copies, waits for them, and re-layouts  3.11 us (2%)
    all_to_all x3, waiting for transfers between devices, exchange(): lax.all_to_all(values, 'blk', split_axis=0, concat_axis=0, tiled=True)  81.5 us
    all_to_all x3, starting transfers between devices, exchange(): lax.all_to_all(values, 'blk', split_axis=0, concat_axis=0, tiled=True)  24.9 us
    pallas_call x1, Pallas kernels, local(): pl.pallas_call(owner_kernel, grid=(slots,), out_shape=[jax.ShapeDtypeStru...  10.7 us
    pallas_call x1, Pallas kernels, local(): pl.pallas_call(fifth_kernel, grid=(2 * slots,), out_shape=[fifth_shape, f...  9.82 us
    ppermute x3, waiting for transfers between devices, butterfly(): lax.ppermute(values, axis, [(i, i ^ step) for i in range(size)])  8.16 us
    pallas_call x1, Pallas kernels, local(): pl.pallas_call(stats_kernel, grid=(blocks // 4,), out_shape=[jax.ShapeDty...  4.78 us
    pallas_call x1, Pallas kernels, local(): pl.pallas_call(functools.partial(pack_kernel, slots), out_shape=jax.Shape...  3.5 us
  transfers between devices with their start and end apart: 6, of which 6 were waited for; matrix products, arithmetic and copies ran while one was open for 0% of the time, Pallas kernels for 18%

profile of v2, /device:TPU:4, one launch (start us, length us, event | category | flops | bytes accessed | tf_op | source)
XLA Modules:
  0.0 157.4 jit_solution(1955138883335748935)
XLA Ops:
  0.6 3.5 %pack.1 = bf16[32,21,16,128]{3,2,1,0:T(8,128)(2,1)} custom-call(s32[1]{0:T(128)} %bitcast.1.me_ref, s32[24]{0:T(128)} %bitcast.19, bf16[2,16,6144]{2,1,0:T(8,128)(2,1)} %grads_ref.3, f32[24,16,512]{2,1,0:T(8,128)} %bitcast.14, f32[24,16,512]{2,1,0:T(8,128)} %bitcast.16), custom_call_target="tpu_custom_call" | custom-call | tf_op jit(solution)/shard_map/pack/pallas_call | solution.py:296
  4.1 11.5 %all-to-all-start = ((bf16[32,21,16,128]{3,2,1,0:T(8,128)(2,1)}), bf16[32,21,16,128]{3,2,1,0:T(8,128)(2,1)S(1)}, u32[]{:S(2)}, u32[]{:S(2)}) async-start(bf16[32,21,16,128]{3,2,1,0:T(8,128)(2,1)} %pack.1), calls=%async_computation | async-start | bytes 5505024 | tf_op jit(solution)/shard_map/all_to_all | solution.py:274
  15.6 9.8 %fifth.1 = (bf16[4,512,512]{2,1,0:T(8,128)(2,1)}, bf16[4,512,512]{2,1,0:T(8,128)(2,1)}) custom-call(bf16[4,512,512]{2,1,0:T(8,128)(2,1)} %bitcast.22), custom_call_target="tpu_custom_call" | custom-call | flops 6442450944 | bytes 6291456 | tf_op jit(solution)/shard_map/fifth/pallas_call | solution.py:312
  25.4 54.2 %all-to-all-done.block_ref.extra_ref.mixed_ref = bf16[32,21,16,128]{3,2,1,0:T(8,128)(2,1)S(1)} async-done(((bf16[32,21,16,128]{3,2,1,0:T(8,128)(2,1)}), bf16[32,21,16,128]{3,2,1,0:T(8,128)(2,1)S(1)}, u32[]{:S(2)}, u32[]{:S(2)}) %all-to-all-start) | async-done | bytes 2752544 | tf_op jit(solution)/shard_map/all_to_all | solution.py:274
  79.6 0.0 copy-start
  79.6 1.5 copy-done
  81.2 2.9 %grams.1 = (bf16[32,8,16,128]{3,2,1,0:T(8,128)(2,1)}, f32[8,128]{1,0:T(8,128)}, f32[2,512]{1,0:T(2,128)}) custom-call(bf16[32,21,16,128]{3,2,1,0:T(8,128)(2,1)} %copy-done, bf16[32,21,16,128]{3,2,1,0:T(8,128)(2,1)} %copy-done, bf16[4,512,512]{2,1,0:T(8,128)(2,1)} %get-tuple-element.16._), custom_call_target="tpu_custom_call" | custom-call | flops 536870912 | bytes 1572864 | tf_op jit(solution)/shard_map/grams/pallas_call | solution.py:323
  84.0 0.0 copy-start.3
  84.0 6.3 %all-to-all-start.2 = ((bf16[32,8,16,128]{3,2,1,0:T(8,128)(2,1)}), bf16[32,8,16,128]{3,2,1,0:T(8,128)(2,1)S(1)}, u32[]{:S(2)}, u32[]{:S(2)}) async-start(bf16[32,8,16,128]{3,2,1,0:T(8,128)(2,1)} %get-tuple-element.23), calls=%async_computation.2 | async-start | bytes 2097152 | tf_op jit(solution)/shard_map/all_to_all | solution.py:274
  90.3 0.0 copy-done.3
  90.3 0.1 collective-permute-start
  90.4 1.2 collective-permute-done
  91.6 1.2 collective-permute-start.1
  92.8 2.4 %collective-permute-done.1 = f32[8,128]{1,0:T(8,128)S(1)} collective-permute-done((f32[8,128]{1,0:T(8,128)S(1)}, f32[8,128]{1,0:T(8,128)S(1)}, u32[]{:S(2)}, u32[]{:S(2)}) %collective-permute-start.1) | collective-permute-done | bytes 4128 | tf_op jit(solution)/shard_map/ppermute | solution.py:268
  95.2 0.5 collective-permute-start.2
  95.7 4.6 %collective-permute-done.2 = f32[8,128]{1,0:T(8,128)S(1)} collective-permute-done((f32[8,128]{1,0:T(8,128)S(1)}, f32[8,128]{1,0:T(8,128)S(1)}, u32[]{:S(2)}, u32[]{:S(2)}) %collective-permute-start.2) | collective-permute-done | bytes 4128 | tf_op jit(solution)/shard_map/ppermute | solution.py:268
  100.3 0.5 slice.3
  101.6 2.6 %adam.1 = (f32[2,16,6144]{2,1,0:T(8,128)}, bf16[16,128]{1,0:T(8,128)(2,1)}) custom-call(f32[1]{0:T(128)} %bitcast.10.scale_ref, bf16[2,16,6144]{2,1,0:T(8,128)(2,1)} %grads_ref.3, f32[2,16,6144]{2,1,0:T(8,128)} %second_ref.1), custom_call_target="tpu_custom_call" | custom-call | tf_op jit(solution)/shard_map/adam/pallas_call | solution.py:353
  104.1 10.7 %owner.1 = (bf16[2,2,512,512]{3,2,1,0:T(8,128)(2,1)}, bf16[32,9,16,128]{3,2,1,0:T(8,128)(2,1)}) custom-call(s32[1]{0:T(128)} %bitcast.1.me_ref, s32[24]{0:T(128)} %bitcast.20, f32[1]{0:T(128)} %bitcast.6.factor_ref, bf16[32,21,16,128]{3,2,1,0:T(8,128)(2,1)} %copy-done, bf16[32,21,16,128]{3,2,1,0:T(8,128)(2,1)} %copy-done, bf16[2,2,512,512]{3,2,1,0:T(8,128)(2,1)} %bitcast.23, ...), custom_call_target="tpu_custom_call" | custom-call | flops 5368709120 | bytes 12582912 | tf_op jit(solution)/shard_map/owner/pallas_call | solution.py:365
  114.8 2.7 %all-to-all-done.2.gram_ref = bf16[32,8,16,128]{3,2,1,0:T(8,128)(2,1)S(1)} async-done(((bf16[32,8,16,128]{3,2,1,0:T(8,128)(2,1)}), bf16[32,8,16,128]{3,2,1,0:T(8,128)(2,1)S(1)}, u32[]{:S(2)}, u32[]{:S(2)}) %all-to-all-start.2) | async-done | bytes 1048608 | tf_op jit(solution)/shard_map/all_to_all | solution.py:274
  117.6 0.0 copy-start.2
  117.6 7.1 %all-to-all-start.1 = ((bf16[32,9,16,128]{3,2,1,0:T(8,128)(2,1)}), bf16[32,9,16,128]{3,2,1,0:T(8,128)(2,1)S(1)}, u32[]{:S(2)}, u32[]{:S(2)}) async-start(bf16[32,9,16,128]{3,2,1,0:T(8,128)(2,1)} %get-tuple-element.21), calls=%async_computation.1 | async-start | bytes 2359296 | tf_op jit(solution)/shard_map/all_to_all | solution.py:274
  124.7 0.0 copy-done.2
  124.7 4.8 %stats.1 = (f32[24,16,512]{2,1,0:T(8,128)}, f32[24,16,512]{2,1,0:T(8,128)}) custom-call(f32[1]{0:T(128)} %bitcast.6.factor_ref, f32[24,16,512]{2,1,0:T(8,128)} %bitcast.15, f32[24,16,512]{2,1,0:T(8,128)} %bitcast.17, bf16[32,8,16,128]{3,2,1,0:T(8,128)(2,1)} %copy-done.2), custom_call_target="tpu_custom_call" | custom-call | tf_op jit(solution)/shard_map/stats/pallas_call | solution.py:405
  129.5 24.6 %all-to-all-done.1.back_ref = bf16[32,9,16,128]{3,2,1,0:T(8,128)(2,1)S(1)} async-done(((bf16[32,9,16,128]{3,2,1,0:T(8,128)(2,1)}), bf16[32,9,16,128]{3,2,1,0:T(8,128)(2,1)S(1)}, u32[]{:S(2)}, u32[]{:S(2)}) %all-to-all-start.1) | async-done | bytes 1179680 | tf_op jit(solution)/shard_map/all_to_all | solution.py:274
  154.1 0.0 copy-start.1
  154.1 1.0 copy-done.1
  155.1 2.2 %place.1 = bf16[2,16,6144]{2,1,0:T(8,128)(2,1)} custom-call(s32[24]{0:T(128)} %bitcast.21, bf16[32,9,16,128]{3,2,1,0:T(8,128)(2,1)} %copy-done.1), custom_call_target="tpu_custom_call" | custom-call | tf_op jit(solution)/shard_map/place/pallas_call | solution.py:420
  (3 shorter events, 0.0 us)
Async XLA Ops:
  4.1 75.5 %all-to-all-start = ((bf16[32,21,16,128]{3,2,1,0:T(8,128)(2,1)}), bf16[32,21,16,128]{3,2,1,0:T(8,128)(2,1)S(1)}, u32[]{:S(2)}, u32[]{:S(2)}) async-start(bf16[32,21,16,128]{3,2,1,0:T(8,128)(2,1)} %pack.1), calls=%async_computation | async-start | bytes 5505024 | tf_op jit(solution)/shard_map/all_to_all | solution.py:274
  79.6 1.5 copy-start
  84.0 6.3 %copy-start.3 = (f32[8,128]{1,0:T(8,128)S(1)}, f32[8,128]{1,0:T(8,128)}, u32[]{:S(2)}) copy-start(f32[8,128]{1,0:T(8,128)} %get-tuple-element.17) | copy-start | bytes 12292
  84.0 33.5 %all-to-all-start.2 = ((bf16[32,8,16,128]{3,2,1,0:T(8,128)(2,1)}), bf16[32,8,16,128]{3,2,1,0:T(8,128)(2,1)S(1)}, u32[]{:S(2)}, u32[]{:S(2)}) async-start(bf16[32,8,16,128]{3,2,1,0:T(8,128)(2,1)} %get-tuple-element.23), calls=%async_computation.2 | async-start | bytes 2097152 | tf_op jit(solution)/shard_map/all_to_all | solution.py:274
  90.3 1.3 collective-permute-start
  91.6 3.6 %collective-permute-start.1 = (f32[8,128]{1,0:T(8,128)S(1)}, f32[8,128]{1,0:T(8,128)S(1)}, u32[]{:S(2)}, u32[]{:S(2)}) collective-permute-start(f32[8,128]{1,0:T(8,128)S(1)} %add.13), channel_id=1, source_target_pairs={{0,2},{1,3},{2,0},{3,1},{4,6},{5,7},{6,4},{7,5},{8,10},{9,11},{10,... | collective-permute-start | bytes 12296 | tf_op jit(solution)/shard_map/ppermute | solution.py:268
  95.2 5.1 %collective-permute-start.2 = (f32[8,128]{1,0:T(8,128)S(1)}, f32[8,128]{1,0:T(8,128)S(1)}, u32[]{:S(2)}, u32[]{:S(2)}) collective-permute-start(f32[8,128]{1,0:T(8,128)S(1)} %add.14), channel_id=1, source_target_pairs={{0,4},{1,5},{2,6},{3,7},{4,0},{5,1},{6,2},{7,3},{8,12},{9,13},{10,... | collective-permute-start | bytes 12296 | tf_op jit(solution)/shard_map/ppermute | solution.py:268
  117.6 7.1 %copy-start.2 = (bf16[32,8,16,128]{3,2,1,0:T(8,128)(2,1)}, bf16[32,8,16,128]{3,2,1,0:T(8,128)(2,1)S(1)}, u32[]{:S(2)}) copy-start(bf16[32,8,16,128]{3,2,1,0:T(8,128)(2,1)S(1)} %all-to-all-done.2.gram_ref) | copy-start | bytes 3145732
  117.6 36.5 %all-to-all-start.1 = ((bf16[32,9,16,128]{3,2,1,0:T(8,128)(2,1)}), bf16[32,9,16,128]{3,2,1,0:T(8,128)(2,1)S(1)}, u32[]{:S(2)}, u32[]{:S(2)}) async-start(bf16[32,9,16,128]{3,2,1,0:T(8,128)(2,1)} %get-tuple-element.21), calls=%async_computation.1 | async-start | bytes 2359296 | tf_op jit(solution)/shard_map/all_to_all | solution.py:274
  154.1 1.0 copy-start.1

commit v3 on v2

v3 whole, which is shorter than its diff:
```python
import functools
import math

import jax
import jax.numpy as jnp
from jax import lax
from jax.experimental import pallas as pl
from jax.experimental.pallas import tpu as pltpu
from jax.sharding import PartitionSpec as P

BETA = 0.95
VMEM_LIMIT = 56 * 1024 * 1024
VMEM = pl.BlockSpec(memory_space=pltpu.VMEM)
SMEM = pl.BlockSpec(memory_space=pltpu.SMEM)
PARAMS = pltpu.CompilerParams(vmem_limit_bytes=VMEM_LIMIT)


def dot(former, latter):
    return jnp.dot(former, latter, preferred_element_type=jnp.float32)


def split(wide):
    high = wide.astype(jnp.bfloat16)
    return high, (wide - high.astype(jnp.float32)).astype(jnp.bfloat16)


LANES = 128


def sublanes(shape):
    return lax.broadcasted_iota(jnp.int32, shape, len(shape) - 2)


def lanes(shape):
    return lax.broadcasted_iota(jnp.int32, shape, len(shape) - 1)


def store_piece(ref, place, first, piece):
    for tile in range(piece.shape[-1] // LANES):
        ref[place, first + tile] = piece[:, tile * LANES : (tile + 1) * LANES]


def whole_block(ref):
    devices, tiles, rows, _ = ref.shape
    return jnp.concatenate(
        [ref[:, tile].reshape(devices * rows, LANES) for tile in range(tiles)], axis=1
    )


OWNER, HELPER, SPARE = 0, 1, 2


class Plan:
    def __init__(self, ref, blocks, devices):
        self.ref, self.blocks, self.devices = ref, blocks, devices

    @staticmethod
    def size(blocks, devices):
        return 3 * blocks + 3 * devices + 4

    def at(self, part, index):
        blocks, devices = self.blocks, self.devices
        start = {
            "slot": 0,
            "single": blocks,
            "owner": 2 * blocks,
            "load": 3 * blocks,
            "helper": 3 * blocks + devices,
            "idle": 3 * blocks + 2 * devices,
            "role": 3 * blocks + 3 * devices + 1,
            "own": 3 * blocks + 3 * devices + 2,
        }[part]
        return start + index

    def get(self, part, index=0):
        return self.ref[self.at(part, index)]

    def put(self, part, index, value):
        self.ref[self.at(part, index)] = value

    def share(self):
        return self.blocks // (self.devices - self.blocks)

    def spare_of(self, block):
        return self.get("idle", block // self.share())

    def fill(self, owner_ref, me):
        blocks, devices = self.blocks, self.devices
        spares = devices - blocks
        for device in range(devices):
            self.put("load", device, 0)
        for k in range(blocks):
            owner = owner_ref[k]
            slot = self.get("load", owner)
            self.put("owner", k, owner)
            self.put("slot", k, slot)
            self.put("load", owner, slot + 1)
        count, role = jnp.int32(0), jnp.int32(OWNER)
        for device in range(devices):
            idle = self.get("load", device) == 0
            self.put("idle", count, device)
            kind = jnp.where(count < spares, SPARE, HELPER)
            role = jnp.where(idle & (me == device), kind, role)
            count = count + idle.astype(jnp.int32)
        count = jnp.int32(spares)
        for device in range(devices):
            double = self.get("load", device) == 2
            helper = self.get("idle", jnp.minimum(count, devices - 1))
            self.put("helper", device, jnp.where(double, helper, device))
            count = count + double.astype(jnp.int32)
        for k in range(blocks):
            load = self.get("load", self.get("owner", k))
            self.put("single", k, (load == 1).astype(jnp.int32))
        self.put("role", 0, role)
        self.put("own", 0, self.get("load", me))


def pack_kernel(slots, me_ref, owner_ref, grads_ref, left_ref, right_ref, out_ref, plan_ref):
    rows_dev, rows, width = grads_ref.shape
    order = left_ref.shape[-1]
    cols = width // order
    blocks = rows_dev * cols
    tiles = order // LANES
    devices, extra = out_ref.shape[0], out_ref.shape[1] - 1
    me = me_ref[0]
    plan = Plan(plan_ref, blocks, devices)
    plan.fill(owner_ref, me)
    tile_row = sublanes((rows, LANES))
    for owner in range(devices):
        out_ref[owner, extra] = jnp.zeros((rows, LANES), jnp.bfloat16)
    row = me * rows + sublanes((rows, order))
    lower = lanes((rows, order)) <= row
    mine = lanes((rows, order)) == row
    for k in range(blocks):
        owner, slot = plan.get("owner", k), plan.get("slot", k)
        piece = grads_ref[k // cols, :, (k % cols) * order : (k % cols + 1) * order]
        store_piece(out_ref, owner, slot * tiles, piece)
        store_piece(out_ref, plan.get("helper", owner), slot * tiles, piece)
        store_piece(out_ref, plan.spare_of(k), k % plan.share() * tiles, piece)
        right = right_ref[k]
        mixed = jnp.where(lower, left_ref[k], right).astype(jnp.bfloat16)
        store_piece(out_ref, owner, (slots + slot) * tiles, mixed)
        marked = jnp.where(mine, right, 0.0)
        diagonal = marked[:, :LANES]
        for tile in range(1, tiles):
            diagonal = diagonal + marked[:, tile * LANES : (tile + 1) * LANES]
        diagonal = jnp.sum(diagonal, axis=0, keepdims=True)
        out_ref[owner, extra] = jnp.where(
            tile_row == slot, diagonal, out_ref[owner, extra].astype(jnp.float32)
        ).astype(jnp.bfloat16)


def square_kernel(grads_ref, _, __, out_ref):
    rows_dev, rows, width = grads_ref.shape
    total = jnp.zeros((8, 4 * LANES), jnp.float32)
    for i in range(rows_dev):
        for part in range(width // (4 * LANES)):
            wide = grads_ref[i, :, part * 4 * LANES : (part + 1) * 4 * LANES].astype(jnp.float32)
            wide = wide * wide
            for half in range(rows // 8):
                total = total + wide[8 * half : 8 * half + 8]
    out_ref[...] = jnp.broadcast_to(jnp.sum(total, keepdims=True), out_ref.shape)


def fifth_kernel(seed_ref, high_ref, low_ref):
    seed = seed_ref[0]
    high, low = split(dot(seed, seed))
    high, low = split(dot(high, high) + (dot(high, low) + dot(low, high)))
    high, low = split(dot(seed, high) + dot(seed, low))
    high_ref[0] = high
    low_ref[0] = low


def adam_kernel(order, scale_ref, grads_ref, second_ref, _, new_ref, sums_ref):
    rows_dev, rows, width = grads_ref.shape
    cols = width // order
    scale = scale_ref[0]
    sums = jnp.zeros((1, LANES), jnp.float32)
    lane = lanes((1, LANES))
    for k in range(rows_dev * cols):
        where = (k // cols, slice(None), slice((k % cols) * order, (k % cols + 1) * order))
        clipped = grads_ref[where].astype(jnp.float32) * scale
        second = 0.95 * second_ref[where] + 0.05 * clipped * clipped
        new_ref[where] = second
        step = clipped / (jnp.sqrt(second) + 1e-08)
        sums = jnp.where(lane == k, jnp.sum(step * step, keepdims=True), sums)
    sums_ref[...] = jnp.broadcast_to(sums, sums_ref.shape)


def owner_kernel(
    blocks,
    plan_ref,
    factor_ref,
    block_ref,
    mixed_ref,
    seed_ref,
    high_ref,
    low_ref,
    extra_ref,
    roots_ref,
    out_ref,
):
    slot = pl.program_id(0)
    devices, tiles, rows, lane_count = block_ref.shape
    order = tiles * lane_count
    plan = Plan(plan_ref, blocks, devices)
    role, load = plan.get("role"), plan.get("own")
    live = slot < load
    factor = factor_ref[0]

    def put(first, value):
        value = value.astype(jnp.bfloat16)
        for tile in range(value.shape[1] // lane_count):
            out_ref[:, pl.ds(first + tile, 1)] = value[
                :, tile * lane_count : (tile + 1) * lane_count
            ].reshape(devices, 1, rows, lane_count)

    def right_gram(block):
        return lax.dot_general(
            block, block, (((0,), (0,)), ((), ())), preferred_element_type=jnp.float32
        )

    def left_part(block, start, stop):
        return lax.dot_general(
            block,
            block[start:stop],
            (((1,), (1,)), ((), ())),
            preferred_element_type=jnp.float32,
        )

    @pl.when(live)
    def _():
        block = whole_block(block_ref)
        mixed = whole_block(mixed_ref).astype(jnp.float32)
        turned = mixed.T
        row, col = sublanes((order, order)), lanes((order, order))
        diagonal = []
        tile_row = sublanes((rows, lane_count))
        for tile in range(tiles):
            total = jnp.zeros((rows, lane_count), jnp.float32)
            for source in range(tile * devices // tiles, (tile + 1) * devices // tiles):
                total = total + extra_ref[source, 0].astype(jnp.float32)
            diagonal.append(
                jnp.sum(jnp.where(tile_row == slot, total, 0.0), axis=0, keepdims=True)
            )
        diagonal = jnp.concatenate(diagonal, axis=1)
        left_old = jnp.where(col <= row, mixed, turned)
        right_old = jnp.where(col > row, mixed, jnp.where(col == row, diagonal, turned))
        left, right = left_part(block, 0, order), right_gram(block)

        def new_root(side, old, gram):
            high, low = split(BETA * old + factor * gram)
            fifth_high, fifth_low = high_ref[side, 0], low_ref[side, 0]
            moved = dot(fifth_high, high) + (dot(fifth_high, low) + dot(fifth_low, high))
            seed = seed_ref[side, 0]
            root = (1.25 * seed.astype(jnp.float32) - 0.25 * moved).astype(jnp.bfloat16)
            roots_ref[side, 0] = root
            return root

        left_root = new_root(0, left_old, left)
        right_root = new_root(1, right_old, right)
        applied = dot(left_root, block).astype(jnp.bfloat16)
        direction = dot(applied, right_root).astype(jnp.bfloat16).astype(jnp.float32)
        norm = jnp.sqrt(jnp.sum(direction * direction, keepdims=True)) + 1e-06
        put(slot * tiles, direction / norm)

        @pl.when(slot == 0)
        def _():
            put(2 * tiles, left[:, :lane_count])

        @pl.when(load == 1)
        def _():
            put(tiles, right)

    @pl.when(jnp.logical_not(live))
    def _():
        roots_ref[...] = seed_ref[...]

    @pl.when(role == HELPER)
    def _():
        block = whole_block(block_ref)
        put(slot * tiles, right_gram(block))

        @pl.when(slot == 1)
        def _():
            put(2 * tiles, left_part(block, 0, lane_count))

    @pl.when(role == SPARE)
    def _():
        put(slot * (tiles - 1), left_part(whole_block(block_ref), lane_count, order))

        @pl.when(slot == 0)
        def _():
            put(2 * (tiles - 1), left_part(whole_block(mixed_ref), lane_count, order))


def finish_kernel(
    plan_ref,
    factor_ref,
    left_ref,
    right_ref,
    back_ref,
    sums_ref,
    out_ref,
    new_left_ref,
    new_right_ref,
):
    rows_dev, rows, width = out_ref.shape
    blocks, _, order = left_ref.shape
    cols = width // order
    tiles = order // LANES
    plan = Plan(plan_ref, blocks, back_ref.shape[0])
    factor = factor_ref[0]
    norms = jnp.sqrt(sums_ref[:1, :])
    lane = lanes((1, LANES))
    for k in range(blocks):
        owner, slot = plan.get("owner", k), plan.get("slot", k)
        helper, single = plan.get("helper", owner), plan.get("single", k)
        spare = plan.spare_of(k)
        norm = jnp.sum(jnp.where(lane == k, norms, 0.0), axis=1, keepdims=True)
        right_from = jnp.where(single == 1, 1, slot) * tiles
        for tile in range(tiles):
            part = slice(tile * LANES, (tile + 1) * LANES)
            first = (k % cols) * order + tile * LANES
            out_ref[k // cols, :, first : first + LANES] = (
                back_ref[owner, slot * tiles + tile].astype(jnp.float32) * norm
            ).astype(jnp.bfloat16)
            if tile == 0:
                gram = back_ref[jnp.where(slot == 0, owner, helper), 2 * tiles]
            else:
                gram = back_ref[spare, k % plan.share() * (tiles - 1) + tile - 1]
            new_left_ref[k, :, part] = BETA * left_ref[k, :, part] + factor * gram.astype(
                jnp.float32
            )
            gram = back_ref[helper, right_from + tile]
            new_right_ref[k, :, part] = BETA * right_ref[k, :, part] + factor * gram.astype(
                jnp.float32
            )


def butterfly(values, axis, steps):
    size = lax.axis_size(axis)
    for step in steps:
        values = values + lax.ppermute(values, axis, [(i, i ^ step) for i in range(size)])
    return values


def blk_sum(values, axis, bit):
    size, width, near, halves = lax.axis_size("blk"), lax.axis_size("zero"), 4, 2
    values = butterfly(values, "blk", (1, 2))
    parts = []
    for turn in range(size // near // halves):
        pairs = []
        for place in range(size):
            for group in range(width):
                upper = ((place if axis == "blk" else group) // bit) % 2
                shift = near * (turn + upper * (size // near // halves))
                source = (place + shift) % size
                pairs.append((source * width + group, place * width + group))
        parts.append(lax.ppermute(values, ("blk", "zero"), pairs))
    return butterfly(functools.reduce(jnp.add, parts), axis, (bit,))


def exchange(values):
    return lax.all_to_all(values, "blk", split_axis=0, concat_axis=0, tiled=True)


def cost(passes, order, moved):
    return pl.CostEstimate(
        flops=2 * passes * order**3, bytes_accessed=moved, transcendentals=0
    )


def local(grads, owners, left_stats, right_stats, second_moment, roots):
    devices = lax.axis_size("blk")
    rows_dev, rows, width = grads.shape
    order = left_stats.shape[-1]
    cols = width // order
    blocks = rows_dev * cols
    slots = roots.shape[2]
    tiles = order // LANES
    me = lax.axis_index("blk").astype(jnp.int32).reshape(1)
    owner_of = owners.reshape(blocks)
    left_old, right_old = left_stats[0], right_stats[0]

    sent, plan = pl.pallas_call(
        functools.partial(pack_kernel, slots),
        out_shape=[
            jax.ShapeDtypeStruct((devices, 2 * slots * tiles + 1, rows, LANES), jnp.bfloat16),
            jax.ShapeDtypeStruct((Plan.size(blocks, devices),), jnp.int32),
        ],
        in_specs=[SMEM, SMEM, VMEM, VMEM, VMEM],
        out_specs=[VMEM, SMEM],
        compiler_params=PARAMS,
        name="pack",
    )(me, owner_of, grads, left_old, right_old)
    arrived = exchange(sent)

    seeds = roots[0]
    square_spec = pl.BlockSpec((1, order, order), lambda i: (i, 0, 0))
    fifth_shape = jax.ShapeDtypeStruct((2 * slots, order, order), jnp.bfloat16)
    high, low = pl.pallas_call(
        fifth_kernel,
        grid=(2 * slots,),
        out_shape=[fifth_shape, fifth_shape],
        in_specs=[square_spec],
        out_specs=[square_spec, square_spec],
        compiler_params=PARAMS,
        cost_estimate=cost(12 * slots, order, 12 * slots * order * order),
        name="fifth",
    )(seeds.reshape(2 * slots, order, order))
    square = pl.pallas_call(
        square_kernel,
        out_shape=jax.ShapeDtypeStruct((8, LANES), jnp.float32),
        in_specs=[VMEM, pl.BlockSpec(memory_space=pl.ANY), pl.BlockSpec(memory_space=pl.ANY)],
        out_specs=VMEM,
        compiler_params=PARAMS,
        name="square",
    )(grads, low, sent)
    total = blk_sum(butterfly(square, "zero", (1, 2, 4)), "zero", 1)[0, 0]
    entries = rows_dev * lax.axis_size("zero") * order * width
    scale = jnp.minimum(1.0, math.sqrt(entries) / (jnp.sqrt(total) + 1e-06))
    factor = (0.05 * scale * scale).reshape(1)

    side_spec = pl.BlockSpec((2, 1, order, order), lambda s: (0, s, 0, 0))
    out_tiles = 2 * tiles + 1
    new_roots, returned = pl.pallas_call(
        functools.partial(owner_kernel, blocks),
        grid=(slots,),
        out_shape=[
            jax.ShapeDtypeStruct((2, slots, order, order), jnp.bfloat16),
            jax.ShapeDtypeStruct((devices, out_tiles, rows, LANES), jnp.bfloat16),
        ],
        in_specs=[
            SMEM,
            SMEM,
            pl.BlockSpec((devices, tiles, rows, LANES), lambda s: (0, s, 0, 0)),
            pl.BlockSpec((devices, tiles, rows, LANES), lambda s: (0, slots + s, 0, 0)),
            side_spec,
            side_spec,
            side_spec,
            pl.BlockSpec((devices, 1, rows, LANES), lambda s: (0, 2 * slots * tiles, 0, 0)),
        ],
        out_specs=[
            side_spec,
            pl.BlockSpec((devices, out_tiles, rows, LANES), lambda s: (0, 0, 0, 0)),
        ],
        compiler_params=PARAMS,
        cost_estimate=cost(10 * slots, order, 24 * slots * order * order),
        name="owner",
    )(
        plan,
        factor,
        arrived,
        arrived,
        seeds,
        high.reshape(2, slots, order, order),
        low.reshape(2, slots, order, order),
        arrived,
    )
    back = exchange(returned)

    new_second, sums = pl.pallas_call(
        functools.partial(adam_kernel, order),
        out_shape=[
            jax.ShapeDtypeStruct(second_moment.shape, jnp.float32),
            jax.ShapeDtypeStruct((8, LANES), jnp.float32),
        ],
        in_specs=[SMEM, VMEM, VMEM, pl.BlockSpec(memory_space=pl.ANY)],
        out_specs=[VMEM, VMEM],
        compiler_params=PARAMS,
        name="adam",
    )(scale.reshape(1), grads, second_moment, returned)
    sums = blk_sum(sums, "blk", 1)

    placed, new_left, new_right = pl.pallas_call(
        finish_kernel,
        out_shape=[
            jax.ShapeDtypeStruct((rows_dev, rows, width), jnp.bfloat16),
            jax.ShapeDtypeStruct(left_old.shape, jnp.float32),
            jax.ShapeDtypeStruct(right_old.shape, jnp.float32),
        ],
        in_specs=[SMEM, SMEM, VMEM, VMEM, VMEM, VMEM],
        out_specs=[VMEM, VMEM, VMEM],
        compiler_params=PARAMS,
        name="finish",
    )(plan, factor, left_old, right_old, back, sums)
    return (placed, new_second, new_left[None], new_right[None], new_roots[None])


def solution(mesh):
    placed = (
        P("zero", "blk", None),
        P("zero", None, None),
        P("zero", None, "blk", None),
        P("zero", None, "blk", None),
        P("zero", "blk", None),
        P("zero", None, "blk", None, None),
    )
    return jax.shard_map(
        local,
        mesh=mesh,
        in_specs=placed,
        out_specs=(
            P("zero", "blk", None),
            P("zero", "blk", None),
            P("zero", None, "blk", None),
            P("zero", None, "blk", None),
            P("zero", None, "blk", None, None),
        ),
        check_vma=False,
    )
```

time: 158 us -> 130 us (0.82)
  waiting for transfers between devices: 89.7 us -> 38.3 us
  starting transfers between devices: 26.7 us -> 55.5 us
  Pallas kernels: 36.5 us -> 28.7 us
  other arithmetic: 0.01 us -> 1.99 us
    all_to_all x3 -> x2, waiting for transfers between devices: 81.5 us -> 0.01 us  [exchange(): lax.all_to_all(values, 'blk', split_axis=0, concat_axis=0, tiled=True)]
    ppermute x0 -> x8, waiting for transfers between devices: none -> 19.7 us  [blk_sum(): parts.append(lax.ppermute(values, ('blk', 'zero'), pairs))]
    ppermute x3 -> x9, starting transfers between devices: 1.81 us -> 19.3 us  [butterfly(): lax.ppermute(values, axis, [(i, i ^ step) for i in range(size)])]
    ppermute x0 -> x8, starting transfers between devices: none -> 14.9 us  [blk_sum(): parts.append(lax.ppermute(values, ('blk', 'zero'), pairs))]
    ppermute x3 -> x9, waiting for transfers between devices: 8.16 us -> 18.5 us  [butterfly(): lax.ppermute(values, axis, [(i, i ^ step) for i in range(size)])]
    pallas_call x5 -> x4, Pallas kernels: 24.1 us -> 16.3 us  [the longest x1 7.61 us: local(): pl.pallas_call(functools.partial(owner_kernel, blocks), grid=(slots,), ou...]
    all_to_all x3 -> x2, starting transfers between devices: 24.9 us -> 21.2 us  [exchange(): lax.all_to_all(values, 'blk', split_axis=0, concat_axis=0, tiled=True)]
    add x3 -> x9, other arithmetic: 0.01 us -> 1.98 us  [butterfly(): values + lax.ppermute(values, axis, [(i, i ^ step) for i in range(size)])]
  transfers between devices with their start and end apart: 6 -> 19, of which waited for: 6 -> 14; matrix products, arithmetic and copies ran while one was open for 0% -> 2% of each run, Pallas kernels for 18% -> 11%
where the time goes in v3:
time: 130 us; the launch traced here: 129 us
  starting transfers between devices  55.5 us (43%)
  waiting for transfers between devices  38.3 us (29%)
  Pallas kernels  28.7 us (22%)
  local copies, waits for them, and re-layouts  2.94 us (2%)
  other arithmetic  1.99 us (2%)
  between operations  1.46 us (1%)
    all_to_all x2, starting transfers between devices, exchange(): lax.all_to_all(values, 'blk', split_axis=0, concat_axis=0, tiled=True)  21.2 us
    ppermute x8, waiting for transfers between devices, blk_sum(): parts.append(lax.ppermute(values, ('blk', 'zero'), pairs))  19.7 us
    ppermute x9, starting transfers between devices, butterfly(): lax.ppermute(values, axis, [(i, i ^ step) for i in range(size)])  19.3 us
    ppermute x9, waiting for transfers between devices, butterfly(): lax.ppermute(values, axis, [(i, i ^ step) for i in range(size)])  18.5 us
    ppermute x8, starting transfers between devices, blk_sum(): parts.append(lax.ppermute(values, ('blk', 'zero'), pairs))  14.9 us
    pallas_call x1, Pallas kernels, local(): pl.pallas_call(fifth_kernel, grid=(2 * slots,), out_shape=[fifth_shape, f...  9.83 us
    pallas_call x1, Pallas kernels, local(): pl.pallas_call(functools.partial(owner_kernel, blocks), grid=(slots,), ou...  7.61 us
    pallas_call x1, Pallas kernels, local(): pl.pallas_call(functools.partial(pack_kernel, slots), out_shape=[jax.Shap...  3.75 us
  transfers between devices with their start and end apart: 19, of which 14 were waited for; matrix products, arithmetic and copies ran while one was open for 2% of the time, Pallas kernels for 11%

profile of v3, /device:TPU:4, one launch (start us, length us, event | category | flops | bytes accessed | tf_op | source)
XLA Modules:
  0.0 128.8 jit_solution(17770642591848926999)
XLA Ops:
  0.6 3.7 %pack.1 = (bf16[32,17,16,128]{3,2,1,0:T(8,128)(2,1)}, s32[172]{0:T(256)}) custom-call(s32[1]{0:T(128)} %bitcast.me_ref, s32[24]{0:T(128)} %bitcast.19, bf16[2,16,6144]{2,1,0:T(8,128)(2,1)} %grads_ref.5, f32[24,16,512]{2,1,0:T(8,128)} %bitcast.14, f32[24,16,512]{2,1,0:T(8,128)} %bitcast.16), custom_call_target="tpu_custom_call" | custom-call | tf_op jit(solution)/shard_map/pack/pallas_call | solution.py:386
  4.4 11.5 %all-to-all-start = ((bf16[32,17,16,128]{3,2,1,0:T(8,128)(2,1)}), bf16[32,17,16,128]{3,2,1,0:T(8,128)(2,1)S(1)}, u32[]{:S(2)}, u32[]{:S(2)}) async-start(bf16[32,17,16,128]{3,2,1,0:T(8,128)(2,1)} %get-tuple-element.18.__), calls=%async_computation | async-start | bytes 4456448 | tf_op jit(solution)/shard_map/all_to_all | solution.py:365
  15.9 9.8 %fifth.1 = (bf16[4,512,512]{2,1,0:T(8,128)(2,1)}, bf16[4,512,512]{2,1,0:T(8,128)(2,1)}) custom-call(bf16[4,512,512]{2,1,0:T(8,128)(2,1)} %bitcast.20), custom_call_target="tpu_custom_call" | custom-call | flops 6442450944 | bytes 6291456 | tf_op jit(solution)/shard_map/fifth/pallas_call | solution.py:402
  25.7 1.7 %square.1 = f32[8,128]{1,0:T(8,128)} custom-call(bf16[2,16,6144]{2,1,0:T(8,128)(2,1)} %grads_ref.5, bf16[4,512,512]{2,1,0:T(8,128)(2,1)} %get-tuple-element.17._, bf16[32,17,16,128]{3,2,1,0:T(8,128)(2,1)} %get-tuple-element.18.__), custom_call_target="tpu_custom_call" | custom-call | tf_op jit(solution)/shard_map/square/pallas_call | solution.py:412
  27.5 0.0 collective-permute-start
  27.5 1.4 %collective-permute-done = f32[8,128]{1,0:T(8,128)S(1)} collective-permute-done((f32[8,128]{1,0:T(8,128)}, f32[8,128]{1,0:T(8,128)S(1)}, u32[]{:S(2)}, u32[]{:S(2)}) %collective-permute-start) | collective-permute-done | bytes 4128 | tf_op jit(solution)/shard_map/ppermute | solution.py:344
  28.8 0.7 add.49
  29.5 1.2 collective-permute-start.1
  30.7 2.4 %collective-permute-done.1 = f32[8,128]{1,0:T(8,128)S(1)} collective-permute-done((f32[8,128]{1,0:T(8,128)S(1)}, f32[8,128]{1,0:T(8,128)S(1)}, u32[]{:S(2)}, u32[]{:S(2)}) %collective-permute-start.1) | collective-permute-done | bytes 4128 | tf_op jit(solution)/shard_map/ppermute | solution.py:344
  33.1 0.5 collective-permute-start.2
  33.6 4.6 %collective-permute-done.2 = f32[8,128]{1,0:T(8,128)S(1)} collective-permute-done((f32[8,128]{1,0:T(8,128)S(1)}, f32[8,128]{1,0:T(8,128)S(1)}, u32[]{:S(2)}, u32[]{:S(2)}) %collective-permute-start.2) | collective-permute-done | bytes 4128 | tf_op jit(solution)/shard_map/ppermute | solution.py:344
  38.3 1.8 %collective-permute-start.3 = (f32[8,128]{1,0:T(8,128)S(1)}, f32[8,128]{1,0:T(8,128)S(1)}, u32[]{:S(2)}, u32[]{:S(2)}) collective-permute-start(f32[8,128]{1,0:T(8,128)S(1)} %add.51), channel_id=1, source_target_pairs={{0,8},{8,0},{16,24},{24,16},{32,40},{40,32},{48,56},{56,48},{64,72... | collective-permute-start | bytes 12296 | tf_op jit(solution)/shard_map/ppermute | solution.py:344
  40.0 1.8 %collective-permute-done.3 = f32[8,128]{1,0:T(8,128)S(1)} collective-permute-done((f32[8,128]{1,0:T(8,128)S(1)}, f32[8,128]{1,0:T(8,128)S(1)}, u32[]{:S(2)}, u32[]{:S(2)}) %collective-permute-start.3) | collective-permute-done | bytes 4128 | tf_op jit(solution)/shard_map/ppermute | solution.py:344
  41.9 3.3 %collective-permute-start.4 = (f32[8,128]{1,0:T(8,128)S(1)}, f32[8,128]{1,0:T(8,128)S(1)}, u32[]{:S(2)}, u32[]{:S(2)}) collective-permute-start(f32[8,128]{1,0:T(8,128)S(1)} %add.52), channel_id=1, source_target_pairs={{0,16},{8,24},{16,0},{24,8},{32,48},{40,56},{48,32},{56,40},{64,80... | collective-permute-start | bytes 12296 | tf_op jit(solution)/shard_map/ppermute | solution.py:344
  45.2 1.8 %collective-permute-done.4 = f32[8,128]{1,0:T(8,128)S(1)} collective-permute-done((f32[8,128]{1,0:T(8,128)S(1)}, f32[8,128]{1,0:T(8,128)S(1)}, u32[]{:S(2)}, u32[]{:S(2)}) %collective-permute-start.4) | collective-permute-done | bytes 4128 | tf_op jit(solution)/shard_map/ppermute | solution.py:344
  47.0 4.8 %collective-permute-start.8 = (f32[8,128]{1,0:T(8,128)S(1)}, f32[8,128]{1,0:T(8,128)S(1)}, u32[]{:S(2)}, u32[]{:S(2)}) collective-permute-start(f32[8,128]{1,0:T(8,128)S(1)} %add.53), channel_id=1, source_target_pairs={{96,0},{225,1},{98,2},{227,3},{100,4},{229,5},{102,6},{231,7},{104... | collective-permute-start | bytes 12296 | tf_op jit(solution)/shard_map/ppermute | solution.py:360
  51.8 1.5 %collective-permute-start.7 = (f32[8,128]{1,0:T(8,128)S(1)}, f32[8,128]{1,0:T(8,128)S(1)}, u32[]{:S(2)}, u32[]{:S(2)}) collective-permute-start(f32[8,128]{1,0:T(8,128)S(1)} %add.53), channel_id=1, source_target_pairs={{64,0},{193,1},{66,2},{195,3},{68,4},{197,5},{70,6},{199,7},{72,8}... | collective-permute-start | bytes 12296 | tf_op jit(solution)/shard_map/ppermute | solution.py:360
  53.4 0.8 collective-permute-start.6
  54.2 0.6 collective-permute-start.5
  54.9 11.0 %collective-permute-done.8 = f32[8,128]{1,0:T(8,128)S(1)} collective-permute-done((f32[8,128]{1,0:T(8,128)S(1)}, f32[8,128]{1,0:T(8,128)S(1)}, u32[]{:S(2)}, u32[]{:S(2)}) %collective-permute-start.8) | collective-permute-done | bytes 4128 | tf_op jit(solution)/shard_map/ppermute | solution.py:360
  65.8 0.0 collective-permute-done.7
  65.8 0.2 collective-permute-done.6
  66.0 0.0 collective-permute-done.5
  66.0 1.7 %collective-permute-start.9 = (f32[8,128]{1,0:T(8,128)S(1)}, f32[8,128]{1,0:T(8,128)S(1)}, u32[]{:S(2)}, u32[]{:S(2)}) collective-permute-start(f32[8,128]{1,0:T(8,128)S(1)} %add_add_fusion.1), channel_id=1, source_target_pairs={{0,1},{1,0},{2,3},{3,2},{4,5},{5,4},{6,7},{7,6},{8,9},{9,8},{10,11... | collective-permute-start | bytes 12296 | tf_op jit(solution)/shard_map/ppermute | solution.py:344
  67.8 0.8 collective-permute-done.9
  68.6 0.5 slice.3
  69.8 0.0 all-to-all-done.block_ref.mixed_ref.extra_ref
  69.9 1.4 %copy-done.1 = bf16[32,17,16,128]{3,2,1,0:T(8,128)(2,1)} copy-done((bf16[32,17,16,128]{3,2,1,0:T(8,128)(2,1)}, bf16[32,17,16,128]{3,2,1,0:T(8,128)(2,1)S(1)}, u32[]{:S(2)}) %copy-start.1) | copy-done | bytes 2228248
  71.2 7.6 %owner.1 = (bf16[2,2,512,512]{3,2,1,0:T(8,128)(2,1)}, bf16[32,9,16,128]{3,2,1,0:T(8,128)(2,1)}) custom-call(s32[172]{0:T(256)} %get-tuple-element.16.plan_ref, f32[1]{0:T(128)} %bitcast.6.factor_ref, bf16[32,17,16,128]{3,2,1,0:T(8,128)(2,1)} %copy-done.1, bf16[32,17,16,128]{3,2,1,0:T(8,128)(2,1)} %copy-done.1, bf16[2,2,512,512]{3,2,1,0:T(8,128)(2,1)} %bitcast.21, ...), custom_call_target="tpu_custom_call" | custom-call | flops 5368709120 | bytes 12582912 | tf_op jit(solution)/shard_map/owner/pallas_call | solution.py:427
  78.8 9.8 %all-to-all-start.1 = ((bf16[32,9,16,128]{3,2,1,0:T(8,128)(2,1)}), bf16[32,9,16,128]{3,2,1,0:T(8,128)(2,1)S(1)}, u32[]{:S(2)}, u32[]{:S(2)}) async-start(bf16[32,9,16,128]{3,2,1,0:T(8,128)(2,1)} %get-tuple-element.20._), calls=%async_computation.1 | async-start | bytes 2359296 | tf_op jit(solution)/shard_map/all_to_all | solution.py:365
  88.6 2.6 %adam.1 = (f32[2,16,6144]{2,1,0:T(8,128)}, f32[8,128]{1,0:T(8,128)}) custom-call(f32[1]{0:T(128)} %bitcast.10.scale_ref, bf16[2,16,6144]{2,1,0:T(8,128)(2,1)} %grads_ref.5, f32[2,16,6144]{2,1,0:T(8,128)} %second_ref.1, bf16[32,9,16,128]{3,2,1,0:T(8,128)(2,1)} %get-tuple-element.20._), custom_call_target="tpu_custom_call" | custom-call | tf_op jit(solution)/shard_map/adam/pallas_call | solution.py:463
  91.2 1.8 %collective-permute-start.10 = (f32[8,128]{1,0:T(8,128)}, f32[8,128]{1,0:T(8,128)S(1)}, u32[]{:S(2)}, u32[]{:S(2)}) collective-permute-start(f32[8,128]{1,0:T(8,128)} %get-tuple-element.21), channel_id=1, source_target_pairs={{0,8},{8,0},{16,24},{24,16},{32,40},{40,32},{48,56},{56,48},{64,72... | collective-permute-start | bytes 12296 | tf_op jit(solution)/shard_map/ppermute | solution.py:344
  93.0 2.1 %collective-permute-done.10 = f32[8,128]{1,0:T(8,128)S(1)} collective-permute-done((f32[8,128]{1,0:T(8,128)}, f32[8,128]{1,0:T(8,128)S(1)}, u32[]{:S(2)}, u32[]{:S(2)}) %collective-permute-start.10) | collective-permute-done | bytes 4128 | tf_op jit(solution)/shard_map/ppermute | solution.py:344
  95.1 0.7 add.59
  95.8 3.5 %collective-permute-start.11 = (f32[8,128]{1,0:T(8,128)S(1)}, f32[8,128]{1,0:T(8,128)S(1)}, u32[]{:S(2)}, u32[]{:S(2)}) collective-permute-start(f32[8,128]{1,0:T(8,128)S(1)} %add.59), channel_id=1, source_target_pairs={{0,16},{8,24},{16,0},{24,8},{32,48},{40,56},{48,32},{56,40},{64,80... | collective-permute-start | bytes 12296 | tf_op jit(solution)/shard_map/ppermute | solution.py:344
  99.3 1.9 %collective-permute-done.11 = f32[8,128]{1,0:T(8,128)S(1)} collective-permute-done((f32[8,128]{1,0:T(8,128)S(1)}, f32[8,128]{1,0:T(8,128)S(1)}, u32[]{:S(2)}, u32[]{:S(2)}) %collective-permute-start.11) | collective-permute-done | bytes 4128 | tf_op jit(solution)/shard_map/ppermute | solution.py:344
  101.3 5.8 %collective-permute-start.15 = (f32[8,128]{1,0:T(8,128)S(1)}, f32[8,128]{1,0:T(8,128)S(1)}, u32[]{:S(2)}, u32[]{:S(2)}) collective-permute-start(f32[8,128]{1,0:T(8,128)S(1)} %add.60), channel_id=1, source_target_pairs={{96,0},{97,1},{98,2},{99,3},{100,4},{101,5},{102,6},{103,7},{232,8... | collective-permute-start | bytes 12296 | tf_op jit(solution)/shard_map/ppermute | solution.py:360
  107.1 0.2 collective-permute-start.14
  107.3 0.4 collective-permute-start.13
  107.7 0.6 collective-permute-start.12
  108.3 7.4 %collective-permute-done.15 = f32[8,128]{1,0:T(8,128)S(1)} collective-permute-done((f32[8,128]{1,0:T(8,128)S(1)}, f32[8,128]{1,0:T(8,128)S(1)}, u32[]{:S(2)}, u32[]{:S(2)}) %collective-permute-start.15) | collective-permute-done | bytes 4128 | tf_op jit(solution)/shard_map/ppermute | solution.py:360
  115.8 0.6 collective-permute-done.14
  116.4 0.6 collective-permute-done.13
  116.9 5.4 %collective-permute-start.16 = (f32[8,128]{1,0:T(8,128)S(1)}, f32[8,128]{1,0:T(8,128)S(1)}, u32[]{:S(2)}, u32[]{:S(2)}) collective-permute-start(f32[8,128]{1,0:T(8,128)S(1)} %add_add_fusion), channel_id=1, source_target_pairs={{0,8},{8,0},{16,24},{24,16},{32,40},{40,32},{48,56},{56,48},{64,72... | collective-permute-start | bytes 12296 | tf_op jit(solution)/shard_map/ppermute | solution.py:344
  122.4 1.6 %collective-permute-done.16 = f32[8,128]{1,0:T(8,128)S(1)} collective-permute-done((f32[8,128]{1,0:T(8,128)S(1)}, f32[8,128]{1,0:T(8,128)S(1)}, u32[]{:S(2)}, u32[]{:S(2)}) %collective-permute-start.16) | collective-permute-done | bytes 4128 | tf_op jit(solution)/shard_map/ppermute | solution.py:344
  124.0 0.6 add.64.sums_ref
  124.6 1.0 copy-done
  125.6 3.2 %finish.1 = (bf16[2,16,6144]{2,1,0:T(8,128)(2,1)}, f32[24,16,512]{2,1,0:T(8,128)}, f32[24,16,512]{2,1,0:T(8,128)}) custom-call(s32[172]{0:T(256)} %get-tuple-element.16.plan_ref, f32[1]{0:T(128)} %bitcast.6.factor_ref, f32[24,16,512]{2,1,0:T(8,128)} %bitcast.15, f32[24,16,512]{2,1,0:T(8,128)} %bitcast.17, bf16[32,9,16,128]{3,2,1,0:T(8,128)(2,1)} %copy-done, ...), custom_call_target="tpu_custom_call" | custom-call | tf_op jit(solution)/shard_map/finish/pallas_call | solution.py:476
  (12 shorter events, 0.0 us)
Async XLA Ops:
  4.4 65.4 %all-to-all-start = ((bf16[32,17,16,128]{3,2,1,0:T(8,128)(2,1)}), bf16[32,17,16,128]{3,2,1,0:T(8,128)(2,1)S(1)}, u32[]{:S(2)}, u32[]{:S(2)}) async-start(bf16[32,17,16,128]{3,2,1,0:T(8,128)(2,1)} %get-tuple-element.18.__), calls=%async_computation | async-start | bytes 4456448 | tf_op jit(solution)/shard_map/all_to_all | solution.py:365
  27.5 1.4 %collective-permute-start = (f32[8,128]{1,0:T(8,128)}, f32[8,128]{1,0:T(8,128)S(1)}, u32[]{:S(2)}, u32[]{:S(2)}) collective-permute-start(f32[8,128]{1,0:T(8,128)} %square.1), channel_id=1, source_target_pairs={{0,1},{1,0},{2,3},{3,2},{4,5},{5,4},{6,7},{7,6},{8,9},{9,8},{10,11... | collective-permute-start | bytes 12296 | tf_op jit(solution)/shard_map/ppermute | solution.py:344
  29.5 3.6 %collective-permute-start.1 = (f32[8,128]{1,0:T(8,128)S(1)}, f32[8,128]{1,0:T(8,128)S(1)}, u32[]{:S(2)}, u32[]{:S(2)}) collective-permute-start(f32[8,128]{1,0:T(8,128)S(1)} %add.49), channel_id=1, source_target_pairs={{0,2},{1,3},{2,0},{3,1},{4,6},{5,7},{6,4},{7,5},{8,10},{9,11},{10,... | collective-permute-start | bytes 12296 | tf_op jit(solution)/shard_map/ppermute | solution.py:344
  33.1 5.1 %collective-permute-start.2 = (f32[8,128]{1,0:T(8,128)S(1)}, f32[8,128]{1,0:T(8,128)S(1)}, u32[]{:S(2)}, u32[]{:S(2)}) collective-permute-start(f32[8,128]{1,0:T(8,128)S(1)} %add.50), channel_id=1, source_target_pairs={{0,4},{1,5},{2,6},{3,7},{4,0},{5,1},{6,2},{7,3},{8,12},{9,13},{10,... | collective-permute-start | bytes 12296 | tf_op jit(solution)/shard_map/ppermute | solution.py:344
  38.3 3.6 %collective-permute-start.3 = (f32[8,128]{1,0:T(8,128)S(1)}, f32[8,128]{1,0:T(8,128)S(1)}, u32[]{:S(2)}, u32[]{:S(2)}) collective-permute-start(f32[8,128]{1,0:T(8,128)S(1)} %add.51), channel_id=1, source_target_pairs={{0,8},{8,0},{16,24},{24,16},{32,40},{40,32},{48,56},{56,48},{64,72... | collective-permute-start | bytes 12296 | tf_op jit(solution)/shard_map/ppermute | solution.py:344
  41.9 5.1 %collective-permute-start.4 = (f32[8,128]{1,0:T(8,128)S(1)}, f32[8,128]{1,0:T(8,128)S(1)}, u32[]{:S(2)}, u32[]{:S(2)}) collective-permute-start(f32[8,128]{1,0:T(8,128)S(1)} %add.52), channel_id=1, source_target_pairs={{0,16},{8,24},{16,0},{24,8},{32,48},{40,56},{48,32},{56,40},{64,80... | collective-permute-start | bytes 12296 | tf_op jit(solution)/shard_map/ppermute | solution.py:344
  47.0 18.8 %collective-permute-start.8 = (f32[8,128]{1,0:T(8,128)S(1)}, f32[8,128]{1,0:T(8,128)S(1)}, u32[]{:S(2)}, u32[]{:S(2)}) collective-permute-start(f32[8,128]{1,0:T(8,128)S(1)} %add.53), channel_id=1, source_target_pairs={{96,0},{225,1},{98,2},{227,3},{100,4},{229,5},{102,6},{231,7},{104... | collective-permute-start | bytes 12296 | tf_op jit(solution)/shard_map/ppermute | solution.py:360
  51.8 14.0 %collective-permute-start.7 = (f32[8,128]{1,0:T(8,128)S(1)}, f32[8,128]{1,0:T(8,128)S(1)}, u32[]{:S(2)}, u32[]{:S(2)}) collective-permute-start(f32[8,128]{1,0:T(8,128)S(1)} %add.53), channel_id=1, source_target_pairs={{64,0},{193,1},{66,2},{195,3},{68,4},{197,5},{70,6},{199,7},{72,8}... | collective-permute-start | bytes 12296 | tf_op jit(solution)/shard_map/ppermute | solution.py:360
  53.4 12.6 %collective-permute-start.6 = (f32[8,128]{1,0:T(8,128)S(1)}, f32[8,128]{1,0:T(8,128)S(1)}, u32[]{:S(2)}, u32[]{:S(2)}) collective-permute-start(f32[8,128]{1,0:T(8,128)S(1)} %add.53), channel_id=1, source_target_pairs={{32,0},{161,1},{34,2},{163,3},{36,4},{165,5},{38,6},{167,7},{40,8}... | collective-permute-start | bytes 12296 | tf_op jit(solution)/shard_map/ppermute | solution.py:360
  54.2 11.8 %collective-permute-start.5 = (f32[8,128]{1,0:T(8,128)S(1)}, f32[8,128]{1,0:T(8,128)S(1)}, u32[]{:S(2)}, u32[]{:S(2)}) collective-permute-start(f32[8,128]{1,0:T(8,128)S(1)} %add.53), channel_id=1, source_target_pairs={{0,0},{129,1},{2,2},{131,3},{4,4},{133,5},{6,6},{135,7},{8,8},{137... | collective-permute-start | bytes 12296 | tf_op jit(solution)/shard_map/ppermute | solution.py:360
  66.0 2.6 %collective-permute-start.9 = (f32[8,128]{1,0:T(8,128)S(1)}, f32[8,128]{1,0:T(8,128)S(1)}, u32[]{:S(2)}, u32[]{:S(2)}) collective-permute-start(f32[8,128]{1,0:T(8,128)S(1)} %add_add_fusion.1), channel_id=1, source_target_pairs={{0,1},{1,0},{2,3},{3,2},{4,5},{5,4},{6,7},{7,6},{8,9},{9,8},{10,11... | collective-permute-start | bytes 12296 | tf_op jit(solution)/shard_map/ppermute | solution.py:344
  69.8 1.4 %copy-start.1 = (bf16[32,17,16,128]{3,2,1,0:T(8,128)(2,1)}, bf16[32,17,16,128]{3,2,1,0:T(8,128)(2,1)S(1)}, u32[]{:S(2)}) copy-start(bf16[32,17,16,128]{3,2,1,0:T(8,128)(2,1)S(1)} %all-to-all-done.block_ref.mixed_ref.extra_ref) | copy-start | bytes 6684676
  78.8 45.7 %all-to-all-start.1 = ((bf16[32,9,16,128]{3,2,1,0:T(8,128)(2,1)}), bf16[32,9,16,128]{3,2,1,0:T(8,128)(2,1)S(1)}, u32[]{:S(2)}, u32[]{:S(2)}) async-start(bf16[32,9,16,128]{3,2,1,0:T(8,128)(2,1)} %get-tuple-element.20._), calls=%async_computation.1 | async-start | bytes 2359296 | tf_op jit(solution)/shard_map/all_to_all | solution.py:365
  91.2 3.9 %collective-permute-start.10 = (f32[8,128]{1,0:T(8,128)}, f32[8,128]{1,0:T(8,128)S(1)}, u32[]{:S(2)}, u32[]{:S(2)}) collective-permute-start(f32[8,128]{1,0:T(8,128)} %get-tuple-element.21), channel_id=1, source_target_pairs={{0,8},{8,0},{16,24},{24,16},{32,40},{40,32},{48,56},{56,48},{64,72... | collective-permute-start | bytes 12296 | tf_op jit(solution)/shard_map/ppermute | solution.py:344
  95.8 5.5 %collective-permute-start.11 = (f32[8,128]{1,0:T(8,128)S(1)}, f32[8,128]{1,0:T(8,128)S(1)}, u32[]{:S(2)}, u32[]{:S(2)}) collective-permute-start(f32[8,128]{1,0:T(8,128)S(1)} %add.59), channel_id=1, source_target_pairs={{0,16},{8,24},{16,0},{24,8},{32,48},{40,56},{48,32},{56,40},{64,80... | collective-permute-start | bytes 12296 | tf_op jit(solution)/shard_map/ppermute | solution.py:344
  101.3 14.5 %collective-permute-start.15 = (f32[8,128]{1,0:T(8,128)S(1)}, f32[8,128]{1,0:T(8,128)S(1)}, u32[]{:S(2)}, u32[]{:S(2)}) collective-permute-start(f32[8,128]{1,0:T(8,128)S(1)} %add.60), channel_id=1, source_target_pairs={{96,0},{97,1},{98,2},{99,3},{100,4},{101,5},{102,6},{103,7},{232,8... | collective-permute-start | bytes 12296 | tf_op jit(solution)/shard_map/ppermute | solution.py:360
  107.1 9.2 %collective-permute-start.14 = (f32[8,128]{1,0:T(8,128)S(1)}, f32[8,128]{1,0:T(8,128)S(1)}, u32[]{:S(2)}, u32[]{:S(2)}) collective-permute-start(f32[8,128]{1,0:T(8,128)S(1)} %add.60), channel_id=1, source_target_pairs={{64,0},{65,1},{66,2},{67,3},{68,4},{69,5},{70,6},{71,7},{200,8},{2... | collective-permute-start | bytes 12296 | tf_op jit(solution)/shard_map/ppermute | solution.py:360
  107.3 9.6 %collective-permute-start.13 = (f32[8,128]{1,0:T(8,128)S(1)}, f32[8,128]{1,0:T(8,128)S(1)}, u32[]{:S(2)}, u32[]{:S(2)}) collective-permute-start(f32[8,128]{1,0:T(8,128)S(1)} %add.60), channel_id=1, source_target_pairs={{32,0},{33,1},{34,2},{35,3},{36,4},{37,5},{38,6},{39,7},{168,8},{1... | collective-permute-start | bytes 12296 | tf_op jit(solution)/shard_map/ppermute | solution.py:360
  107.7 9.3 %collective-permute-start.12 = (f32[8,128]{1,0:T(8,128)S(1)}, f32[8,128]{1,0:T(8,128)S(1)}, u32[]{:S(2)}, u32[]{:S(2)}) collective-permute-start(f32[8,128]{1,0:T(8,128)S(1)} %add.60), channel_id=1, source_target_pairs={{0,0},{1,1},{2,2},{3,3},{4,4},{5,5},{6,6},{7,7},{136,8},{137,9},{1... | collective-permute-start | bytes 12296 | tf_op jit(solution)/shard_map/ppermute | solution.py:360
  116.9 7.0 %collective-permute-start.16 = (f32[8,128]{1,0:T(8,128)S(1)}, f32[8,128]{1,0:T(8,128)S(1)}, u32[]{:S(2)}, u32[]{:S(2)}) collective-permute-start(f32[8,128]{1,0:T(8,128)S(1)} %add_add_fusion), channel_id=1, source_target_pairs={{0,8},{8,0},{16,24},{24,16},{32,40},{40,32},{48,56},{56,48},{64,72... | collective-permute-start | bytes 12296 | tf_op jit(solution)/shard_map/ppermute | solution.py:344
  124.6 1.0 copy-start

commit v4 on v3

--- a/solution.py
+++ b/solution.py
@@ -9,10 +9,13 @@
 from jax.sharding import PartitionSpec as P
 
 BETA = 0.95
-VMEM_LIMIT = 56 * 1024 * 1024
 VMEM = pl.BlockSpec(memory_space=pltpu.VMEM)
 SMEM = pl.BlockSpec(memory_space=pltpu.SMEM)
-PARAMS = pltpu.CompilerParams(vmem_limit_bytes=VMEM_LIMIT)
+ANY = pl.BlockSpec(memory_space=pl.ANY)
+
+
+def grant(mebibytes):
+    return pltpu.CompilerParams(vmem_limit_bytes=mebibytes * 1024 * 1024)
 
 
 def dot(former, latter):
@@ -25,6 +28,13 @@
 
 
 LANES = 128
+HBM = pl.BlockSpec(memory_space=pltpu.HBM)
+
+
+def thirds(wide):
+    first = wide.astype(jnp.bfloat16).astype(jnp.float32)
+    second = (wide - first).astype(jnp.bfloat16).astype(jnp.float32)
+    return first, second, wide - first - second
 
 
 def sublanes(shape):
@@ -40,11 +50,16 @@
         ref[place, first + tile] = piece[:, tile * LANES : (tile + 1) * LANES]
 
 
-def whole_block(ref):
-    devices, tiles, rows, _ = ref.shape
+def whole_block(ref, first, tiles):
+    devices, _, rows, _ = ref.shape
     return jnp.concatenate(
-        [ref[:, tile].reshape(devices * rows, LANES) for tile in range(tiles)], axis=1
+        [ref[:, first + tile].reshape(devices * rows, LANES) for tile in range(tiles)], axis=1
     )
+
+
+def scale_of(entries, half_ref, other_ref):
+    total = half_ref[:1, :1] + other_ref[:1, :1]
+    return jnp.minimum(1.0, math.sqrt(entries) / (jnp.sqrt(total) + 1e-06))
 
 
 OWNER, HELPER, SPARE = 0, 1, 2
@@ -162,19 +177,23 @@
     out_ref[...] = jnp.broadcast_to(jnp.sum(total, keepdims=True), out_ref.shape)
 
 
-def fifth_kernel(seed_ref, high_ref, low_ref):
-    seed = seed_ref[0]
-    high, low = split(dot(seed, seed))
-    high, low = split(dot(high, high) + (dot(high, low) + dot(low, high)))
-    high, low = split(dot(seed, high) + dot(seed, low))
-    high_ref[0] = high
-    low_ref[0] = low
-
-
-def adam_kernel(order, scale_ref, grads_ref, second_ref, _, new_ref, sums_ref):
+def fifth_kernel(seed_ref, out_ref):
+    order = seed_ref.shape[-1]
+    for place in range(seed_ref.shape[0]):
+        seed = seed_ref[place]
+        high, low = split(dot(seed, seed))
+        high, low = split(dot(high, high) + (dot(high, low) + dot(low, high)))
+        high, low = split(-0.25 * (dot(seed, high) + dot(seed, low)))
+        out_ref[place, :, :order] = high
+        out_ref[place, :, order:] = low
+
+
+def adam_kernel(
+    order, entries, half_ref, other_ref, grads_ref, second_ref, new_ref, tile_ref
+):
     rows_dev, rows, width = grads_ref.shape
     cols = width // order
-    scale = scale_ref[0]
+    scale = scale_of(entries, half_ref, other_ref)
     sums = jnp.zeros((1, LANES), jnp.float32)
     lane = lanes((1, LANES))
     for k in range(rows_dev * cols):
@@ -184,36 +203,81 @@
         new_ref[where] = second
         step = clipped / (jnp.sqrt(second) + 1e-08)
         sums = jnp.where(lane == k, jnp.sum(step * step, keepdims=True), sums)
-    sums_ref[...] = jnp.broadcast_to(sums, sums_ref.shape)
+    tile_row = sublanes(tile_ref.shape)
+    tile = jnp.zeros(tile_ref.shape, jnp.float32)
+    for place, term in enumerate(thirds(sums)):
+        tile = jnp.where(tile_row == place, term, tile)
+    tile_ref[...] = tile.astype(jnp.bfloat16)
 
 
 def owner_kernel(
     blocks,
+    slots,
+    entries,
     plan_ref,
-    factor_ref,
-    block_ref,
-    mixed_ref,
+    half_ref,
+    other_ref,
+    adam_ref,
+    arrived_hbm,
+    seed_hbm,
+    fifth_hbm,
+    roots_hbm,
+    out_hbm,
+    arrived_ref,
     seed_ref,
-    high_ref,
-    low_ref,
-    extra_ref,
+    fifth_ref,
     roots_ref,
     out_ref,
+    in_sems,
+    out_sems,
 ):
-    slot = pl.program_id(0)
-    devices, tiles, rows, lane_count = block_ref.shape
-    order = tiles * lane_count
+    devices, arrived_tiles, rows, lane_count = arrived_ref.shape
+    order = seed_ref.shape[-1]
+    tiles = order // lane_count
     plan = Plan(plan_ref, blocks, devices)
     role, load = plan.get("role"), plan.get("own")
-    live = slot < load
-    factor = factor_ref[0]
+
+    sources = []
+    for slot in range(slots):
+        sources.append((arrived_hbm, arrived_ref, (slice(None), pl.ds(slot * tiles, tiles))))
+    mixed_at = (slice(None), pl.ds(slots * tiles, arrived_tiles - slots * tiles))
+    sources.append((arrived_hbm, arrived_ref, mixed_at))
+    for slot in range(slots):
+        sources.append((fifth_hbm, fifth_ref, (slice(None), slot)))
+        sources.append((seed_hbm, seed_ref, (slice(None), slot)))
+    copies = [
+        pltpu.make_async_copy(source.at[where], target.at[where], in_sems.at[place])
+        for place, (source, target, where) in enumerate(sources)
+    ]
+    gradient_in, mixed_in, root_in = copies[:slots], copies[slots], copies[slots + 1 :]
+    for copy in (gradient_in[0], mixed_in, *root_in[:2], *gradient_in[1:], *root_in[2:]):
+        copy.start()
+    shares = [
+        (slice(None), pl.ds(0, tiles)),
+        (slice(None), pl.ds(tiles, out_ref.shape[1] - tiles)),
+    ]
+    outs = [
+        pltpu.make_async_copy(out_ref.at[where], out_hbm.at[where], out_sems.at[place])
+        for place, where in enumerate(shares)
+    ] + [
+        pltpu.make_async_copy(
+            roots_ref.at[:, slot], roots_hbm.at[:, slot], out_sems.at[len(shares) + slot]
+        )
+        for slot in range(slots)
+    ]
+    out_ref[:, out_ref.shape[1] - 1] = jnp.broadcast_to(
+        adam_ref[...][None], (devices, rows, lane_count)
+    )
 
     def put(first, value):
         value = value.astype(jnp.bfloat16)
         for tile in range(value.shape[1] // lane_count):
-            out_ref[:, pl.ds(first + tile, 1)] = value[
+            out_ref[:, first + tile] = value[
                 :, tile * lane_count : (tile + 1) * lane_count
-            ].reshape(devices, 1, rows, lane_count)
+            ].reshape(devices, rows, lane_count)
+
+    def gradient(slot):
+        return whole_block(arrived_ref, slot * tiles, tiles)
 
     def right_gram(block):
         return lax.dot_general(
@@ -228,79 +292,110 @@
             preferred_element_type=jnp.float32,
         )
 
-    @pl.when(live)
-    def _():
-        block = whole_block(block_ref)
-        mixed = whole_block(mixed_ref).astype(jnp.float32)
-        turned = mixed.T
+    def old_stats(slot):
+        mixed = whole_block(arrived_ref, (slots + slot) * tiles, tiles)
+        turned = mixed.T.astype(jnp.float32)
+        mixed = mixed.astype(jnp.float32)
         row, col = sublanes((order, order)), lanes((order, order))
         diagonal = []
         tile_row = sublanes((rows, lane_count))
         for tile in range(tiles):
             total = jnp.zeros((rows, lane_count), jnp.float32)
             for source in range(tile * devices // tiles, (tile + 1) * devices // tiles):
-                total = total + extra_ref[source, 0].astype(jnp.float32)
+                total = total + arrived_ref[source, arrived_tiles - 1].astype(jnp.float32)
             diagonal.append(
                 jnp.sum(jnp.where(tile_row == slot, total, 0.0), axis=0, keepdims=True)
             )
         diagonal = jnp.concatenate(diagonal, axis=1)
         left_old = jnp.where(col <= row, mixed, turned)
         right_old = jnp.where(col > row, mixed, jnp.where(col == row, diagonal, turned))
-        left, right = left_part(block, 0, order), right_gram(block)
-
-        def new_root(side, old, gram):
+        return left_old, right_old
+
+    def work(slot):
+        factor = scale_of(entries, half_ref, other_ref)
+        factor = 0.05 * factor * factor
+        gradient_in[slot].wait()
+        block = gradient(slot)
+        grams = left_part(block, 0, order), right_gram(block)
+        if slot == 0:
+            mixed_in.wait()
+        olds = old_stats(slot)
+        for copy in root_in[2 * slot : 2 * slot + 2]:
+            copy.wait()
+        new_pair = []
+        for side, (old, gram) in enumerate(zip(olds, grams)):
             high, low = split(BETA * old + factor * gram)
-            fifth_high, fifth_low = high_ref[side, 0], low_ref[side, 0]
-            moved = dot(fifth_high, high) + (dot(fifth_high, low) + dot(fifth_low, high))
-            seed = seed_ref[side, 0]
-            root = (1.25 * seed.astype(jnp.float32) - 0.25 * moved).astype(jnp.bfloat16)
-            roots_ref[side, 0] = root
-            return root
-
-        left_root = new_root(0, left_old, left)
-        right_root = new_root(1, right_old, right)
-        applied = dot(left_root, block).astype(jnp.bfloat16)
-        direction = dot(applied, right_root).astype(jnp.bfloat16).astype(jnp.float32)
+            moved = dot(fifth_ref[side, slot], jnp.concatenate([high, high]))
+            moved = moved + dot(fifth_ref[side, slot, :, :order], low)
+            root = 1.25 * seed_ref[side, slot].astype(jnp.float32) + moved
+            new_pair.append(root.astype(jnp.bfloat16))
+            roots_ref[side, slot] = new_pair[-1]
+        outs[len(shares) + slot].start()
+        applied = dot(new_pair[0], block).astype(jnp.bfloat16)
+        direction = dot(applied, new_pair[1]).astype(jnp.bfloat16).astype(jnp.float32)
         norm = jnp.sqrt(jnp.sum(direction * direction, keepdims=True)) + 1e-06
-        put(slot * tiles, direction / norm)
-
-        @pl.when(slot == 0)
+        put(slot * tiles, direction * (1.0 / norm))
+        return grams
+
+    def keep(slot):
+        for copy in root_in[2 * slot : 2 * slot + 2]:
+            copy.wait()
+        for side in range(2):
+            roots_ref[side, slot] = seed_ref[side, slot]
+        outs[len(shares) + slot].start()
+
+    @pl.when(load == 2)
+    def _():
+        left, _ = work(0)
+        put(2 * tiles, left[:, :lane_count])
+        outs[0].start()
+        work(1)
+        outs[1].start()
+
+    @pl.when(load == 1)
+    def _():
+        left, right = work(0)
+        outs[0].start()
+        put(tiles, right)
+        put(2 * tiles, left[:, :lane_count])
+        outs[1].start()
+        gradient_in[1].wait()
+        keep(1)
+
+    @pl.when(load == 0)
+    def _():
+        gradient_in[0].wait()
+        gradient_in[1].wait()
+        mixed_in.wait()
+
+        @pl.when(role == HELPER)
         def _():
-            put(2 * tiles, left[:, :lane_count])
-
-        @pl.when(load == 1)
+            for slot in range(slots):
+                put(slot * tiles, right_gram(gradient(slot)))
+            put(slots * tiles, left_part(gradient(1), 0, lane_count))
+
+        @pl.when(role == SPARE)
         def _():
-            put(tiles, right)
-
-    @pl.when(jnp.logical_not(live))
-    def _():
-        roots_ref[...] = seed_ref[...]
-
-    @pl.when(role == HELPER)
-    def _():
-        block = whole_block(block_ref)
-        put(slot * tiles, right_gram(block))
-
-        @pl.when(slot == 1)
-        def _():
-            put(2 * tiles, left_part(block, 0, lane_count))
-
-    @pl.when(role == SPARE)
-    def _():
-        put(slot * (tiles - 1), left_part(whole_block(block_ref), lane_count, order))
-
-        @pl.when(slot == 0)
-        def _():
-            put(2 * (tiles - 1), left_part(whole_block(mixed_ref), lane_count, order))
+            for turn in range(3):
+                put(turn * (tiles - 1), left_part(gradient(turn), lane_count, order))
+
+        outs[0].start()
+        outs[1].start()
+        keep(0)
+        keep(1)
+
+    for copy in outs:
+        copy.wait()
 
 
 def finish_kernel(
+    entries,
     plan_ref,
-    factor_ref,
+    half_ref,
+    other_ref,
     left_ref,
     right_ref,
     back_ref,
-    sums_ref,
     out_ref,
     new_left_ref,
     new_right_ref,
@@ -309,9 +404,14 @@
     blocks, _, order = left_ref.shape
     cols = width // order
     tiles = order // LANES
-    plan = Plan(plan_ref, blocks, back_ref.shape[0])
-    factor = factor_ref[0]
-    norms = jnp.sqrt(sums_ref[:1, :])
+    devices, extra = back_ref.shape[0], back_ref.shape[1] - 1
+    plan = Plan(plan_ref, blocks, devices)
+    factor = scale_of(entries, half_ref, other_ref)
+    factor = 0.05 * factor * factor
+    total = jnp.zeros((rows, LANES), jnp.float32)
+    for source in range(devices):
+        total = total + back_ref[source, extra].astype(jnp.float32)
+    norms = jnp.sqrt(jnp.sum(total, axis=0, keepdims=True))
     lane = lanes((1, LANES))
     for k in range(blocks):
         owner, slot = plan.get("owner", k), plan.get("slot", k)
@@ -338,16 +438,18 @@
             )
 
 
-def butterfly(values, axis, steps):
-    size = lax.axis_size(axis)
-    for step in steps:
-        values = values + lax.ppermute(values, axis, [(i, i ^ step) for i in range(size)])
-    return values
-
-
-def blk_sum(values, axis, bit):
+def swap(values, axis, bit):
+    return lax.ppermute(values, axis, [(i, i ^ bit) for i in range(lax.axis_size(axis))])
+
+
+def ring_sum(values, axis, unit):
+    values = values + swap(values, axis, unit)
+    return values + swap(values, axis, 3 * unit)
+
+
+def blk_halves(values, axis, bit):
     size, width, near, halves = lax.axis_size("blk"), lax.axis_size("zero"), 4, 2
-    values = butterfly(values, "blk", (1, 2))
+    values = ring_sum(values, "blk", 1)
     parts = []
     for turn in range(size // near // halves):
         pairs = []
@@ -358,7 +460,8 @@
                 source = (place + shift) % size
                 pairs.append((source * width + group, place * width + group))
         parts.append(lax.ppermute(values, ("blk", "zero"), pairs))
-    return butterfly(functools.reduce(jnp.add, parts), axis, (bit,))
+    half = functools.reduce(jnp.add, parts)
+    return half, swap(half, axis, bit)
 
 
 def exchange(values):
@@ -379,9 +482,10 @@
     blocks = rows_dev * cols
     slots = roots.shape[2]
     tiles = order // LANES
+    entries = rows_dev * lax.axis_size("zero") * order * width
     me = lax.axis_index("blk").astype(jnp.int32).reshape(1)
     owner_of = owners.reshape(blocks)
-    left_old, right_old = left_stats[0], right_stats[0]
+    left_old, right_old, seeds = left_stats[0], right_stats[0], roots[0]
 
     sent, plan = pl.pallas_call(
         functools.partial(pack_kernel, slots),
@@ -391,100 +495,80 @@
         ],
         in_specs=[SMEM, SMEM, VMEM, VMEM, VMEM],
         out_specs=[VMEM, SMEM],
-        compiler_params=PARAMS,
+        compiler_params=grant(56),
         name="pack",
     )(me, owner_of, grads, left_old, right_old)
     arrived = exchange(sent)
 
-    seeds = roots[0]
-    square_spec = pl.BlockSpec((1, order, order), lambda i: (i, 0, 0))
-    fifth_shape = jax.ShapeDtypeStruct((2 * slots, order, order), jnp.bfloat16)
-    high, low = pl.pallas_call(
+    fifth = pl.pallas_call(
         fifth_kernel,
-        grid=(2 * slots,),
-        out_shape=[fifth_shape, fifth_shape],
-        in_specs=[square_spec],
-        out_specs=[square_spec, square_spec],
-        compiler_params=PARAMS,
+        out_shape=jax.ShapeDtypeStruct((2 * slots, order, 2 * order), jnp.bfloat16),
+        in_specs=[VMEM],
+        out_specs=VMEM,
+        compiler_params=grant(28),
         cost_estimate=cost(12 * slots, order, 12 * slots * order * order),
         name="fifth",
     )(seeds.reshape(2 * slots, order, order))
     square = pl.pallas_call(
         square_kernel,
         out_shape=jax.ShapeDtypeStruct((8, LANES), jnp.float32),
-        in_specs=[VMEM, pl.BlockSpec(memory_space=pl.ANY), pl.BlockSpec(memory_space=pl.ANY)],
+        in_specs=[VMEM, ANY, ANY],
         out_specs=VMEM,
-        compiler_params=PARAMS,
+        compiler_params=grant(8),
         name="square",
-    )(grads, low, sent)
-    total = blk_sum(butterfly(square, "zero", (1, 2, 4)), "zero", 1)[0, 0]
-    entries = rows_dev * lax.axis_size("zero") * order * width
-    scale = jnp.minimum(1.0, math.sqrt(entries) / (jnp.sqrt(total) + 1e-06))
-    factor = (0.05 * scale * scale).reshape(1)
-
-    side_spec = pl.BlockSpec((2, 1, order, order), lambda s: (0, s, 0, 0))
-    out_tiles = 2 * tiles + 1
+    )(grads, fifth, sent)
+    square = ring_sum(square + swap(square, "zero", 1), "zero", 2)
+    square_halves = blk_halves(square, "zero", 1)
+
+    new_second, adam = pl.pallas_call(
+        functools.partial(adam_kernel, order, entries),
+        out_shape=[
+            jax.ShapeDtypeStruct(second_moment.shape, jnp.float32),
+            jax.ShapeDtypeStruct((rows, LANES), jnp.bfloat16),
+        ],
+        in_specs=[VMEM, VMEM, VMEM, VMEM],
+        out_specs=[VMEM, VMEM],
+        compiler_params=grant(12),
+        name="adam",
+    )(*square_halves, grads, second_moment)
+
+    returned_shape = (devices, 2 * tiles + 2, rows, LANES)
+    fifth = fifth.reshape(2, slots, order, 2 * order)
     new_roots, returned = pl.pallas_call(
-        functools.partial(owner_kernel, blocks),
-        grid=(slots,),
+        functools.partial(owner_kernel, blocks, slots, entries),
         out_shape=[
-            jax.ShapeDtypeStruct((2, slots, order, order), jnp.bfloat16),
-            jax.ShapeDtypeStruct((devices, out_tiles, rows, LANES), jnp.bfloat16),
+            jax.ShapeDtypeStruct(seeds.shape, jnp.bfloat16),
+            jax.ShapeDtypeStruct(returned_shape, jnp.bfloat16),
         ],
-        in_specs=[
-            SMEM,
-            SMEM,
-            pl.BlockSpec((devices, tiles, rows, LANES), lambda s: (0, s, 0, 0)),
-            pl.BlockSpec((devices, tiles, rows, LANES), lambda s: (0, slots + s, 0, 0)),
-            side_spec,
-            side_spec,
-            side_spec,
-            pl.BlockSpec((devices, 1, rows, LANES), lambda s: (0, 2 * slots * tiles, 0, 0)),
+        in_specs=[SMEM, VMEM, VMEM, VMEM, HBM, HBM, HBM],
+        out_specs=[HBM, HBM],
+        scratch_shapes=[
+            pltpu.VMEM(arrived.shape, jnp.bfloat16),
+            pltpu.VMEM(seeds.shape, jnp.bfloat16),
+            pltpu.VMEM(fifth.shape, jnp.bfloat16),
+            pltpu.VMEM(seeds.shape, jnp.bfloat16),
+            pltpu.VMEM(returned_shape, jnp.bfloat16),
+            pltpu.SemaphoreType.DMA((3 * slots + 1,)),
+            pltpu.SemaphoreType.DMA((slots + 2,)),
         ],
-        out_specs=[
-            side_spec,
-            pl.BlockSpec((devices, out_tiles, rows, LANES), lambda s: (0, 0, 0, 0)),
-        ],
-        compiler_params=PARAMS,
+        compiler_params=grant(60),
         cost_estimate=cost(10 * slots, order, 24 * slots * order * order),
         name="owner",
-    )(
-        plan,
-        factor,
-        arrived,
-        arrived,
-        seeds,
-        high.reshape(2, slots, order, order),
-        low.reshape(2, slots, order, order),
-        arrived,
-    )
+    )(plan, *square_halves, adam, arrived, seeds, fifth)
     back = exchange(returned)
 
-    new_second, sums = pl.pallas_call(
-        functools.partial(adam_kernel, order),
-        out_shape=[
-            jax.ShapeDtypeStruct(second_moment.shape, jnp.float32),
-            jax.ShapeDtypeStruct((8, LANES), jnp.float32),
-        ],
-        in_specs=[SMEM, VMEM, VMEM, pl.BlockSpec(memory_space=pl.ANY)],
-        out_specs=[VMEM, VMEM],
-        compiler_params=PARAMS,
-        name="adam",
-    )(scale.reshape(1), grads, second_moment, returned)
-    sums = blk_sum(sums, "blk", 1)
-
     placed, new_left, new_right = pl.pallas_call(
-        finish_kernel,
+        functools.partial(finish_kernel, entries),
         out_shape=[
             jax.ShapeDtypeStruct((rows_dev, rows, width), jnp.bfloat16),
             jax.ShapeDtypeStruct(left_old.shape, jnp.float32),
             jax.ShapeDtypeStruct(right_old.shape, jnp.float32),
         ],
-        in_specs=[SMEM, SMEM, VMEM, VMEM, VMEM, VMEM],
+        in_specs=[SMEM, VMEM, VMEM, VMEM, VMEM, VMEM],
         out_specs=[VMEM, VMEM, VMEM],
-        compiler_params=PARAMS,
+        compiler_params=grant(16),
         name="finish",
-    )(plan, factor, left_old, right_old, back, sums)
+    )(plan, *square_halves, left_old, right_old, back)
     return (placed, new_second, new_left[None], new_right[None], new_roots[None])
 
 

time: 130 us -> 125 us (0.962); the launches traced: 129 us -> 125 us
  blocking collectives: 0 us -> 41.5 us
  starting transfers between devices: 55.5 us -> 27.3 us
  waiting for transfers between devices: 38.3 us -> 26.2 us
  Pallas kernels: 28.7 us -> 25.4 us
  other arithmetic: 1.99 us -> 0.02 us
    all_to_all x0 -> x1, blocking collectives: none -> 41.5 us  [exchange(): lax.all_to_all(values, 'blk', split_axis=0, concat_axis=0, tiled=True)]
    ppermute x17 -> x10, starting transfers between devices: 34.2 us -> 15.7 us  [the longest x6 8.26 us: swap(): lax.ppermute(values, axis, [(i, i ^ bit) for i in range(lax.axis_size(axi...]
    ppermute x17 -> x10, waiting for transfers between devices: 38.2 us -> 26.2 us  [the longest x4 14.9 us: blk_halves(): parts.append(lax.ppermute(values, ('blk', 'zero'), pairs))]
    all_to_all x2 -> x1, starting transfers between devices: 21.2 us -> 11.6 us  [exchange(): lax.all_to_all(values, 'blk', split_axis=0, concat_axis=0, tiled=True)]
    add x11 -> x6, other arithmetic: 1.99 us -> 0.02 us  [the longest x2 0.01 us: ring_sum(): values = values + swap(values, axis, unit)]
    pallas_call x4, Pallas kernels: 23.2 us -> 21.4 us  [the longest x1 10.8 us: local(): pl.pallas_call(functools.partial(owner_kernel, blocks, slots, entries), o...]
    pallas_call x1, Pallas kernels: 1.73 us -> 0.15 us  [local(): pl.pallas_call(square_kernel, out_shape=jax.ShapeDtypeStruct((8, LANES),...]
    unnamed x4 -> x26, local copies, waits for them, and re-layouts: 2.43 us -> 4 us
  transfers between devices with their start and end apart: 19 -> 11, of which waited for: 14 -> 8; matrix products, arithmetic and copies ran while one was open for 2% -> 0% of each run, Pallas kernels for 11% -> 7%
where the time goes in v4:
time: 125 us
  blocking collectives  41.5 us (33%)
  starting transfers between devices  27.3 us (22%)
  waiting for transfers between devices  26.2 us (21%)
  Pallas kernels  25.4 us (20%)
  local copies, waits for them, and re-layouts  4 us (3%)
    all_to_all x1, blocking collectives, exchange(): lax.all_to_all(values, 'blk', split_axis=0, concat_axis=0, tiled=True)  41.5 us
    ppermute x4, waiting for transfers between devices, blk_halves(): parts.append(lax.ppermute(values, ('blk', 'zero'), pairs))  14.9 us
    all_to_all x1, starting transfers between devices, exchange(): lax.all_to_all(values, 'blk', split_axis=0, concat_axis=0, tiled=True)  11.6 us
    ppermute x6, waiting for transfers between devices, swap(): lax.ppermute(values, axis, [(i, i ^ bit) for i in range(lax.axis_size(axi...  11.3 us
    pallas_call x1, Pallas kernels, local(): pl.pallas_call(functools.partial(owner_kernel, blocks, slots, entries), o...  10.8 us
    ppermute x6, starting transfers between devices, swap(): lax.ppermute(values, axis, [(i, i ^ bit) for i in range(lax.axis_size(axi...  8.26 us
    ppermute x4, starting transfers between devices, blk_halves(): parts.append(lax.ppermute(values, ('blk', 'zero'), pairs))  7.39 us
    pallas_call x1, Pallas kernels, local(): pl.pallas_call(fifth_kernel, out_shape=jax.ShapeDtypeStruct((2 * slots, o...  7.27 us
  transfers between devices with their start and end apart: 11, of which 8 were waited for; matrix products, arithmetic and copies ran while one was open for 0% of the time, Pallas kernels for 7%

profile of v4, /device:TPU:4, one launch (start us, length us, event | category | flops | bytes accessed | tf_op | source)
XLA Modules:
  0.0 125.1 jit_solution(15400008598805523662)
XLA Ops:
  0.6 3.8 %pack.1 = (bf16[32,17,16,128]{3,2,1,0:T(8,128)(2,1)}, s32[172]{0:T(256)}) custom-call(s32[1]{0:T(128)} %bitcast.me_ref, s32[24]{0:T(128)} %bitcast.17, bf16[2,16,6144]{2,1,0:T(8,128)(2,1)} %grads_ref.5, f32[24,16,512]{2,1,0:T(8,128)} %bitcast.11, f32[24,16,512]{2,1,0:T(8,128)} %bitcast.13), custom_call_target="tpu_custom_call" | custom-call | tf_op jit(solution)/shard_map/pack/pallas_call | solution.py:490
  4.4 11.6 %all-to-all-start = ((bf16[32,17,16,128]{3,2,1,0:T(8,128)(2,1)}), bf16[32,17,16,128]{3,2,1,0:T(8,128)(2,1)}, u32[]{:S(2)}, u32[]{:S(2)}) async-start(bf16[32,17,16,128]{3,2,1,0:T(8,128)(2,1)} %get-tuple-element.15.__), calls=%async_computation | async-start | bytes 4456448 | tf_op jit(solution)/shard_map/all_to_all | solution.py:468
  16.1 0.0 copy-start.11
  16.1 1.6 %copy-done.11 = bf16[1,2,2,512,512]{4,3,2,1,0:T(8,128)(2,1)S(1)} copy-done((bf16[1,2,2,512,512]{4,3,2,1,0:T(8,128)(2,1)S(1)}, bf16[1,2,2,512,512]{4,3,2,1,0:T(8,128)(2,1)}, u32[]{:S(2)}) %copy-start.11) | copy-done | bytes 2097176
  17.7 7.3 %fifth.1._ = bf16[4,512,1024]{2,1,0:T(8,128)(2,1)S(1)} custom-call(bf16[4,512,512]{2,1,0:T(8,128)(2,1)S(1)} %bitcast.16), custom_call_target="tpu_custom_call" | custom-call | flops 6442450944 | bytes 6291456 | tf_op jit(solution)/shard_map/fifth/pallas_call | solution.py:503
  24.9 0.0 copy-done
  24.9 0.0 copy-done.2
  25.0 0.0 copy-start.1
  25.0 0.0 copy-start.5
  25.0 0.1 square.1
  25.1 1.8 %copy-done.1 = bf16[4,512,1024]{2,1,0:T(8,128)(2,1)} copy-done((bf16[4,512,1024]{2,1,0:T(8,128)(2,1)}, bf16[4,512,1024]{2,1,0:T(8,128)(2,1)S(1)}, u32[]{:S(2)}) %copy-start.1) | copy-done | bytes 4194328
  26.9 0.0 collective-permute-start
  26.9 1.2 collective-permute-done
  28.1 1.2 collective-permute-start.1
  29.3 2.4 %collective-permute-done.1 = f32[8,128]{1,0:T(8,128)S(1)} collective-permute-done((f32[8,128]{1,0:T(8,128)S(1)}, f32[8,128]{1,0:T(8,128)S(1)}, u32[]{:S(2)}, u32[]{:S(2)}) %collective-permute-start.1) | collective-permute-done | bytes 4128 | tf_op jit(solution)/shard_map/ppermute | solution.py:442
  31.7 0.5 collective-permute-start.2
  32.2 3.1 %collective-permute-done.2 = f32[8,128]{1,0:T(8,128)S(1)} collective-permute-done((f32[8,128]{1,0:T(8,128)S(1)}, f32[8,128]{1,0:T(8,128)S(1)}, u32[]{:S(2)}, u32[]{:S(2)}) %collective-permute-start.2) | collective-permute-done | bytes 4128 | tf_op jit(solution)/shard_map/ppermute | solution.py:442
  35.3 1.7 %collective-permute-start.3 = (f32[8,128]{1,0:T(8,128)S(1)}, f32[8,128]{1,0:T(8,128)S(1)}, u32[]{:S(2)}, u32[]{:S(2)}) collective-permute-start(f32[8,128]{1,0:T(8,128)S(1)} %add.26), channel_id=1, source_target_pairs={{0,8},{8,0},{16,24},{24,16},{32,40},{40,32},{48,56},{56,48},{64,72... | collective-permute-start | bytes 12296 | tf_op jit(solution)/shard_map/ppermute | solution.py:442
  37.0 1.9 %collective-permute-done.3 = f32[8,128]{1,0:T(8,128)S(1)} collective-permute-done((f32[8,128]{1,0:T(8,128)S(1)}, f32[8,128]{1,0:T(8,128)S(1)}, u32[]{:S(2)}, u32[]{:S(2)}) %collective-permute-start.3) | collective-permute-done | bytes 4128 | tf_op jit(solution)/shard_map/ppermute | solution.py:442
  38.9 2.9 %collective-permute-start.4 = (f32[8,128]{1,0:T(8,128)S(1)}, f32[8,128]{1,0:T(8,128)S(1)}, u32[]{:S(2)}, u32[]{:S(2)}) collective-permute-start(f32[8,128]{1,0:T(8,128)S(1)} %add.27), channel_id=1, source_target_pairs={{0,24},{8,16},{16,8},{24,0},{32,56},{40,48},{48,40},{56,32},{64,88... | collective-permute-start | bytes 12296 | tf_op jit(solution)/shard_map/ppermute | solution.py:442
  41.9 1.9 %collective-permute-done.4 = f32[8,128]{1,0:T(8,128)S(1)} collective-permute-done((f32[8,128]{1,0:T(8,128)S(1)}, f32[8,128]{1,0:T(8,128)S(1)}, u32[]{:S(2)}, u32[]{:S(2)}) %collective-permute-start.4) | collective-permute-done | bytes 4128 | tf_op jit(solution)/shard_map/ppermute | solution.py:442
  43.8 4.7 %collective-permute-start.8 = (f32[8,128]{1,0:T(8,128)S(1)}, f32[8,128]{1,0:T(8,128)S(1)}, u32[]{:S(2)}, u32[]{:S(2)}) collective-permute-start(f32[8,128]{1,0:T(8,128)S(1)} %add.28), channel_id=1, source_target_pairs={{96,0},{225,1},{98,2},{227,3},{100,4},{229,5},{102,6},{231,7},{104... | collective-permute-start | bytes 12296 | tf_op jit(solution)/shard_map/ppermute | solution.py:462
  48.5 1.5 %collective-permute-start.7 = (f32[8,128]{1,0:T(8,128)S(1)}, f32[8,128]{1,0:T(8,128)S(1)}, u32[]{:S(2)}, u32[]{:S(2)}) collective-permute-start(f32[8,128]{1,0:T(8,128)S(1)} %add.28), channel_id=1, source_target_pairs={{64,0},{193,1},{66,2},{195,3},{68,4},{197,5},{70,6},{199,7},{72,8}... | collective-permute-start | bytes 12296 | tf_op jit(solution)/shard_map/ppermute | solution.py:462
  50.0 0.5 collective-permute-start.6
  50.5 0.6 collective-permute-start.5
  51.2 14.7 %collective-permute-done.8 = f32[8,128]{1,0:T(8,128)S(1)} collective-permute-done((f32[8,128]{1,0:T(8,128)S(1)}, f32[8,128]{1,0:T(8,128)S(1)}, u32[]{:S(2)}, u32[]{:S(2)}) %collective-permute-start.8) | collective-permute-done | bytes 4128 | tf_op jit(solution)/shard_map/ppermute | solution.py:462
  65.9 0.0 collective-permute-done.7
  65.9 0.2 collective-permute-done.6
  66.1 0.0 collective-permute-done.5
  66.1 0.0 copy-start.6
  66.1 1.9 %collective-permute-start.9 = (f32[8,128]{1,0:T(8,128)S(1)}, f32[8,128]{1,0:T(8,128)S(1)}, u32[]{:S(2)}, u32[]{:S(2)}) collective-permute-start(f32[8,128]{1,0:T(8,128)S(1)} %add_add_fusion.half_ref), channel_id=1, source_target_pairs={{0,1},{1,0},{2,3},{3,2},{4,5},{5,4},{6,7},{7,6},{8,9},{9,8},{10,11... | collective-permute-start | bytes 12296 | tf_op jit(solution)/shard_map/ppermute | solution.py:442
  67.9 0.8 collective-permute-done.9.other_ref
  68.8 0.0 copy-done.5
  68.8 1.4 %adam.1 = (f32[2,16,6144]{2,1,0:T(8,128)}, bf16[16,128]{1,0:T(8,128)(2,1)S(1)}) custom-call(f32[8,128]{1,0:T(8,128)S(1)} %add_add_fusion.half_ref, f32[8,128]{1,0:T(8,128)S(1)} %collective-permute-done.9.other_ref, bf16[2,16,6144]{2,1,0:T(8,128)(2,1)S(1)} %copy-done.2, f32[2,16,6144]{2,1,0:T(8,128)S(1)} %copy-done.5), custom_call_target="tpu_custom_call" | custom-call | tf_op jit(solution)/shard_map/adam/pallas_call | solution.py:523
  70.1 0.6 copy-done.12
  70.7 0.0 all-to-all-done.arrived_hbm
  70.7 0.0 copy-done.6
  70.7 0.0 copy-done.8
  70.7 10.8 %owner.1 = (bf16[2,2,512,512]{3,2,1,0:T(8,128)(2,1)}, bf16[32,10,16,128]{3,2,1,0:T(8,128)(2,1)}) custom-call(s32[172]{0:T(256)} %get-tuple-element.14.plan_ref, f32[8,128]{1,0:T(8,128)} %copy-done.6, f32[8,128]{1,0:T(8,128)} %copy-done.8, bf16[16,128]{1,0:T(8,128)(2,1)} %copy-done.12, bf16[32,17,16,128]{3,2,1,0:T(8,128)(2,1)} %all-to-all-done.arrived_hbm, ...), custom_call_target="tpu_custom_call" | custom-call | flops 5368709120 | bytes 12582912 | tf_op jit(solution)/shard_map/owner/pallas_call | solution.py:537
  81.5 0.0 copy-start.3
  81.5 0.0 copy-start.4
  81.5 0.0 copy-start.7
  81.5 0.0 copy-start.9
  81.5 0.0 copy-start.10
  81.6 41.5 %all_to_all.10.back_ref = bf16[32,10,16,128]{3,2,1,0:T(8,128)(2,1)S(1)} all-to-all(bf16[32,10,16,128]{3,2,1,0:T(8,128)(2,1)} %get-tuple-element.17), channel_id=1, replica_groups=mesh['blk'=32,'zero'=8] {'blk'}, dimensions={0} | all-to-all | bytes 2621440 | tf_op jit(solution)/shard_map/all_to_all | solution.py:468
  123.1 0.0 copy-done.9
  123.1 0.0 copy-done.10
  123.1 2.0 %finish.1 = (bf16[2,16,6144]{2,1,0:T(8,128)(2,1)}, f32[24,16,512]{2,1,0:T(8,128)}, f32[24,16,512]{2,1,0:T(8,128)}) custom-call(s32[172]{0:T(256)S(1)} %copy-done.10, f32[8,128]{1,0:T(8,128)S(1)} %copy-done.7, f32[8,128]{1,0:T(8,128)S(1)} %copy-done.9, f32[24,16,512]{2,1,0:T(8,128)S(1)} %bitcast.12, f32[24,16,512]{2,1,0:T(8,128)S(1)} %bitcast.14, ...), custom_call_target="tpu_custom_call" | custom-call | tf_op jit(solution)/shard_map/finish/pallas_call | solution.py:560
  (13 shorter events, 0.0 us)
Async XLA Ops:
  4.4 66.3 %all-to-all-start = ((bf16[32,17,16,128]{3,2,1,0:T(8,128)(2,1)}), bf16[32,17,16,128]{3,2,1,0:T(8,128)(2,1)}, u32[]{:S(2)}, u32[]{:S(2)}) async-start(bf16[32,17,16,128]{3,2,1,0:T(8,128)(2,1)} %get-tuple-element.15.__), calls=%async_computation | async-start | bytes 4456448 | tf_op jit(solution)/shard_map/all_to_all | solution.py:468
  16.1 1.6 %copy-start.11 = (bf16[1,2,2,512,512]{4,3,2,1,0:T(8,128)(2,1)S(1)}, bf16[1,2,2,512,512]{4,3,2,1,0:T(8,128)(2,1)}, u32[]{:S(2)}) copy-start(bf16[1,2,2,512,512]{4,3,2,1,0:T(8,128)(2,1)} %param.11) | copy-start | bytes 6291460
  17.7 7.3 %copy-start = (bf16[32,17,16,128]{3,2,1,0:T(8,128)(2,1)S(1)}, bf16[32,17,16,128]{3,2,1,0:T(8,128)(2,1)}, u32[]{:S(2)}) copy-start(bf16[32,17,16,128]{3,2,1,0:T(8,128)(2,1)} %get-tuple-element.15.__) | copy-start | bytes 6684676
  17.7 7.3 %copy-start.2 = (bf16[2,16,6144]{2,1,0:T(8,128)(2,1)S(1)}, bf16[2,16,6144]{2,1,0:T(8,128)(2,1)}, u32[]{:S(2)}) copy-start(bf16[2,16,6144]{2,1,0:T(8,128)(2,1)} %grads_ref.5) | copy-start | bytes 1179652
  25.0 1.9 %copy-start.1 = (bf16[4,512,1024]{2,1,0:T(8,128)(2,1)}, bf16[4,512,1024]{2,1,0:T(8,128)(2,1)S(1)}, u32[]{:S(2)}) copy-start(bf16[4,512,1024]{2,1,0:T(8,128)(2,1)S(1)} %fifth.1._) | copy-start | bytes 12582916
  25.0 43.8 %copy-start.5 = (f32[2,16,6144]{2,1,0:T(8,128)S(1)}, f32[2,16,6144]{2,1,0:T(8,128)}, u32[]{:S(2)}) copy-start(f32[2,16,6144]{2,1,0:T(8,128)} %second_ref.1) | copy-start | bytes 2359300
  26.9 1.2 collective-permute-start
  28.1 3.6 %collective-permute-start.1 = (f32[8,128]{1,0:T(8,128)S(1)}, f32[8,128]{1,0:T(8,128)S(1)}, u32[]{:S(2)}, u32[]{:S(2)}) collective-permute-start(f32[8,128]{1,0:T(8,128)S(1)} %add.24), channel_id=1, source_target_pairs={{0,2},{1,3},{2,0},{3,1},{4,6},{5,7},{6,4},{7,5},{8,10},{9,11},{10,... | collective-permute-start | bytes 12296 | tf_op jit(solution)/shard_map/ppermute | solution.py:442
  31.7 3.6 %collective-permute-start.2 = (f32[8,128]{1,0:T(8,128)S(1)}, f32[8,128]{1,0:T(8,128)S(1)}, u32[]{:S(2)}, u32[]{:S(2)}) collective-permute-start(f32[8,128]{1,0:T(8,128)S(1)} %add.25), channel_id=1, source_target_pairs={{0,6},{1,7},{2,4},{3,5},{4,2},{5,3},{6,0},{7,1},{8,14},{9,15},{10,... | collective-permute-start | bytes 12296 | tf_op jit(solution)/shard_map/ppermute | solution.py:442
  35.3 3.6 %collective-permute-start.3 = (f32[8,128]{1,0:T(8,128)S(1)}, f32[8,128]{1,0:T(8,128)S(1)}, u32[]{:S(2)}, u32[]{:S(2)}) collective-permute-start(f32[8,128]{1,0:T(8,128)S(1)} %add.26), channel_id=1, source_target_pairs={{0,8},{8,0},{16,24},{24,16},{32,40},{40,32},{48,56},{56,48},{64,72... | collective-permute-start | bytes 12296 | tf_op jit(solution)/shard_map/ppermute | solution.py:442
  38.9 4.9 %collective-permute-start.4 = (f32[8,128]{1,0:T(8,128)S(1)}, f32[8,128]{1,0:T(8,128)S(1)}, u32[]{:S(2)}, u32[]{:S(2)}) collective-permute-start(f32[8,128]{1,0:T(8,128)S(1)} %add.27), channel_id=1, source_target_pairs={{0,24},{8,16},{16,8},{24,0},{32,56},{40,48},{48,40},{56,32},{64,88... | collective-permute-start | bytes 12296 | tf_op jit(solution)/shard_map/ppermute | solution.py:442
  43.8 22.1 %collective-permute-start.8 = (f32[8,128]{1,0:T(8,128)S(1)}, f32[8,128]{1,0:T(8,128)S(1)}, u32[]{:S(2)}, u32[]{:S(2)}) collective-permute-start(f32[8,128]{1,0:T(8,128)S(1)} %add.28), channel_id=1, source_target_pairs={{96,0},{225,1},{98,2},{227,3},{100,4},{229,5},{102,6},{231,7},{104... | collective-permute-start | bytes 12296 | tf_op jit(solution)/shard_map/ppermute | solution.py:462
  48.5 17.3 %collective-permute-start.7 = (f32[8,128]{1,0:T(8,128)S(1)}, f32[8,128]{1,0:T(8,128)S(1)}, u32[]{:S(2)}, u32[]{:S(2)}) collective-permute-start(f32[8,128]{1,0:T(8,128)S(1)} %add.28), channel_id=1, source_target_pairs={{64,0},{193,1},{66,2},{195,3},{68,4},{197,5},{70,6},{199,7},{72,8}... | collective-permute-start | bytes 12296 | tf_op jit(solution)/shard_map/ppermute | solution.py:462
  50.0 16.1 %collective-permute-start.6 = (f32[8,128]{1,0:T(8,128)S(1)}, f32[8,128]{1,0:T(8,128)S(1)}, u32[]{:S(2)}, u32[]{:S(2)}) collective-permute-start(f32[8,128]{1,0:T(8,128)S(1)} %add.28), channel_id=1, source_target_pairs={{32,0},{161,1},{34,2},{163,3},{36,4},{165,5},{38,6},{167,7},{40,8}... | collective-permute-start | bytes 12296 | tf_op jit(solution)/shard_map/ppermute | solution.py:462
  50.5 15.6 %collective-permute-start.5 = (f32[8,128]{1,0:T(8,128)S(1)}, f32[8,128]{1,0:T(8,128)S(1)}, u32[]{:S(2)}, u32[]{:S(2)}) collective-permute-start(f32[8,128]{1,0:T(8,128)S(1)} %add.28), channel_id=1, source_target_pairs={{0,0},{129,1},{2,2},{131,3},{4,4},{133,5},{6,6},{135,7},{8,8},{137... | collective-permute-start | bytes 12296 | tf_op jit(solution)/shard_map/ppermute | solution.py:462
  66.1 4.7 %copy-start.6 = (f32[8,128]{1,0:T(8,128)}, f32[8,128]{1,0:T(8,128)S(1)}, u32[]{:S(2)}) copy-start(f32[8,128]{1,0:T(8,128)S(1)} %add_add_fusion.half_ref) | copy-start | bytes 12292
  66.1 2.7 %collective-permute-start.9 = (f32[8,128]{1,0:T(8,128)S(1)}, f32[8,128]{1,0:T(8,128)S(1)}, u32[]{:S(2)}, u32[]{:S(2)}) collective-permute-start(f32[8,128]{1,0:T(8,128)S(1)} %add_add_fusion.half_ref), channel_id=1, source_target_pairs={{0,1},{1,0},{2,3},{3,2},{4,5},{5,4},{6,7},{7,6},{8,9},{9,8},{10,11... | collective-permute-start | bytes 12296 | tf_op jit(solution)/shard_map/ppermute | solution.py:442
  68.8 2.0 %copy-start.8 = (f32[8,128]{1,0:T(8,128)}, f32[8,128]{1,0:T(8,128)S(1)}, u32[]{:S(2)}) copy-start(f32[8,128]{1,0:T(8,128)S(1)} %collective-permute-done.9.other_ref) | copy-start | bytes 12292
  70.1 0.6 copy-start.12
  81.5 41.6 %copy-start.3 = (f32[1,24,16,512]{3,2,1,0:T(8,128)S(1)}, f32[1,24,16,512]{3,2,1,0:T(8,128)}, u32[]{:S(2)}) copy-start(f32[1,24,16,512]{3,2,1,0:T(8,128)} %param.8) | copy-start | bytes 2359300
  81.5 41.6 %copy-start.4 = (f32[1,24,16,512]{3,2,1,0:T(8,128)S(1)}, f32[1,24,16,512]{3,2,1,0:T(8,128)}, u32[]{:S(2)}) copy-start(f32[1,24,16,512]{3,2,1,0:T(8,128)} %param.9) | copy-start | bytes 2359300
  81.5 41.6 %copy-start.7 = (f32[8,128]{1,0:T(8,128)S(1)}, f32[8,128]{1,0:T(8,128)}, u32[]{:S(2)}) copy-start(f32[8,128]{1,0:T(8,128)} %copy-done.6) | copy-start | bytes 12292
  81.5 41.6 %copy-start.9 = (f32[8,128]{1,0:T(8,128)S(1)}, f32[8,128]{1,0:T(8,128)}, u32[]{:S(2)}) copy-start(f32[8,128]{1,0:T(8,128)} %copy-done.8) | copy-start | bytes 12292
  81.5 41.6 %copy-start.10 = (s32[172]{0:T(256)S(1)}, s32[172]{0:T(256)}, u32[]{:S(2)}) copy-start(s32[172]{0:T(256)} %get-tuple-element.14.plan_ref) | copy-start | bytes 2068

commit v5 on v4

--- a/solution.py
+++ b/solution.py
@@ -130,28 +130,76 @@
         self.put("own", 0, self.get("load", me))
 
 
-def pack_kernel(slots, me_ref, owner_ref, grads_ref, left_ref, right_ref, out_ref, plan_ref):
+def pack_kernel(
+    slots,
+    me_ref,
+    owner_ref,
+    grads_hbm,
+    left_hbm,
+    right_hbm,
+    out_hbm,
+    plan_ref,
+    role_ref,
+    grads_ref,
+    left_ref,
+    right_ref,
+    out_ref,
+    in_sems,
+    out_sems,
+):
     rows_dev, rows, width = grads_ref.shape
     order = left_ref.shape[-1]
     cols = width // order
     blocks = rows_dev * cols
     tiles = order // LANES
     devices, extra = out_ref.shape[0], out_ref.shape[1] - 1
+    parts = 4
+    grads_in = pltpu.make_async_copy(grads_hbm, grads_ref, in_sems.at[0])
+    grads_in.start()
+    stats_in = []
+    for part in range(parts):
+        where = pl.ds(part * blocks // parts, blocks // parts)
+        pair = []
+        for side, (source, target) in enumerate(((left_hbm, left_ref), (right_hbm, right_ref))):
+            pair.append(
+                pltpu.make_async_copy(
+                    source.at[where], target.at[where], in_sems.at[1 + 2 * part + side]
+                )
+            )
+            pair[-1].start()
+        stats_in.append(pair)
     me = me_ref[0]
     plan = Plan(plan_ref, blocks, devices)
     plan.fill(owner_ref, me)
+    role_ref[0] = plan.get("role")
+    role_ref[1] = plan.get("own")
     tile_row = sublanes((rows, LANES))
     for owner in range(devices):
         out_ref[owner, extra] = jnp.zeros((rows, LANES), jnp.bfloat16)
-    row = me * rows + sublanes((rows, order))
-    lower = lanes((rows, order)) <= row
-    mine = lanes((rows, order)) == row
+    grads_in.wait()
     for k in range(blocks):
         owner, slot = plan.get("owner", k), plan.get("slot", k)
         piece = grads_ref[k // cols, :, (k % cols) * order : (k % cols + 1) * order]
         store_piece(out_ref, owner, slot * tiles, piece)
         store_piece(out_ref, plan.get("helper", owner), slot * tiles, piece)
         store_piece(out_ref, plan.spare_of(k), k % plan.share() * tiles, piece)
+    outs = []
+    for turn, (first, count) in enumerate(
+        ((0, slots * tiles), (slots * tiles, out_ref.shape[1] - slots * tiles))
+    ):
+        where = (slice(None), pl.ds(first, count))
+        outs.append(
+            pltpu.make_async_copy(out_ref.at[where], out_hbm.at[where], out_sems.at[turn])
+        )
+    outs[0].start()
+    row = me * rows + sublanes((rows, order))
+    lower = lanes((rows, order)) <= row
+    mine = lanes((rows, order)) == row
+    for k in range(blocks):
+        if k % (blocks // parts) == 0:
+            for copy in stats_in[k // (blocks // parts)]:
+                copy.wait()
+        owner, slot = plan.get("owner", k), plan.get("slot", k)
         right = right_ref[k]
         mixed = jnp.where(lower, left_ref[k], right).astype(jnp.bfloat16)
         store_piece(out_ref, owner, (slots + slot) * tiles, mixed)
@@ -163,6 +211,9 @@
         out_ref[owner, extra] = jnp.where(
             tile_row == slot, diagonal, out_ref[owner, extra].astype(jnp.float32)
         ).astype(jnp.bfloat16)
+    outs[1].start()
+    for copy in outs:
+        copy.wait()
 
 
 def square_kernel(grads_ref, _, __, out_ref):
@@ -177,23 +228,29 @@
     out_ref[...] = jnp.broadcast_to(jnp.sum(total, keepdims=True), out_ref.shape)
 
 
-def fifth_kernel(seed_ref, out_ref):
+def exact_ratio(diagonal):
+    rounded = diagonal.astype(jnp.bfloat16).astype(jnp.float32)
+    return jnp.where(rounded == 0.0, 1.0, diagonal / jnp.where(rounded == 0.0, 1.0, rounded))
+
+
+def fifth_kernel(seed_ref, out_ref, ratio_ref):
     order = seed_ref.shape[-1]
+    same = sublanes((order, order)) == lanes((order, order))
     for place in range(seed_ref.shape[0]):
         seed = seed_ref[place]
         high, low = split(dot(seed, seed))
         high, low = split(dot(high, high) + (dot(high, low) + dot(low, high)))
-        high, low = split(-0.25 * (dot(seed, high) + dot(seed, low)))
-        out_ref[place, :, :order] = high
-        out_ref[place, :, order:] = low
-
-
-def adam_kernel(
-    order, entries, half_ref, other_ref, grads_ref, second_ref, new_ref, tile_ref
-):
+        fifth = -0.25 * (dot(seed, high) + dot(seed, low))
+        marked = jnp.where(same, fifth, 0.0)
+        across = exact_ratio(jnp.sum(marked, axis=0, keepdims=True))
+        down = exact_ratio(jnp.sum(marked, axis=1, keepdims=True))
+        out_ref[place] = (fifth / across).astype(jnp.bfloat16)
+        ratio_ref[place] = jnp.broadcast_to(down, ratio_ref.shape[1:])
+
+
+def adam_work(scale, grads_ref, second_ref, new_ref, order):
     rows_dev, rows, width = grads_ref.shape
     cols = width // order
-    scale = scale_of(entries, half_ref, other_ref)
     sums = jnp.zeros((1, LANES), jnp.float32)
     lane = lanes((1, LANES))
     for k in range(rows_dev * cols):
@@ -203,55 +260,69 @@
         new_ref[where] = second
         step = clipped / (jnp.sqrt(second) + 1e-08)
         sums = jnp.where(lane == k, jnp.sum(step * step, keepdims=True), sums)
-    tile_row = sublanes(tile_ref.shape)
-    tile = jnp.zeros(tile_ref.shape, jnp.float32)
+    tile_row = sublanes((rows, LANES))
+    tile = jnp.zeros((rows, LANES), jnp.float32)
     for place, term in enumerate(thirds(sums)):
         tile = jnp.where(tile_row == place, term, tile)
-    tile_ref[...] = tile.astype(jnp.bfloat16)
+    return tile
 
 
 def owner_kernel(
-    blocks,
     slots,
     entries,
-    plan_ref,
+    role_ref,
     half_ref,
     other_ref,
-    adam_ref,
+    grads_hbm,
+    second_hbm,
     arrived_hbm,
     seed_hbm,
     fifth_hbm,
+    ratio_hbm,
     roots_hbm,
     out_hbm,
+    new_hbm,
+    grads_ref,
+    second_ref,
     arrived_ref,
     seed_ref,
     fifth_ref,
+    ratio_ref,
     roots_ref,
     out_ref,
+    new_ref,
     in_sems,
     out_sems,
 ):
     devices, arrived_tiles, rows, lane_count = arrived_ref.shape
     order = seed_ref.shape[-1]
     tiles = order // lane_count
-    plan = Plan(plan_ref, blocks, devices)
-    role, load = plan.get("role"), plan.get("own")
-
-    sources = []
-    for slot in range(slots):
-        sources.append((arrived_hbm, arrived_ref, (slice(None), pl.ds(slot * tiles, tiles))))
+    role, load = role_ref[0], role_ref[1]
+    scale = scale_of(entries, half_ref, other_ref)
+    factor = 0.05 * scale * scale
+
+    sources = [(grads_hbm, grads_ref, ()), (second_hbm, second_ref, ())]
+    sources.append((arrived_hbm, arrived_ref, (slice(None), pl.ds(0, tiles))))
     mixed_at = (slice(None), pl.ds(slots * tiles, arrived_tiles - slots * tiles))
     sources.append((arrived_hbm, arrived_ref, mixed_at))
     for slot in range(slots):
-        sources.append((fifth_hbm, fifth_ref, (slice(None), slot)))
-        sources.append((seed_hbm, seed_ref, (slice(None), slot)))
+        if slot > 0:
+            sources.append((arrived_hbm, arrived_ref, (slice(None), pl.ds(slot * tiles, tiles))))
+        for source, target in ((fifth_hbm, fifth_ref), (ratio_hbm, ratio_ref), (seed_hbm, seed_ref)):
+            sources.append((source, target, (slice(None), slot)))
     copies = [
-        pltpu.make_async_copy(source.at[where], target.at[where], in_sems.at[place])
+        pltpu.make_async_copy(
+            source.at[where] if where else source,
+            target.at[where] if where else target,
+            in_sems.at[place],
+        )
         for place, (source, target, where) in enumerate(sources)
     ]
-    gradient_in, mixed_in, root_in = copies[:slots], copies[slots], copies[slots + 1 :]
-    for copy in (gradient_in[0], mixed_in, *root_in[:2], *gradient_in[1:], *root_in[2:]):
+    for copy in copies:
         copy.start()
+    adam_in, mixed_in = copies[:2], copies[3]
+    gradient_in = [copies[2], copies[7]]
+    root_in = [copies[4:7], copies[8:11]]
     shares = [
         (slice(None), pl.ds(0, tiles)),
         (slice(None), pl.ds(tiles, out_ref.shape[1] - tiles)),
@@ -264,10 +335,21 @@
             roots_ref.at[:, slot], roots_hbm.at[:, slot], out_sems.at[len(shares) + slot]
         )
         for slot in range(slots)
-    ]
-    out_ref[:, out_ref.shape[1] - 1] = jnp.broadcast_to(
-        adam_ref[...][None], (devices, rows, lane_count)
-    )
+    ] + [pltpu.make_async_copy(new_ref, new_hbm, out_sems.at[len(shares) + slots])]
+    for copy in adam_in:
+        copy.wait()
+    adam = adam_work(scale, grads_ref, second_ref, new_ref, order)
+    outs[-1].start()
+
+    def put_sums(norms):
+        tile = adam
+        tile_row, lane = sublanes((rows, lane_count)), lanes((rows, lane_count))
+        for slot, norm in enumerate(norms):
+            for place, term in enumerate(thirds(norm)):
+                tile = jnp.where((tile_row == 3 + place) & (lane == slot), term, tile)
+        out_ref[:, out_ref.shape[1] - 1] = jnp.broadcast_to(
+            tile.astype(jnp.bfloat16)[None], (devices, rows, lane_count)
+        )
 
     def put(first, value):
         value = value.astype(jnp.bfloat16)
@@ -312,33 +394,34 @@
         return left_old, right_old
 
     def work(slot):
-        factor = scale_of(entries, half_ref, other_ref)
-        factor = 0.05 * factor * factor
         gradient_in[slot].wait()
         block = gradient(slot)
         grams = left_part(block, 0, order), right_gram(block)
         if slot == 0:
             mixed_in.wait()
         olds = old_stats(slot)
-        for copy in root_in[2 * slot : 2 * slot + 2]:
+        for copy in root_in[slot]:
             copy.wait()
+        same = sublanes((order, order)) == lanes((order, order))
         new_pair = []
         for side, (old, gram) in enumerate(zip(olds, grams)):
-            high, low = split(BETA * old + factor * gram)
-            moved = dot(fifth_ref[side, slot], jnp.concatenate([high, high]))
-            moved = moved + dot(fifth_ref[side, slot, :, :order], low)
-            root = 1.25 * seed_ref[side, slot].astype(jnp.float32) + moved
+            ratio = jnp.concatenate([ratio_ref[side, slot]] * tiles, axis=1)
+            new = (BETA * old + factor * gram) * ratio
+            across = exact_ratio(jnp.sum(jnp.where(same, new, 0.0), axis=0, keepdims=True))
+            moved = dot(fifth_ref[side, slot], (new * (1.0 / across)).astype(jnp.bfloat16))
+            root = 1.25 * seed_ref[side, slot].astype(jnp.float32) + moved * across
             new_pair.append(root.astype(jnp.bfloat16))
             roots_ref[side, slot] = new_pair[-1]
         outs[len(shares) + slot].start()
         applied = dot(new_pair[0], block).astype(jnp.bfloat16)
-        direction = dot(applied, new_pair[1]).astype(jnp.bfloat16).astype(jnp.float32)
-        norm = jnp.sqrt(jnp.sum(direction * direction, keepdims=True)) + 1e-06
-        put(slot * tiles, direction * (1.0 / norm))
-        return grams
+        direction = dot(applied, new_pair[1]).astype(jnp.bfloat16)
+        put(slot * tiles, direction)
+        wide = direction.astype(jnp.float32)
+        norm = 1.0 / (jnp.sqrt(jnp.sum(wide * wide, keepdims=True)) + 1e-06)
+        return grams, norm
 
     def keep(slot):
-        for copy in root_in[2 * slot : 2 * slot + 2]:
+        for copy in root_in[slot]:
             copy.wait()
         for side in range(2):
             roots_ref[side, slot] = seed_ref[side, slot]
@@ -346,18 +429,20 @@
 
     @pl.when(load == 2)
     def _():
-        left, _ = work(0)
+        (left, _), first = work(0)
         put(2 * tiles, left[:, :lane_count])
         outs[0].start()
-        work(1)
+        _, second = work(1)
+        put_sums([first, second])
         outs[1].start()
 
     @pl.when(load == 1)
     def _():
-        left, right = work(0)
+        (left, right), first = work(0)
         outs[0].start()
         put(tiles, right)
         put(2 * tiles, left[:, :lane_count])
+        put_sums([first])
         outs[1].start()
         gradient_in[1].wait()
         keep(1)
@@ -367,6 +452,7 @@
         gradient_in[0].wait()
         gradient_in[1].wait()
         mixed_in.wait()
+        put_sums([])
 
         @pl.when(role == HELPER)
         def _():
@@ -411,13 +497,19 @@
     total = jnp.zeros((rows, LANES), jnp.float32)
     for source in range(devices):
         total = total + back_ref[source, extra].astype(jnp.float32)
-    norms = jnp.sqrt(jnp.sum(total, axis=0, keepdims=True))
-    lane = lanes((1, LANES))
+    tile_row, lane = sublanes((rows, LANES)), lanes((rows, LANES))
+    norms = jnp.sqrt(jnp.sum(jnp.where(tile_row < 3, total, 0.0), axis=0, keepdims=True))
     for k in range(blocks):
         owner, slot = plan.get("owner", k), plan.get("slot", k)
         helper, single = plan.get("helper", owner), plan.get("single", k)
         spare = plan.spare_of(k)
-        norm = jnp.sum(jnp.where(lane == k, norms, 0.0), axis=1, keepdims=True)
+        norm = jnp.sum(jnp.where(lane[:1] == k, norms, 0.0), axis=1, keepdims=True)
+        inverse = jnp.where(
+            (lane == slot) & (tile_row >= 3) & (tile_row < 6),
+            back_ref[owner, extra].astype(jnp.float32),
+            0.0,
+        )
+        norm = norm * jnp.sum(inverse, keepdims=True)
         right_from = jnp.where(single == 1, 1, slot) * tiles
         for tile in range(tiles):
             part = slice(tile * LANES, (tile + 1) * LANES)
@@ -487,24 +579,37 @@
     owner_of = owners.reshape(blocks)
     left_old, right_old, seeds = left_stats[0], right_stats[0], roots[0]
 
-    sent, plan = pl.pallas_call(
+    sent_shape = (devices, 2 * slots * tiles + 1, rows, LANES)
+    sent, plan, role = pl.pallas_call(
         functools.partial(pack_kernel, slots),
         out_shape=[
-            jax.ShapeDtypeStruct((devices, 2 * slots * tiles + 1, rows, LANES), jnp.bfloat16),
+            jax.ShapeDtypeStruct(sent_shape, jnp.bfloat16),
             jax.ShapeDtypeStruct((Plan.size(blocks, devices),), jnp.int32),
+            jax.ShapeDtypeStruct((2,), jnp.int32),
         ],
-        in_specs=[SMEM, SMEM, VMEM, VMEM, VMEM],
-        out_specs=[VMEM, SMEM],
-        compiler_params=grant(56),
+        in_specs=[SMEM, SMEM, HBM, HBM, HBM],
+        out_specs=[HBM, SMEM, SMEM],
+        scratch_shapes=[
+            pltpu.VMEM(grads.shape, jnp.bfloat16),
+            pltpu.VMEM(left_old.shape, jnp.float32),
+            pltpu.VMEM(right_old.shape, jnp.float32),
+            pltpu.VMEM(sent_shape, jnp.bfloat16),
+            pltpu.SemaphoreType.DMA((9,)),
+            pltpu.SemaphoreType.DMA((2,)),
+        ],
+        compiler_params=grant(60),
         name="pack",
     )(me, owner_of, grads, left_old, right_old)
     arrived = exchange(sent)
 
-    fifth = pl.pallas_call(
+    fifth, ratio = pl.pallas_call(
         fifth_kernel,
-        out_shape=jax.ShapeDtypeStruct((2 * slots, order, 2 * order), jnp.bfloat16),
+        out_shape=[
+            jax.ShapeDtypeStruct((2 * slots, order, order), jnp.bfloat16),
+            jax.ShapeDtypeStruct((2 * slots, order, LANES), jnp.float32),
+        ],
         in_specs=[VMEM],
-        out_specs=VMEM,
+        out_specs=[VMEM, VMEM],
         compiler_params=grant(28),
         cost_estimate=cost(12 * slots, order, 12 * slots * order * order),
         name="fifth",
@@ -520,41 +625,35 @@
     square = ring_sum(square + swap(square, "zero", 1), "zero", 2)
     square_halves = blk_halves(square, "zero", 1)
 
-    new_second, adam = pl.pallas_call(
-        functools.partial(adam_kernel, order, entries),
-        out_shape=[
-            jax.ShapeDtypeStruct(second_moment.shape, jnp.float32),
-            jax.ShapeDtypeStruct((rows, LANES), jnp.bfloat16),
-        ],
-        in_specs=[VMEM, VMEM, VMEM, VMEM],
-        out_specs=[VMEM, VMEM],
-        compiler_params=grant(12),
-        name="adam",
-    )(*square_halves, grads, second_moment)
-
     returned_shape = (devices, 2 * tiles + 2, rows, LANES)
-    fifth = fifth.reshape(2, slots, order, 2 * order)
-    new_roots, returned = pl.pallas_call(
-        functools.partial(owner_kernel, blocks, slots, entries),
+    fifth = fifth.reshape(2, slots, order, order)
+    ratio = ratio.reshape(2, slots, order, LANES)
+    new_roots, returned, new_second = pl.pallas_call(
+        functools.partial(owner_kernel, slots, entries),
         out_shape=[
             jax.ShapeDtypeStruct(seeds.shape, jnp.bfloat16),
             jax.ShapeDtypeStruct(returned_shape, jnp.bfloat16),
+            jax.ShapeDtypeStruct(second_moment.shape, jnp.float32),
         ],
-        in_specs=[SMEM, VMEM, VMEM, VMEM, HBM, HBM, HBM],
-        out_specs=[HBM, HBM],
+        in_specs=[SMEM, VMEM, VMEM, HBM, HBM, HBM, HBM, HBM, HBM],
+        out_specs=[HBM, HBM, HBM],
         scratch_shapes=[
+            pltpu.VMEM(grads.shape, jnp.bfloat16),
+            pltpu.VMEM(second_moment.shape, jnp.float32),
             pltpu.VMEM(arrived.shape, jnp.bfloat16),
             pltpu.VMEM(seeds.shape, jnp.bfloat16),
             pltpu.VMEM(fifth.shape, jnp.bfloat16),
+            pltpu.VMEM(ratio.shape, jnp.float32),
             pltpu.VMEM(seeds.shape, jnp.bfloat16),
             pltpu.VMEM(returned_shape, jnp.bfloat16),
-            pltpu.SemaphoreType.DMA((3 * slots + 1,)),
-            pltpu.SemaphoreType.DMA((slots + 2,)),
+            pltpu.VMEM(second_moment.shape, jnp.float32),
+            pltpu.SemaphoreType.DMA((4 * slots + 3,)),
+            pltpu.SemaphoreType.DMA((slots + 3,)),
         ],
         compiler_params=grant(60),
-        cost_estimate=cost(10 * slots, order, 24 * slots * order * order),
+        cost_estimate=cost(8 * slots, order, 24 * slots * order * order),
         name="owner",
-    )(plan, *square_halves, adam, arrived, seeds, fifth)
+    )(role, *square_halves, grads, second_moment, arrived, seeds, fifth, ratio)
     back = exchange(returned)
 
     placed, new_left, new_right = pl.pallas_call(

time: 125 us -> 124 us (level)
  Pallas kernels: 25.4 us -> 20.8 us
  blocking collectives: 41.5 us -> 45.4 us
    pallas_call x3 -> x2, Pallas kernels: 19.4 us -> 14.4 us  [the longest x1 7.59 us: local(): pl.pallas_call(fifth_kernel, out_shape=[jax.ShapeDtypeStruct((2 * slots,...]
    all_to_all x1, blocking collectives: 41.5 us -> 45.4 us  [exchange(): lax.all_to_all(values, 'blk', split_axis=0, concat_axis=0, tiled=True)]
    unnamed x26 -> x24, local copies, waits for them, and re-layouts: 4 us -> 3.18 us
  transfers between devices with their start and end apart: 11 -> 11, of which waited for: 8 -> 9; matrix products, arithmetic and copies ran while one was open for 0% -> 0% of each run, Pallas kernels for 7% -> 6%
where the time goes in v5:
time: 124 us
  blocking collectives  45.4 us (37%)
  starting transfers between devices  27.3 us (22%)
  waiting for transfers between devices  26.6 us (21%)
  Pallas kernels  20.8 us (17%)
  local copies, waits for them, and re-layouts  3.18 us (3%)
    all_to_all x1, blocking collectives, exchange(): lax.all_to_all(values, 'blk', split_axis=0, concat_axis=0, tiled=True)  45.4 us
    ppermute x4, waiting for transfers between devices, blk_halves(): parts.append(lax.ppermute(values, ('blk', 'zero'), pairs))  14.9 us
    all_to_all x1, starting transfers between devices, exchange(): lax.all_to_all(values, 'blk', split_axis=0, concat_axis=0, tiled=True)  11.6 us
    ppermute x6, waiting for transfers between devices, swap(): lax.ppermute(values, axis, [(i, i ^ bit) for i in range(lax.axis_size(axi...  11.2 us
    ppermute x6, starting transfers between devices, swap(): lax.ppermute(values, axis, [(i, i ^ bit) for i in range(lax.axis_size(axi...  8.28 us
    pallas_call x1, Pallas kernels, local(): pl.pallas_call(fifth_kernel, out_shape=[jax.ShapeDtypeStruct((2 * slots,...  7.59 us
    ppermute x4, starting transfers between devices, blk_halves(): parts.append(lax.ppermute(values, ('blk', 'zero'), pairs))  7.39 us
    pallas_call x1, Pallas kernels, local(): pl.pallas_call(functools.partial(owner_kernel, slots, entries), out_shape...  6.84 us
  transfers between devices with their start and end apart: 11, of which 9 were waited for; matrix products, arithmetic and copies ran while one was open for 0% of the time, Pallas kernels for 6%

profile of v5, /device:TPU:4, one launch (start us, length us, event | category | flops | bytes accessed | tf_op | source)
XLA Modules:
  0.0 124.1 jit_solution(11951038790277803708)
XLA Ops:
  0.6 3.9 %pack.1 = (bf16[32,17,16,128]{3,2,1,0:T(8,128)(2,1)}, s32[172]{0:T(256)}, s32[2]{0:T(128)}) custom-call(s32[1]{0:T(128)} %bitcast.me_ref, s32[24]{0:T(128)} %bitcast.19, bf16[2,16,6144]{2,1,0:T(8,128)(2,1)} %grads_hbm.3, f32[24,16,512]{2,1,0:T(8,128)} %bitcast.11, f32[24,16,512]{2,1,0:T(8,128)} %bitcast.13), custom_call_target="tpu_custom_call" | custom-call | tf_op jit(solution)/shard_map/pack/pallas_call | solution.py:583
  4.6 11.6 %all-to-all-start = ((bf16[32,17,16,128]{3,2,1,0:T(8,128)(2,1)}), bf16[32,17,16,128]{3,2,1,0:T(8,128)(2,1)}, u32[]{:S(2)}, u32[]{:S(2)}) async-start(bf16[32,17,16,128]{3,2,1,0:T(8,128)(2,1)} %get-tuple-element.18.__), calls=%async_computation | async-start | bytes 4456448 | tf_op jit(solution)/shard_map/all_to_all | solution.py:560
  16.2 0.0 copy-start.10
  16.2 1.6 %copy-done.10 = bf16[1,2,2,512,512]{4,3,2,1,0:T(8,128)(2,1)S(1)} copy-done((bf16[1,2,2,512,512]{4,3,2,1,0:T(8,128)(2,1)S(1)}, bf16[1,2,2,512,512]{4,3,2,1,0:T(8,128)(2,1)}, u32[]{:S(2)}) %copy-start.10) | copy-done | bytes 2097176
  17.8 7.6 %fifth.1 = (bf16[4,512,512]{2,1,0:T(8,128)(2,1)S(1)}, f32[4,512,128]{2,1,0:T(8,128)S(1)}) custom-call(bf16[4,512,512]{2,1,0:T(8,128)(2,1)S(1)} %bitcast.17), custom_call_target="tpu_custom_call" | custom-call | flops 6442450944 | bytes 6291456 | tf_op jit(solution)/shard_map/fifth/pallas_call | solution.py:605
  25.4 0.0 copy-start.3
  25.4 0.0 copy-start.11
  25.4 0.0 copy-done
  25.4 0.0 copy-done.4
  25.4 0.1 square.1
  25.6 1.2 copy-done.3
  26.8 0.3 copy-done.11
  27.0 0.0 collective-permute-start
  27.0 1.2 collective-permute-done
  28.2 1.2 collective-permute-start.1
  29.4 2.4 %collective-permute-done.1 = f32[8,128]{1,0:T(8,128)S(1)} collective-permute-done((f32[8,128]{1,0:T(8,128)S(1)}, f32[8,128]{1,0:T(8,128)S(1)}, u32[]{:S(2)}, u32[]{:S(2)}) %collective-permute-start.1) | collective-permute-done | bytes 4128 | tf_op jit(solution)/shard_map/ppermute | solution.py:534
  31.8 0.5 collective-permute-start.2
  32.3 3.1 %collective-permute-done.2 = f32[8,128]{1,0:T(8,128)S(1)} collective-permute-done((f32[8,128]{1,0:T(8,128)S(1)}, f32[8,128]{1,0:T(8,128)S(1)}, u32[]{:S(2)}, u32[]{:S(2)}) %collective-permute-start.2) | collective-permute-done | bytes 4128 | tf_op jit(solution)/shard_map/ppermute | solution.py:534
  35.4 1.7 %collective-permute-start.3 = (f32[8,128]{1,0:T(8,128)S(1)}, f32[8,128]{1,0:T(8,128)S(1)}, u32[]{:S(2)}, u32[]{:S(2)}) collective-permute-start(f32[8,128]{1,0:T(8,128)S(1)} %add.26), channel_id=1, source_target_pairs={{0,8},{8,0},{16,24},{24,16},{32,40},{40,32},{48,56},{56,48},{64,72... | collective-permute-start | bytes 12296 | tf_op jit(solution)/shard_map/ppermute | solution.py:534
  37.1 1.9 %collective-permute-done.3 = f32[8,128]{1,0:T(8,128)S(1)} collective-permute-done((f32[8,128]{1,0:T(8,128)S(1)}, f32[8,128]{1,0:T(8,128)S(1)}, u32[]{:S(2)}, u32[]{:S(2)}) %collective-permute-start.3) | collective-permute-done | bytes 4128 | tf_op jit(solution)/shard_map/ppermute | solution.py:534
  39.0 3.0 %collective-permute-start.4 = (f32[8,128]{1,0:T(8,128)S(1)}, f32[8,128]{1,0:T(8,128)S(1)}, u32[]{:S(2)}, u32[]{:S(2)}) collective-permute-start(f32[8,128]{1,0:T(8,128)S(1)} %add.27), channel_id=1, source_target_pairs={{0,24},{8,16},{16,8},{24,0},{32,56},{40,48},{48,40},{56,32},{64,88... | collective-permute-start | bytes 12296 | tf_op jit(solution)/shard_map/ppermute | solution.py:534
  42.0 1.9 %collective-permute-done.4 = f32[8,128]{1,0:T(8,128)S(1)} collective-permute-done((f32[8,128]{1,0:T(8,128)S(1)}, f32[8,128]{1,0:T(8,128)S(1)}, u32[]{:S(2)}, u32[]{:S(2)}) %collective-permute-start.4) | collective-permute-done | bytes 4128 | tf_op jit(solution)/shard_map/ppermute | solution.py:534
  43.9 4.7 %collective-permute-start.8 = (f32[8,128]{1,0:T(8,128)S(1)}, f32[8,128]{1,0:T(8,128)S(1)}, u32[]{:S(2)}, u32[]{:S(2)}) collective-permute-start(f32[8,128]{1,0:T(8,128)S(1)} %add.28), channel_id=1, source_target_pairs={{96,0},{225,1},{98,2},{227,3},{100,4},{229,5},{102,6},{231,7},{104... | collective-permute-start | bytes 12296 | tf_op jit(solution)/shard_map/ppermute | solution.py:554
  48.6 1.5 %collective-permute-start.7 = (f32[8,128]{1,0:T(8,128)S(1)}, f32[8,128]{1,0:T(8,128)S(1)}, u32[]{:S(2)}, u32[]{:S(2)}) collective-permute-start(f32[8,128]{1,0:T(8,128)S(1)} %add.28), channel_id=1, source_target_pairs={{64,0},{193,1},{66,2},{195,3},{68,4},{197,5},{70,6},{199,7},{72,8}... | collective-permute-start | bytes 12296 | tf_op jit(solution)/shard_map/ppermute | solution.py:554
  50.1 0.5 collective-permute-start.6
  50.6 0.6 collective-permute-start.5
  51.3 14.7 %collective-permute-done.8 = f32[8,128]{1,0:T(8,128)S(1)} collective-permute-done((f32[8,128]{1,0:T(8,128)S(1)}, f32[8,128]{1,0:T(8,128)S(1)}, u32[]{:S(2)}, u32[]{:S(2)}) %collective-permute-start.8) | collective-permute-done | bytes 4128 | tf_op jit(solution)/shard_map/ppermute | solution.py:554
  66.0 0.0 collective-permute-done.7
  66.0 0.2 collective-permute-done.6
  66.2 0.0 collective-permute-done.5
  66.2 0.0 copy-start.5
  66.2 1.9 %collective-permute-start.9 = (f32[8,128]{1,0:T(8,128)S(1)}, f32[8,128]{1,0:T(8,128)S(1)}, u32[]{:S(2)}, u32[]{:S(2)}) collective-permute-start(f32[8,128]{1,0:T(8,128)S(1)} %add_add_fusion.half_ref), channel_id=1, source_target_pairs={{0,1},{1,0},{2,3},{3,2},{4,5},{5,4},{6,7},{7,6},{8,9},{9,8},{10,11... | collective-permute-start | bytes 12296 | tf_op jit(solution)/shard_map/ppermute | solution.py:534
  68.1 0.8 collective-permute-done.9.other_ref
  68.9 0.5 all-to-all-done.arrived_hbm
  69.4 0.0 copy-done.5
  69.4 0.1 copy-done.7
  69.5 6.8 %owner.1 = (bf16[2,2,512,512]{3,2,1,0:T(8,128)(2,1)}, bf16[32,10,16,128]{3,2,1,0:T(8,128)(2,1)}, f32[2,16,6144]{2,1,0:T(8,128)}) custom-call(s32[2]{0:T(128)} %get-tuple-element.19.role_ref, f32[8,128]{1,0:T(8,128)} %copy-done.5, f32[8,128]{1,0:T(8,128)} %copy-done.7, bf16[2,16,6144]{2,1,0:T(8,128)(2,1)} %grads_hbm.3, f32[2,16,6144]{2,1,0:T(8,128)} %second_hbm.1, ...), custom_call_target="tpu_custom_call" | custom-call | flops 4294967296 | bytes 12582912 | tf_op jit(solution)/shard_map/owner/pallas_call | solution.py:631
  76.3 0.0 copy-start.1
  76.3 0.0 copy-start.2
  76.4 0.0 copy-start.6
  76.4 0.0 copy-start.8
  76.4 0.0 copy-start.9
  76.4 45.4 %all_to_all.10.back_ref = bf16[32,10,16,128]{3,2,1,0:T(8,128)(2,1)S(1)} all-to-all(bf16[32,10,16,128]{3,2,1,0:T(8,128)(2,1)} %get-tuple-element.21), channel_id=1, replica_groups=mesh['blk'=32,'zero'=8] {'blk'}, dimensions={0} | all-to-all | bytes 2621440 | tf_op jit(solution)/shard_map/all_to_all | solution.py:560
  121.8 0.0 copy-done.1
  121.8 0.0 copy-done.2
  121.8 0.0 copy-done.6
  121.8 0.0 copy-done.8
  121.8 2.3 %finish.1 = (bf16[2,16,6144]{2,1,0:T(8,128)(2,1)}, f32[24,16,512]{2,1,0:T(8,128)}, f32[24,16,512]{2,1,0:T(8,128)}) custom-call(s32[172]{0:T(256)S(1)} %copy-done.9, f32[8,128]{1,0:T(8,128)S(1)} %copy-done.6, f32[8,128]{1,0:T(8,128)S(1)} %copy-done.8, f32[24,16,512]{2,1,0:T(8,128)S(1)} %bitcast.12, f32[24,16,512]{2,1,0:T(8,128)S(1)} %bitcast.14, ...), custom_call_target="tpu_custom_call" | custom-call | tf_op jit(solution)/shard_map/finish/pallas_call | solution.py:659
  (10 shorter events, 0.0 us)
Async XLA Ops:
  4.6 64.8 %all-to-all-start = ((bf16[32,17,16,128]{3,2,1,0:T(8,128)(2,1)}), bf16[32,17,16,128]{3,2,1,0:T(8,128)(2,1)}, u32[]{:S(2)}, u32[]{:S(2)}) async-start(bf16[32,17,16,128]{3,2,1,0:T(8,128)(2,1)} %get-tuple-element.18.__), calls=%async_computation | async-start | bytes 4456448 | tf_op jit(solution)/shard_map/all_to_all | solution.py:560
  16.2 1.6 %copy-start.10 = (bf16[1,2,2,512,512]{4,3,2,1,0:T(8,128)(2,1)S(1)}, bf16[1,2,2,512,512]{4,3,2,1,0:T(8,128)(2,1)}, u32[]{:S(2)}) copy-start(bf16[1,2,2,512,512]{4,3,2,1,0:T(8,128)(2,1)} %param.11) | copy-start | bytes 6291460
  17.8 7.6 %copy-start = (bf16[32,17,16,128]{3,2,1,0:T(8,128)(2,1)S(1)}, bf16[32,17,16,128]{3,2,1,0:T(8,128)(2,1)}, u32[]{:S(2)}) copy-start(bf16[32,17,16,128]{3,2,1,0:T(8,128)(2,1)} %get-tuple-element.18.__) | copy-start | bytes 6684676
  17.8 7.6 %copy-start.4 = (bf16[2,16,6144]{2,1,0:T(8,128)(2,1)S(1)}, bf16[2,16,6144]{2,1,0:T(8,128)(2,1)}, u32[]{:S(2)}) copy-start(bf16[2,16,6144]{2,1,0:T(8,128)(2,1)} %grads_hbm.3) | copy-start | bytes 1179652
  25.4 1.4 %copy-start.3 = (bf16[4,512,512]{2,1,0:T(8,128)(2,1)}, bf16[4,512,512]{2,1,0:T(8,128)(2,1)S(1)}, u32[]{:S(2)}) copy-start(bf16[4,512,512]{2,1,0:T(8,128)(2,1)S(1)} %get-tuple-element.17._) | copy-start | bytes 6291460
  25.4 1.6 %copy-start.11 = (f32[4,512,128]{2,1,0:T(8,128)}, f32[4,512,128]{2,1,0:T(8,128)S(1)}, u32[]{:S(2)}) copy-start(f32[4,512,128]{2,1,0:T(8,128)S(1)} %get-tuple-element.20) | copy-start | bytes 3145732
  27.0 1.2 collective-permute-start
  28.2 3.6 %collective-permute-start.1 = (f32[8,128]{1,0:T(8,128)S(1)}, f32[8,128]{1,0:T(8,128)S(1)}, u32[]{:S(2)}, u32[]{:S(2)}) collective-permute-start(f32[8,128]{1,0:T(8,128)S(1)} %add.24), channel_id=1, source_target_pairs={{0,2},{1,3},{2,0},{3,1},{4,6},{5,7},{6,4},{7,5},{8,10},{9,11},{10,... | collective-permute-start | bytes 12296 | tf_op jit(solution)/shard_map/ppermute | solution.py:534
  31.8 3.6 %collective-permute-start.2 = (f32[8,128]{1,0:T(8,128)S(1)}, f32[8,128]{1,0:T(8,128)S(1)}, u32[]{:S(2)}, u32[]{:S(2)}) collective-permute-start(f32[8,128]{1,0:T(8,128)S(1)} %add.25), channel_id=1, source_target_pairs={{0,6},{1,7},{2,4},{3,5},{4,2},{5,3},{6,0},{7,1},{8,14},{9,15},{10,... | collective-permute-start | bytes 12296 | tf_op jit(solution)/shard_map/ppermute | solution.py:534
  35.4 3.6 %collective-permute-start.3 = (f32[8,128]{1,0:T(8,128)S(1)}, f32[8,128]{1,0:T(8,128)S(1)}, u32[]{:S(2)}, u32[]{:S(2)}) collective-permute-start(f32[8,128]{1,0:T(8,128)S(1)} %add.26), channel_id=1, source_target_pairs={{0,8},{8,0},{16,24},{24,16},{32,40},{40,32},{48,56},{56,48},{64,72... | collective-permute-start | bytes 12296 | tf_op jit(solution)/shard_map/ppermute | solution.py:534
  39.0 4.8 %collective-permute-start.4 = (f32[8,128]{1,0:T(8,128)S(1)}, f32[8,128]{1,0:T(8,128)S(1)}, u32[]{:S(2)}, u32[]{:S(2)}) collective-permute-start(f32[8,128]{1,0:T(8,128)S(1)} %add.27), channel_id=1, source_target_pairs={{0,24},{8,16},{16,8},{24,0},{32,56},{40,48},{48,40},{56,32},{64,88... | collective-permute-start | bytes 12296 | tf_op jit(solution)/shard_map/ppermute | solution.py:534
  43.9 22.1 %collective-permute-start.8 = (f32[8,128]{1,0:T(8,128)S(1)}, f32[8,128]{1,0:T(8,128)S(1)}, u32[]{:S(2)}, u32[]{:S(2)}) collective-permute-start(f32[8,128]{1,0:T(8,128)S(1)} %add.28), channel_id=1, source_target_pairs={{96,0},{225,1},{98,2},{227,3},{100,4},{229,5},{102,6},{231,7},{104... | collective-permute-start | bytes 12296 | tf_op jit(solution)/shard_map/ppermute | solution.py:554
  48.6 17.3 %collective-permute-start.7 = (f32[8,128]{1,0:T(8,128)S(1)}, f32[8,128]{1,0:T(8,128)S(1)}, u32[]{:S(2)}, u32[]{:S(2)}) collective-permute-start(f32[8,128]{1,0:T(8,128)S(1)} %add.28), channel_id=1, source_target_pairs={{64,0},{193,1},{66,2},{195,3},{68,4},{197,5},{70,6},{199,7},{72,8}... | collective-permute-start | bytes 12296 | tf_op jit(solution)/shard_map/ppermute | solution.py:554
  50.1 16.1 %collective-permute-start.6 = (f32[8,128]{1,0:T(8,128)S(1)}, f32[8,128]{1,0:T(8,128)S(1)}, u32[]{:S(2)}, u32[]{:S(2)}) collective-permute-start(f32[8,128]{1,0:T(8,128)S(1)} %add.28), channel_id=1, source_target_pairs={{32,0},{161,1},{34,2},{163,3},{36,4},{165,5},{38,6},{167,7},{40,8}... | collective-permute-start | bytes 12296 | tf_op jit(solution)/shard_map/ppermute | solution.py:554
  50.6 15.6 %collective-permute-start.5 = (f32[8,128]{1,0:T(8,128)S(1)}, f32[8,128]{1,0:T(8,128)S(1)}, u32[]{:S(2)}, u32[]{:S(2)}) collective-permute-start(f32[8,128]{1,0:T(8,128)S(1)} %add.28), channel_id=1, source_target_pairs={{0,0},{129,1},{2,2},{131,3},{4,4},{133,5},{6,6},{135,7},{8,8},{137... | collective-permute-start | bytes 12296 | tf_op jit(solution)/shard_map/ppermute | solution.py:554
  66.2 3.2 %copy-start.5 = (f32[8,128]{1,0:T(8,128)}, f32[8,128]{1,0:T(8,128)S(1)}, u32[]{:S(2)}) copy-start(f32[8,128]{1,0:T(8,128)S(1)} %add_add_fusion.half_ref) | copy-start | bytes 12292
  66.2 2.7 %collective-permute-start.9 = (f32[8,128]{1,0:T(8,128)S(1)}, f32[8,128]{1,0:T(8,128)S(1)}, u32[]{:S(2)}, u32[]{:S(2)}) collective-permute-start(f32[8,128]{1,0:T(8,128)S(1)} %add_add_fusion.half_ref), channel_id=1, source_target_pairs={{0,1},{1,0},{2,3},{3,2},{4,5},{5,4},{6,7},{7,6},{8,9},{9,8},{10,11... | collective-permute-start | bytes 12296 | tf_op jit(solution)/shard_map/ppermute | solution.py:534
  68.9 0.6 copy-start.7
  76.3 45.4 %copy-start.1 = (f32[1,24,16,512]{3,2,1,0:T(8,128)S(1)}, f32[1,24,16,512]{3,2,1,0:T(8,128)}, u32[]{:S(2)}) copy-start(f32[1,24,16,512]{3,2,1,0:T(8,128)} %param.8) | copy-start | bytes 2359300
  76.3 45.4 %copy-start.2 = (f32[1,24,16,512]{3,2,1,0:T(8,128)S(1)}, f32[1,24,16,512]{3,2,1,0:T(8,128)}, u32[]{:S(2)}) copy-start(f32[1,24,16,512]{3,2,1,0:T(8,128)} %param.9) | copy-start | bytes 2359300
  76.4 45.4 %copy-start.6 = (f32[8,128]{1,0:T(8,128)S(1)}, f32[8,128]{1,0:T(8,128)}, u32[]{:S(2)}) copy-start(f32[8,128]{1,0:T(8,128)} %copy-done.5) | copy-start | bytes 12292
  76.4 45.4 %copy-start.8 = (f32[8,128]{1,0:T(8,128)S(1)}, f32[8,128]{1,0:T(8,128)}, u32[]{:S(2)}) copy-start(f32[8,128]{1,0:T(8,128)} %copy-done.7) | copy-start | bytes 12292
  76.4 45.4 %copy-start.9 = (s32[172]{0:T(256)S(1)}, s32[172]{0:T(256)}, u32[]{:S(2)}) copy-start(s32[172]{0:T(256)} %get-tuple-element.16.plan_ref) | copy-start | bytes 2068

commit v6 on v5

--- a/solution.py
+++ b/solution.py
@@ -28,6 +28,8 @@
 
 
 LANES = 128
+ROWS = 16
+EXTRA = 8
 HBM = pl.BlockSpec(memory_space=pltpu.HBM)
 
 
@@ -45,15 +47,20 @@
     return lax.broadcasted_iota(jnp.int32, shape, len(shape) - 1)
 
 
+def span(tile):
+    if isinstance(tile, int):
+        return pl.ds(tile * ROWS, ROWS)
+    return pl.ds(pl.multiple_of(tile * ROWS, ROWS), ROWS)
+
+
 def store_piece(ref, place, first, piece):
     for tile in range(piece.shape[-1] // LANES):
-        ref[place, first + tile] = piece[:, tile * LANES : (tile + 1) * LANES]
+        ref[place, span(first + tile)] = piece[:, tile * LANES : (tile + 1) * LANES]
 
 
 def whole_block(ref, first, tiles):
-    devices, _, rows, _ = ref.shape
     return jnp.concatenate(
-        [ref[:, first + tile].reshape(devices * rows, LANES) for tile in range(tiles)], axis=1
+        [ref[:, span(first + tile)].reshape(-1, LANES) for tile in range(tiles)], axis=1
     )
 
 
@@ -152,7 +159,7 @@
     cols = width // order
     blocks = rows_dev * cols
     tiles = order // LANES
-    devices, extra = out_ref.shape[0], out_ref.shape[1] - 1
+    devices, extra = out_ref.shape[0], pl.ds(out_ref.shape[1] - EXTRA, EXTRA)
     parts = 4
     grads_in = pltpu.make_async_copy(grads_hbm, grads_ref, in_sems.at[0])
     grads_in.start()
@@ -173,9 +180,9 @@
     plan.fill(owner_ref, me)
     role_ref[0] = plan.get("role")
     role_ref[1] = plan.get("own")
-    tile_row = sublanes((rows, LANES))
+    tile_row = sublanes((EXTRA, LANES))
     for owner in range(devices):
-        out_ref[owner, extra] = jnp.zeros((rows, LANES), jnp.bfloat16)
+        out_ref[owner, extra] = jnp.zeros((EXTRA, LANES), jnp.bfloat16)
     grads_in.wait()
     for k in range(blocks):
         owner, slot = plan.get("owner", k), plan.get("slot", k)
@@ -185,7 +192,10 @@
         store_piece(out_ref, plan.spare_of(k), k % plan.share() * tiles, piece)
     outs = []
     for turn, (first, count) in enumerate(
-        ((0, slots * tiles), (slots * tiles, out_ref.shape[1] - slots * tiles))
+        (
+            (0, slots * tiles * rows),
+            (slots * tiles * rows, out_ref.shape[1] - slots * tiles * rows),
+        )
     ):
         where = (slice(None), pl.ds(first, count))
         outs.append(
@@ -260,8 +270,8 @@
         new_ref[where] = second
         step = clipped / (jnp.sqrt(second) + 1e-08)
         sums = jnp.where(lane == k, jnp.sum(step * step, keepdims=True), sums)
-    tile_row = sublanes((rows, LANES))
-    tile = jnp.zeros((rows, LANES), jnp.float32)
+    tile_row = sublanes((EXTRA, LANES))
+    tile = jnp.zeros((EXTRA, LANES), jnp.float32)
     for place, term in enumerate(thirds(sums)):
         tile = jnp.where(tile_row == place, term, tile)
     return tile
@@ -294,20 +304,21 @@
     in_sems,
     out_sems,
 ):
-    devices, arrived_tiles, rows, lane_count = arrived_ref.shape
+    devices, arrived_rows, lane_count = arrived_ref.shape
     order = seed_ref.shape[-1]
     tiles = order // lane_count
+    piece = tiles * ROWS
     role, load = role_ref[0], role_ref[1]
     scale = scale_of(entries, half_ref, other_ref)
     factor = 0.05 * scale * scale
 
     sources = [(grads_hbm, grads_ref, ()), (second_hbm, second_ref, ())]
-    sources.append((arrived_hbm, arrived_ref, (slice(None), pl.ds(0, tiles))))
-    mixed_at = (slice(None), pl.ds(slots * tiles, arrived_tiles - slots * tiles))
+    sources.append((arrived_hbm, arrived_ref, (slice(None), pl.ds(0, piece))))
+    mixed_at = (slice(None), pl.ds(slots * piece, arrived_rows - slots * piece))
     sources.append((arrived_hbm, arrived_ref, mixed_at))
     for slot in range(slots):
         if slot > 0:
-            sources.append((arrived_hbm, arrived_ref, (slice(None), pl.ds(slot * tiles, tiles))))
+            sources.append((arrived_hbm, arrived_ref, (slice(None), pl.ds(slot * piece, piece))))
         for source, target in ((fifth_hbm, fifth_ref), (ratio_hbm, ratio_ref), (seed_hbm, seed_ref)):
             sources.append((source, target, (slice(None), slot)))
     copies = [
@@ -324,8 +335,8 @@
     gradient_in = [copies[2], copies[7]]
     root_in = [copies[4:7], copies[8:11]]
     shares = [
-        (slice(None), pl.ds(0, tiles)),
-        (slice(None), pl.ds(tiles, out_ref.shape[1] - tiles)),
+        (slice(None), pl.ds(0, piece)),
+        (slice(None), pl.ds(piece, out_ref.shape[1] - piece)),
     ]
     outs = [
         pltpu.make_async_copy(out_ref.at[where], out_hbm.at[where], out_sems.at[place])
@@ -343,20 +354,20 @@
 
     def put_sums(norms):
         tile = adam
-        tile_row, lane = sublanes((rows, lane_count)), lanes((rows, lane_count))
+        tile_row, lane = sublanes((EXTRA, lane_count)), lanes((EXTRA, lane_count))
         for slot, norm in enumerate(norms):
             for place, term in enumerate(thirds(norm)):
                 tile = jnp.where((tile_row == 3 + place) & (lane == slot), term, tile)
-        out_ref[:, out_ref.shape[1] - 1] = jnp.broadcast_to(
-            tile.astype(jnp.bfloat16)[None], (devices, rows, lane_count)
+        out_ref[:, pl.ds(out_ref.shape[1] - EXTRA, EXTRA)] = jnp.broadcast_to(
+            tile.astype(jnp.bfloat16)[None], (devices, EXTRA, lane_count)
         )
 
     def put(first, value):
         value = value.astype(jnp.bfloat16)
         for tile in range(value.shape[1] // lane_count):
-            out_ref[:, first + tile] = value[
+            out_ref[:, span(first + tile)] = value[
                 :, tile * lane_count : (tile + 1) * lane_count
-            ].reshape(devices, rows, lane_count)
+            ].reshape(devices, ROWS, lane_count)
 
     def gradient(slot):
         return whole_block(arrived_ref, slot * tiles, tiles)
@@ -380,11 +391,13 @@
         mixed = mixed.astype(jnp.float32)
         row, col = sublanes((order, order)), lanes((order, order))
         diagonal = []
-        tile_row = sublanes((rows, lane_count))
+        tile_row = sublanes((EXTRA, lane_count))
         for tile in range(tiles):
-            total = jnp.zeros((rows, lane_count), jnp.float32)
+            total = jnp.zeros((EXTRA, lane_count), jnp.float32)
             for source in range(tile * devices // tiles, (tile + 1) * devices // tiles):
-                total = total + arrived_ref[source, arrived_tiles - 1].astype(jnp.float32)
+                total = total + arrived_ref[source, pl.ds(arrived_rows - EXTRA, EXTRA)].astype(
+                    jnp.float32
+                )
             diagonal.append(
                 jnp.sum(jnp.where(tile_row == slot, total, 0.0), axis=0, keepdims=True)
             )
@@ -490,14 +503,14 @@
     blocks, _, order = left_ref.shape
     cols = width // order
     tiles = order // LANES
-    devices, extra = back_ref.shape[0], back_ref.shape[1] - 1
+    devices, extra = back_ref.shape[0], pl.ds(back_ref.shape[1] - EXTRA, EXTRA)
     plan = Plan(plan_ref, blocks, devices)
     factor = scale_of(entries, half_ref, other_ref)
     factor = 0.05 * factor * factor
-    total = jnp.zeros((rows, LANES), jnp.float32)
+    total = jnp.zeros((EXTRA, LANES), jnp.float32)
     for source in range(devices):
         total = total + back_ref[source, extra].astype(jnp.float32)
-    tile_row, lane = sublanes((rows, LANES)), lanes((rows, LANES))
+    tile_row, lane = sublanes((EXTRA, LANES)), lanes((EXTRA, LANES))
     norms = jnp.sqrt(jnp.sum(jnp.where(tile_row < 3, total, 0.0), axis=0, keepdims=True))
     for k in range(blocks):
         owner, slot = plan.get("owner", k), plan.get("slot", k)
@@ -515,16 +528,16 @@
             part = slice(tile * LANES, (tile + 1) * LANES)
             first = (k % cols) * order + tile * LANES
             out_ref[k // cols, :, first : first + LANES] = (
-                back_ref[owner, slot * tiles + tile].astype(jnp.float32) * norm
+                back_ref[owner, span(slot * tiles + tile)].astype(jnp.float32) * norm
             ).astype(jnp.bfloat16)
             if tile == 0:
-                gram = back_ref[jnp.where(slot == 0, owner, helper), 2 * tiles]
+                gram = back_ref[jnp.where(slot == 0, owner, helper), span(2 * tiles)]
             else:
-                gram = back_ref[spare, k % plan.share() * (tiles - 1) + tile - 1]
+                gram = back_ref[spare, span(k % plan.share() * (tiles - 1) + tile - 1)]
             new_left_ref[k, :, part] = BETA * left_ref[k, :, part] + factor * gram.astype(
                 jnp.float32
             )
-            gram = back_ref[helper, right_from + tile]
+            gram = back_ref[helper, span(right_from + tile)]
             new_right_ref[k, :, part] = BETA * right_ref[k, :, part] + factor * gram.astype(
                 jnp.float32
             )
@@ -579,7 +592,7 @@
     owner_of = owners.reshape(blocks)
     left_old, right_old, seeds = left_stats[0], right_stats[0], roots[0]
 
-    sent_shape = (devices, 2 * slots * tiles + 1, rows, LANES)
+    sent_shape = (devices, 2 * slots * tiles * rows + EXTRA, LANES)
     sent, plan, role = pl.pallas_call(
         functools.partial(pack_kernel, slots),
         out_shape=[
@@ -625,7 +638,7 @@
     square = ring_sum(square + swap(square, "zero", 1), "zero", 2)
     square_halves = blk_halves(square, "zero", 1)
 
-    returned_shape = (devices, 2 * tiles + 2, rows, LANES)
+    returned_shape = (devices, (2 * tiles + 1) * rows + EXTRA, LANES)
     fifth = fifth.reshape(2, slots, order, order)
     ratio = ratio.reshape(2, slots, order, LANES)
     new_roots, returned, new_second = pl.pallas_call(

time: 124 us -> 122 us (0.984)
  blocking collectives: 45.4 us -> 43.9 us
  waiting for transfers between devices: 26.6 us -> 25.3 us
    all_to_all x1, blocking collectives: 45.4 us -> 43.9 us  [exchange(): lax.all_to_all(values, 'blk', split_axis=0, concat_axis=0, tiled=True)]
    ppermute x4, waiting for transfers between devices: 14.9 us -> 13.5 us  [blk_halves(): parts.append(lax.ppermute(values, ('blk', 'zero'), pairs))]
where the time goes in v6:
time: 122 us; the launch traced here: 121 us
  blocking collectives  43.9 us (36%)
  starting transfers between devices  27.2 us (22%)
  waiting for transfers between devices  25.3 us (21%)
  Pallas kernels  21 us (17%)
  local copies, waits for them, and re-layouts  3.17 us (3%)
    all_to_all x1, blocking collectives, exchange(): lax.all_to_all(values, 'blk', split_axis=0, concat_axis=0, tiled=True)  43.9 us
    ppermute x4, waiting for transfers between devices, blk_halves(): parts.append(lax.ppermute(values, ('blk', 'zero'), pairs))  13.5 us
    all_to_all x1, starting transfers between devices, exchange(): lax.all_to_all(values, 'blk', split_axis=0, concat_axis=0, tiled=True)  11.6 us
    ppermute x6, waiting for transfers between devices, swap(): lax.ppermute(values, axis, [(i, i ^ bit) for i in range(lax.axis_size(axi...  11.3 us
    ppermute x6, starting transfers between devices, swap(): lax.ppermute(values, axis, [(i, i ^ bit) for i in range(lax.axis_size(axi...  8.22 us
    pallas_call x1, Pallas kernels, local(): pl.pallas_call(fifth_kernel, out_shape=[jax.ShapeDtypeStruct((2 * slots,...  7.59 us
    ppermute x4, starting transfers between devices, blk_halves(): parts.append(lax.ppermute(values, ('blk', 'zero'), pairs))  7.36 us
    pallas_call x1, Pallas kernels, local(): pl.pallas_call(functools.partial(owner_kernel, slots, entries), out_shape...  6.84 us
  transfers between devices with their start and end apart: 11, of which 9 were waited for; matrix products, arithmetic and copies ran while one was open for 0% of the time, Pallas kernels for 6%

profile of v6, /device:TPU:4, one launch (start us, length us, event | category | flops | bytes accessed | tf_op | source)
XLA Modules:
  0.0 121.4 jit_solution(17568286507524747628)
XLA Ops:
  0.6 4.0 %pack.1 = (bf16[32,264,128]{2,1,0:T(8,128)(2,1)}, s32[172]{0:T(256)}, s32[2]{0:T(128)}) custom-call(s32[1]{0:T(128)} %bitcast.me_ref, s32[24]{0:T(128)} %bitcast.19, bf16[2,16,6144]{2,1,0:T(8,128)(2,1)} %grads_hbm.3, f32[24,16,512]{2,1,0:T(8,128)} %bitcast.11, f32[24,16,512]{2,1,0:T(8,128)} %bitcast.13), custom_call_target="tpu_custom_call" | custom-call | tf_op jit(solution)/shard_map/pack/pallas_call | solution.py:596
  4.6 11.6 %all-to-all-start = ((bf16[32,264,128]{2,1,0:T(8,128)(2,1)}), bf16[32,264,128]{2,1,0:T(8,128)(2,1)}, u32[]{:S(2)}, u32[]{:S(2)}) async-start(bf16[32,264,128]{2,1,0:T(8,128)(2,1)} %get-tuple-element.18.__), calls=%async_computation | async-start | bytes 4325376 | tf_op jit(solution)/shard_map/all_to_all | solution.py:573
  16.2 0.0 copy-start.10
  16.2 1.6 %copy-done.10 = bf16[1,2,2,512,512]{4,3,2,1,0:T(8,128)(2,1)S(1)} copy-done((bf16[1,2,2,512,512]{4,3,2,1,0:T(8,128)(2,1)S(1)}, bf16[1,2,2,512,512]{4,3,2,1,0:T(8,128)(2,1)}, u32[]{:S(2)}) %copy-start.10) | copy-done | bytes 2097176
  17.8 7.6 %fifth.1 = (bf16[4,512,512]{2,1,0:T(8,128)(2,1)S(1)}, f32[4,512,128]{2,1,0:T(8,128)S(1)}) custom-call(bf16[4,512,512]{2,1,0:T(8,128)(2,1)S(1)} %bitcast.17), custom_call_target="tpu_custom_call" | custom-call | flops 6442450944 | bytes 6291456 | tf_op jit(solution)/shard_map/fifth/pallas_call | solution.py:618
  25.4 0.0 copy-start.3
  25.4 0.0 copy-start.11
  25.5 0.0 copy-done
  25.5 0.0 copy-done.4
  25.5 0.1 square.1
  25.6 1.2 copy-done.3
  26.8 0.3 copy-done.11
  27.1 0.0 collective-permute-start
  27.1 1.2 collective-permute-done
  28.3 1.2 collective-permute-start.1
  29.5 2.4 %collective-permute-done.1 = f32[8,128]{1,0:T(8,128)S(1)} collective-permute-done((f32[8,128]{1,0:T(8,128)S(1)}, f32[8,128]{1,0:T(8,128)S(1)}, u32[]{:S(2)}, u32[]{:S(2)}) %collective-permute-start.1) | collective-permute-done | bytes 4128 | tf_op jit(solution)/shard_map/ppermute | solution.py:547
  31.9 0.5 collective-permute-start.2
  32.4 3.1 %collective-permute-done.2 = f32[8,128]{1,0:T(8,128)S(1)} collective-permute-done((f32[8,128]{1,0:T(8,128)S(1)}, f32[8,128]{1,0:T(8,128)S(1)}, u32[]{:S(2)}, u32[]{:S(2)}) %collective-permute-start.2) | collective-permute-done | bytes 4128 | tf_op jit(solution)/shard_map/ppermute | solution.py:547
  35.5 1.7 %collective-permute-start.3 = (f32[8,128]{1,0:T(8,128)S(1)}, f32[8,128]{1,0:T(8,128)S(1)}, u32[]{:S(2)}, u32[]{:S(2)}) collective-permute-start(f32[8,128]{1,0:T(8,128)S(1)} %add.26), channel_id=1, source_target_pairs={{0,8},{8,0},{16,24},{24,16},{32,40},{40,32},{48,56},{56,48},{64,72... | collective-permute-start | bytes 12296 | tf_op jit(solution)/shard_map/ppermute | solution.py:547
  37.2 1.9 %collective-permute-done.3 = f32[8,128]{1,0:T(8,128)S(1)} collective-permute-done((f32[8,128]{1,0:T(8,128)S(1)}, f32[8,128]{1,0:T(8,128)S(1)}, u32[]{:S(2)}, u32[]{:S(2)}) %collective-permute-start.3) | collective-permute-done | bytes 4128 | tf_op jit(solution)/shard_map/ppermute | solution.py:547
  39.1 2.9 %collective-permute-start.4 = (f32[8,128]{1,0:T(8,128)S(1)}, f32[8,128]{1,0:T(8,128)S(1)}, u32[]{:S(2)}, u32[]{:S(2)}) collective-permute-start(f32[8,128]{1,0:T(8,128)S(1)} %add.27), channel_id=1, source_target_pairs={{0,24},{8,16},{16,8},{24,0},{32,56},{40,48},{48,40},{56,32},{64,88... | collective-permute-start | bytes 12296 | tf_op jit(solution)/shard_map/ppermute | solution.py:547
  42.0 1.9 %collective-permute-done.4 = f32[8,128]{1,0:T(8,128)S(1)} collective-permute-done((f32[8,128]{1,0:T(8,128)S(1)}, f32[8,128]{1,0:T(8,128)S(1)}, u32[]{:S(2)}, u32[]{:S(2)}) %collective-permute-start.4) | collective-permute-done | bytes 4128 | tf_op jit(solution)/shard_map/ppermute | solution.py:547
  44.0 4.7 %collective-permute-start.8 = (f32[8,128]{1,0:T(8,128)S(1)}, f32[8,128]{1,0:T(8,128)S(1)}, u32[]{:S(2)}, u32[]{:S(2)}) collective-permute-start(f32[8,128]{1,0:T(8,128)S(1)} %add.28), channel_id=1, source_target_pairs={{96,0},{225,1},{98,2},{227,3},{100,4},{229,5},{102,6},{231,7},{104... | collective-permute-start | bytes 12296 | tf_op jit(solution)/shard_map/ppermute | solution.py:567
  48.7 1.5 %collective-permute-start.7 = (f32[8,128]{1,0:T(8,128)S(1)}, f32[8,128]{1,0:T(8,128)S(1)}, u32[]{:S(2)}, u32[]{:S(2)}) collective-permute-start(f32[8,128]{1,0:T(8,128)S(1)} %add.28), channel_id=1, source_target_pairs={{64,0},{193,1},{66,2},{195,3},{68,4},{197,5},{70,6},{199,7},{72,8}... | collective-permute-start | bytes 12296 | tf_op jit(solution)/shard_map/ppermute | solution.py:567
  50.2 0.5 collective-permute-start.6
  50.7 0.6 collective-permute-start.5
  51.4 13.2 %collective-permute-done.8 = f32[8,128]{1,0:T(8,128)S(1)} collective-permute-done((f32[8,128]{1,0:T(8,128)S(1)}, f32[8,128]{1,0:T(8,128)S(1)}, u32[]{:S(2)}, u32[]{:S(2)}) %collective-permute-start.8) | collective-permute-done | bytes 4128 | tf_op jit(solution)/shard_map/ppermute | solution.py:567
  64.6 0.0 collective-permute-done.7
  64.6 0.3 collective-permute-done.6
  64.8 0.0 collective-permute-done.5
  64.8 0.0 copy-start.5
  64.9 1.8 %collective-permute-start.9 = (f32[8,128]{1,0:T(8,128)S(1)}, f32[8,128]{1,0:T(8,128)S(1)}, u32[]{:S(2)}, u32[]{:S(2)}) collective-permute-start(f32[8,128]{1,0:T(8,128)S(1)} %add_add_fusion.half_ref), channel_id=1, source_target_pairs={{0,1},{1,0},{2,3},{3,2},{4,5},{5,4},{6,7},{7,6},{8,9},{9,8},{10,11... | collective-permute-start | bytes 12296 | tf_op jit(solution)/shard_map/ppermute | solution.py:547
  66.7 0.8 collective-permute-done.9.other_ref
  67.5 0.5 all-to-all-done.arrived_hbm
  68.0 0.0 copy-done.5
  68.0 0.1 copy-done.7
  68.1 6.8 %owner.1 = (bf16[2,2,512,512]{3,2,1,0:T(8,128)(2,1)}, bf16[32,152,128]{2,1,0:T(8,128)(2,1)}, f32[2,16,6144]{2,1,0:T(8,128)}) custom-call(s32[2]{0:T(128)} %get-tuple-element.19.role_ref, f32[8,128]{1,0:T(8,128)} %copy-done.5, f32[8,128]{1,0:T(8,128)} %copy-done.7, bf16[2,16,6144]{2,1,0:T(8,128)(2,1)} %grads_hbm.3, f32[2,16,6144]{2,1,0:T(8,128)} %second_hbm.1, ...), custom_call_target="tpu_custom_call" | custom-call | flops 4294967296 | bytes 12582912 | tf_op jit(solution)/shard_map/owner/pallas_call | solution.py:644
  75.0 0.0 copy-start.1
  75.0 0.0 copy-start.2
  75.0 0.0 copy-start.6
  75.0 0.0 copy-start.8
  75.0 0.0 copy-start.9
  75.0 43.9 %all_to_all.10.back_ref = bf16[32,152,128]{2,1,0:T(8,128)(2,1)S(1)} all-to-all(bf16[32,152,128]{2,1,0:T(8,128)(2,1)} %get-tuple-element.21), channel_id=1, replica_groups=mesh['blk'=32,'zero'=8] {'blk'}, dimensions={0} | all-to-all | bytes 2490368 | tf_op jit(solution)/shard_map/all_to_all | solution.py:573
  118.9 0.0 copy-done.1
  118.9 0.0 copy-done.2
  118.9 0.0 copy-done.6
  118.9 0.0 copy-done.8
  118.9 2.5 %finish.1 = (bf16[2,16,6144]{2,1,0:T(8,128)(2,1)}, f32[24,16,512]{2,1,0:T(8,128)}, f32[24,16,512]{2,1,0:T(8,128)}) custom-call(s32[172]{0:T(256)S(1)} %copy-done.9, f32[8,128]{1,0:T(8,128)S(1)} %copy-done.6, f32[8,128]{1,0:T(8,128)S(1)} %copy-done.8, f32[24,16,512]{2,1,0:T(8,128)S(1)} %bitcast.12, f32[24,16,512]{2,1,0:T(8,128)S(1)} %bitcast.14, ...), custom_call_target="tpu_custom_call" | custom-call | tf_op jit(solution)/shard_map/finish/pallas_call | solution.py:672
  (10 shorter events, 0.0 us)
Async XLA Ops:
  4.6 63.4 %all-to-all-start = ((bf16[32,264,128]{2,1,0:T(8,128)(2,1)}), bf16[32,264,128]{2,1,0:T(8,128)(2,1)}, u32[]{:S(2)}, u32[]{:S(2)}) async-start(bf16[32,264,128]{2,1,0:T(8,128)(2,1)} %get-tuple-element.18.__), calls=%async_computation | async-start | bytes 4325376 | tf_op jit(solution)/shard_map/all_to_all | solution.py:573
  16.2 1.6 %copy-start.10 = (bf16[1,2,2,512,512]{4,3,2,1,0:T(8,128)(2,1)S(1)}, bf16[1,2,2,512,512]{4,3,2,1,0:T(8,128)(2,1)}, u32[]{:S(2)}) copy-start(bf16[1,2,2,512,512]{4,3,2,1,0:T(8,128)(2,1)} %param.11) | copy-start | bytes 6291460
  17.8 7.6 %copy-start = (bf16[32,264,128]{2,1,0:T(8,128)(2,1)S(1)}, bf16[32,264,128]{2,1,0:T(8,128)(2,1)}, u32[]{:S(2)}) copy-start(bf16[32,264,128]{2,1,0:T(8,128)(2,1)} %get-tuple-element.18.__) | copy-start | bytes 6488068
  17.8 7.6 %copy-start.4 = (bf16[2,16,6144]{2,1,0:T(8,128)(2,1)S(1)}, bf16[2,16,6144]{2,1,0:T(8,128)(2,1)}, u32[]{:S(2)}) copy-start(bf16[2,16,6144]{2,1,0:T(8,128)(2,1)} %grads_hbm.3) | copy-start | bytes 1179652
  25.4 1.4 %copy-start.3 = (bf16[4,512,512]{2,1,0:T(8,128)(2,1)}, bf16[4,512,512]{2,1,0:T(8,128)(2,1)S(1)}, u32[]{:S(2)}) copy-start(bf16[4,512,512]{2,1,0:T(8,128)(2,1)S(1)} %get-tuple-element.17._) | copy-start | bytes 6291460
  25.4 1.7 %copy-start.11 = (f32[4,512,128]{2,1,0:T(8,128)}, f32[4,512,128]{2,1,0:T(8,128)S(1)}, u32[]{:S(2)}) copy-start(f32[4,512,128]{2,1,0:T(8,128)S(1)} %get-tuple-element.20) | copy-start | bytes 3145732
  27.1 1.2 collective-permute-start
  28.3 3.6 %collective-permute-start.1 = (f32[8,128]{1,0:T(8,128)S(1)}, f32[8,128]{1,0:T(8,128)S(1)}, u32[]{:S(2)}, u32[]{:S(2)}) collective-permute-start(f32[8,128]{1,0:T(8,128)S(1)} %add.24), channel_id=1, source_target_pairs={{0,2},{1,3},{2,0},{3,1},{4,6},{5,7},{6,4},{7,5},{8,10},{9,11},{10,... | collective-permute-start | bytes 12296 | tf_op jit(solution)/shard_map/ppermute | solution.py:547
  31.9 3.6 %collective-permute-start.2 = (f32[8,128]{1,0:T(8,128)S(1)}, f32[8,128]{1,0:T(8,128)S(1)}, u32[]{:S(2)}, u32[]{:S(2)}) collective-permute-start(f32[8,128]{1,0:T(8,128)S(1)} %add.25), channel_id=1, source_target_pairs={{0,6},{1,7},{2,4},{3,5},{4,2},{5,3},{6,0},{7,1},{8,14},{9,15},{10,... | collective-permute-start | bytes 12296 | tf_op jit(solution)/shard_map/ppermute | solution.py:547
  35.5 3.6 %collective-permute-start.3 = (f32[8,128]{1,0:T(8,128)S(1)}, f32[8,128]{1,0:T(8,128)S(1)}, u32[]{:S(2)}, u32[]{:S(2)}) collective-permute-start(f32[8,128]{1,0:T(8,128)S(1)} %add.26), channel_id=1, source_target_pairs={{0,8},{8,0},{16,24},{24,16},{32,40},{40,32},{48,56},{56,48},{64,72... | collective-permute-start | bytes 12296 | tf_op jit(solution)/shard_map/ppermute | solution.py:547
  39.1 4.9 %collective-permute-start.4 = (f32[8,128]{1,0:T(8,128)S(1)}, f32[8,128]{1,0:T(8,128)S(1)}, u32[]{:S(2)}, u32[]{:S(2)}) collective-permute-start(f32[8,128]{1,0:T(8,128)S(1)} %add.27), channel_id=1, source_target_pairs={{0,24},{8,16},{16,8},{24,0},{32,56},{40,48},{48,40},{56,32},{64,88... | collective-permute-start | bytes 12296 | tf_op jit(solution)/shard_map/ppermute | solution.py:547
  44.0 20.6 %collective-permute-start.8 = (f32[8,128]{1,0:T(8,128)S(1)}, f32[8,128]{1,0:T(8,128)S(1)}, u32[]{:S(2)}, u32[]{:S(2)}) collective-permute-start(f32[8,128]{1,0:T(8,128)S(1)} %add.28), channel_id=1, source_target_pairs={{96,0},{225,1},{98,2},{227,3},{100,4},{229,5},{102,6},{231,7},{104... | collective-permute-start | bytes 12296 | tf_op jit(solution)/shard_map/ppermute | solution.py:567
  48.7 15.9 %collective-permute-start.7 = (f32[8,128]{1,0:T(8,128)S(1)}, f32[8,128]{1,0:T(8,128)S(1)}, u32[]{:S(2)}, u32[]{:S(2)}) collective-permute-start(f32[8,128]{1,0:T(8,128)S(1)} %add.28), channel_id=1, source_target_pairs={{64,0},{193,1},{66,2},{195,3},{68,4},{197,5},{70,6},{199,7},{72,8}... | collective-permute-start | bytes 12296 | tf_op jit(solution)/shard_map/ppermute | solution.py:567
  50.2 14.7 %collective-permute-start.6 = (f32[8,128]{1,0:T(8,128)S(1)}, f32[8,128]{1,0:T(8,128)S(1)}, u32[]{:S(2)}, u32[]{:S(2)}) collective-permute-start(f32[8,128]{1,0:T(8,128)S(1)} %add.28), channel_id=1, source_target_pairs={{32,0},{161,1},{34,2},{163,3},{36,4},{165,5},{38,6},{167,7},{40,8}... | collective-permute-start | bytes 12296 | tf_op jit(solution)/shard_map/ppermute | solution.py:567
  50.7 14.1 %collective-permute-start.5 = (f32[8,128]{1,0:T(8,128)S(1)}, f32[8,128]{1,0:T(8,128)S(1)}, u32[]{:S(2)}, u32[]{:S(2)}) collective-permute-start(f32[8,128]{1,0:T(8,128)S(1)} %add.28), channel_id=1, source_target_pairs={{0,0},{129,1},{2,2},{131,3},{4,4},{133,5},{6,6},{135,7},{8,8},{137... | collective-permute-start | bytes 12296 | tf_op jit(solution)/shard_map/ppermute | solution.py:567
  64.8 3.2 %copy-start.5 = (f32[8,128]{1,0:T(8,128)}, f32[8,128]{1,0:T(8,128)S(1)}, u32[]{:S(2)}) copy-start(f32[8,128]{1,0:T(8,128)S(1)} %add_add_fusion.half_ref) | copy-start | bytes 12292
  64.9 2.7 %collective-permute-start.9 = (f32[8,128]{1,0:T(8,128)S(1)}, f32[8,128]{1,0:T(8,128)S(1)}, u32[]{:S(2)}, u32[]{:S(2)}) collective-permute-start(f32[8,128]{1,0:T(8,128)S(1)} %add_add_fusion.half_ref), channel_id=1, source_target_pairs={{0,1},{1,0},{2,3},{3,2},{4,5},{5,4},{6,7},{7,6},{8,9},{9,8},{10,11... | collective-permute-start | bytes 12296 | tf_op jit(solution)/shard_map/ppermute | solution.py:547
  67.5 0.6 copy-start.7
  75.0 43.9 %copy-start.1 = (f32[1,24,16,512]{3,2,1,0:T(8,128)S(1)}, f32[1,24,16,512]{3,2,1,0:T(8,128)}, u32[]{:S(2)}) copy-start(f32[1,24,16,512]{3,2,1,0:T(8,128)} %param.8) | copy-start | bytes 2359300
  75.0 43.9 %copy-start.2 = (f32[1,24,16,512]{3,2,1,0:T(8,128)S(1)}, f32[1,24,16,512]{3,2,1,0:T(8,128)}, u32[]{:S(2)}) copy-start(f32[1,24,16,512]{3,2,1,0:T(8,128)} %param.9) | copy-start | bytes 2359300
  75.0 43.9 %copy-start.6 = (f32[8,128]{1,0:T(8,128)S(1)}, f32[8,128]{1,0:T(8,128)}, u32[]{:S(2)}) copy-start(f32[8,128]{1,0:T(8,128)} %copy-done.5) | copy-start | bytes 12292
  75.0 43.9 %copy-start.8 = (f32[8,128]{1,0:T(8,128)S(1)}, f32[8,128]{1,0:T(8,128)}, u32[]{:S(2)}) copy-start(f32[8,128]{1,0:T(8,128)} %copy-done.7) | copy-start | bytes 12292
  75.0 43.9 %copy-start.9 = (s32[172]{0:T(256)S(1)}, s32[172]{0:T(256)}, u32[]{:S(2)}) copy-start(s32[172]{0:T(256)} %get-tuple-element.16.plan_ref) | copy-start | bytes 2068

commit v7 on v6

--- a/solution.py
+++ b/solution.py
@@ -130,9 +130,6 @@
             helper = self.get("idle", jnp.minimum(count, devices - 1))
             self.put("helper", device, jnp.where(double, helper, device))
             count = count + double.astype(jnp.int32)
-        for k in range(blocks):
-            load = self.get("load", self.get("owner", k))
-            self.put("single", k, (load == 1).astype(jnp.int32))
         self.put("role", 0, role)
         self.put("own", 0, self.get("load", me))
 
@@ -178,8 +175,6 @@
     me = me_ref[0]
     plan = Plan(plan_ref, blocks, devices)
     plan.fill(owner_ref, me)
-    role_ref[0] = plan.get("role")
-    role_ref[1] = plan.get("own")
     tile_row = sublanes((EXTRA, LANES))
     for owner in range(devices):
         out_ref[owner, extra] = jnp.zeros((EXTRA, LANES), jnp.bfloat16)
@@ -222,6 +217,15 @@
             tile_row == slot, diagonal, out_ref[owner, extra].astype(jnp.float32)
         ).astype(jnp.bfloat16)
     outs[1].start()
+    role_ref[0] = plan.get("role")
+    role_ref[1] = plan.get("own")
+    own = [jnp.int32(0)] * slots
+    for k in range(blocks):
+        owner, slot = plan.get("owner", k), plan.get("slot", k)
+        plan.put("single", k, (plan.get("load", owner) == 1).astype(jnp.int32))
+        own = [jnp.where((owner == me) & (slot == i), k, own[i]) for i in range(slots)]
+    for i in range(slots):
+        role_ref[2 + i] = own[i]
     for copy in outs:
         copy.wait()
 
@@ -357,7 +361,7 @@
         tile_row, lane = sublanes((EXTRA, lane_count)), lanes((EXTRA, lane_count))
         for slot, norm in enumerate(norms):
             for place, term in enumerate(thirds(norm)):
-                tile = jnp.where((tile_row == 3 + place) & (lane == slot), term, tile)
+                tile = jnp.where((tile_row == 3 + place) & (lane == role_ref[2 + slot]), term, tile)
         out_ref[:, pl.ds(out_ref.shape[1] - EXTRA, EXTRA)] = jnp.broadcast_to(
             tile.astype(jnp.bfloat16)[None], (devices, EXTRA, lane_count)
         )
@@ -512,17 +516,13 @@
         total = total + back_ref[source, extra].astype(jnp.float32)
     tile_row, lane = sublanes((EXTRA, LANES)), lanes((EXTRA, LANES))
     norms = jnp.sqrt(jnp.sum(jnp.where(tile_row < 3, total, 0.0), axis=0, keepdims=True))
+    inverse = (tile_row >= 3) & (tile_row < 6)
+    norms = norms * jnp.sum(jnp.where(inverse, total, 0.0), axis=0, keepdims=True)
     for k in range(blocks):
         owner, slot = plan.get("owner", k), plan.get("slot", k)
         helper, single = plan.get("helper", owner), plan.get("single", k)
         spare = plan.spare_of(k)
         norm = jnp.sum(jnp.where(lane[:1] == k, norms, 0.0), axis=1, keepdims=True)
-        inverse = jnp.where(
-            (lane == slot) & (tile_row >= 3) & (tile_row < 6),
-            back_ref[owner, extra].astype(jnp.float32),
-            0.0,
-        )
-        norm = norm * jnp.sum(inverse, keepdims=True)
         right_from = jnp.where(single == 1, 1, slot) * tiles
         for tile in range(tiles):
             part = slice(tile * LANES, (tile + 1) * LANES)
@@ -598,7 +598,7 @@
         out_shape=[
             jax.ShapeDtypeStruct(sent_shape, jnp.bfloat16),
             jax.ShapeDtypeStruct((Plan.size(blocks, devices),), jnp.int32),
-            jax.ShapeDtypeStruct((2,), jnp.int32),
+            jax.ShapeDtypeStruct((2 + slots,), jnp.int32),
         ],
         in_specs=[SMEM, SMEM, HBM, HBM, HBM],
         out_specs=[HBM, SMEM, SMEM],

time: 122 us -> 121 us (level)
  blocking collectives: 43.9 us -> 42.6 us
    all_to_all x1, blocking collectives: 43.9 us -> 42.6 us  [exchange(): lax.all_to_all(values, 'blk', split_axis=0, concat_axis=0, tiled=True)]
where the time goes in v7:
time: 121 us; the launch traced here: 120 us
  blocking collectives  42.6 us (35%)
  starting transfers between devices  27.2 us (22%)
  waiting for transfers between devices  25.3 us (21%)
  Pallas kernels  20.6 us (17%)
  local copies, waits for them, and re-layouts  3.17 us (3%)
    all_to_all x1, blocking collectives, exchange(): lax.all_to_all(values, 'blk', split_axis=0, concat_axis=0, tiled=True)  42.6 us
    ppermute x4, waiting for transfers between devices, blk_halves(): parts.append(lax.ppermute(values, ('blk', 'zero'), pairs))  13.5 us
    all_to_all x1, starting transfers between devices, exchange(): lax.all_to_all(values, 'blk', split_axis=0, concat_axis=0, tiled=True)  11.6 us
    ppermute x6, waiting for transfers between devices, swap(): lax.ppermute(values, axis, [(i, i ^ bit) for i in range(lax.axis_size(axi...  11.3 us
    ppermute x6, starting transfers between devices, swap(): lax.ppermute(values, axis, [(i, i ^ bit) for i in range(lax.axis_size(axi...  8.21 us
    pallas_call x1, Pallas kernels, local(): pl.pallas_call(fifth_kernel, out_shape=[jax.ShapeDtypeStruct((2 * slots,...  7.59 us
    ppermute x4, starting transfers between devices, blk_halves(): parts.append(lax.ppermute(values, ('blk', 'zero'), pairs))  7.36 us
    pallas_call x1, Pallas kernels, local(): pl.pallas_call(functools.partial(owner_kernel, slots, entries), out_shape...  6.83 us
  transfers between devices with their start and end apart: 11, of which 9 were waited for; matrix products, arithmetic and copies ran while one was open for 0% of the time, Pallas kernels for 6%

profile of v7, /device:TPU:4, one launch (start us, length us, event | category | flops | bytes accessed | tf_op | source)
XLA Modules:
  0.0 119.8 jit_solution(12701538378923114228)
XLA Ops:
  0.6 4.0 %pack.1 = (bf16[32,264,128]{2,1,0:T(8,128)(2,1)}, s32[172]{0:T(256)}, s32[4]{0:T(128)}) custom-call(s32[1]{0:T(128)} %bitcast.me_ref, s32[24]{0:T(128)} %bitcast.19, bf16[2,16,6144]{2,1,0:T(8,128)(2,1)} %grads_hbm.3, f32[24,16,512]{2,1,0:T(8,128)} %bitcast.11, f32[24,16,512]{2,1,0:T(8,128)} %bitcast.13), custom_call_target="tpu_custom_call" | custom-call | tf_op jit(solution)/shard_map/pack/pallas_call | solution.py:596
  4.6 11.6 %all-to-all-start = ((bf16[32,264,128]{2,1,0:T(8,128)(2,1)}), bf16[32,264,128]{2,1,0:T(8,128)(2,1)}, u32[]{:S(2)}, u32[]{:S(2)}) async-start(bf16[32,264,128]{2,1,0:T(8,128)(2,1)} %get-tuple-element.18.__), calls=%async_computation | async-start | bytes 4325376 | tf_op jit(solution)/shard_map/all_to_all | solution.py:573
  16.2 0.0 copy-start.10
  16.2 1.6 %copy-done.10 = bf16[1,2,2,512,512]{4,3,2,1,0:T(8,128)(2,1)S(1)} copy-done((bf16[1,2,2,512,512]{4,3,2,1,0:T(8,128)(2,1)S(1)}, bf16[1,2,2,512,512]{4,3,2,1,0:T(8,128)(2,1)}, u32[]{:S(2)}) %copy-start.10) | copy-done | bytes 2097176
  17.8 7.6 %fifth.1 = (bf16[4,512,512]{2,1,0:T(8,128)(2,1)S(1)}, f32[4,512,128]{2,1,0:T(8,128)S(1)}) custom-call(bf16[4,512,512]{2,1,0:T(8,128)(2,1)S(1)} %bitcast.17), custom_call_target="tpu_custom_call" | custom-call | flops 6442450944 | bytes 6291456 | tf_op jit(solution)/shard_map/fifth/pallas_call | solution.py:618
  25.4 0.0 copy-start.3
  25.4 0.0 copy-start.11
  25.5 0.0 copy-done
  25.5 0.0 copy-done.4
  25.5 0.1 square.1
  25.6 1.2 copy-done.3
  26.8 0.3 copy-done.11
  27.1 0.0 collective-permute-start
  27.1 1.2 collective-permute-done
  28.3 1.2 collective-permute-start.1
  29.5 2.4 %collective-permute-done.1 = f32[8,128]{1,0:T(8,128)S(1)} collective-permute-done((f32[8,128]{1,0:T(8,128)S(1)}, f32[8,128]{1,0:T(8,128)S(1)}, u32[]{:S(2)}, u32[]{:S(2)}) %collective-permute-start.1) | collective-permute-done | bytes 4128 | tf_op jit(solution)/shard_map/ppermute | solution.py:547
  31.9 0.5 collective-permute-start.2
  32.4 3.1 %collective-permute-done.2 = f32[8,128]{1,0:T(8,128)S(1)} collective-permute-done((f32[8,128]{1,0:T(8,128)S(1)}, f32[8,128]{1,0:T(8,128)S(1)}, u32[]{:S(2)}, u32[]{:S(2)}) %collective-permute-start.2) | collective-permute-done | bytes 4128 | tf_op jit(solution)/shard_map/ppermute | solution.py:547
  35.5 1.7 %collective-permute-start.3 = (f32[8,128]{1,0:T(8,128)S(1)}, f32[8,128]{1,0:T(8,128)S(1)}, u32[]{:S(2)}, u32[]{:S(2)}) collective-permute-start(f32[8,128]{1,0:T(8,128)S(1)} %add.26), channel_id=1, source_target_pairs={{0,8},{8,0},{16,24},{24,16},{32,40},{40,32},{48,56},{56,48},{64,72... | collective-permute-start | bytes 12296 | tf_op jit(solution)/shard_map/ppermute | solution.py:547
  37.2 1.9 %collective-permute-done.3 = f32[8,128]{1,0:T(8,128)S(1)} collective-permute-done((f32[8,128]{1,0:T(8,128)S(1)}, f32[8,128]{1,0:T(8,128)S(1)}, u32[]{:S(2)}, u32[]{:S(2)}) %collective-permute-start.3) | collective-permute-done | bytes 4128 | tf_op jit(solution)/shard_map/ppermute | solution.py:547
  39.1 2.9 %collective-permute-start.4 = (f32[8,128]{1,0:T(8,128)S(1)}, f32[8,128]{1,0:T(8,128)S(1)}, u32[]{:S(2)}, u32[]{:S(2)}) collective-permute-start(f32[8,128]{1,0:T(8,128)S(1)} %add.27), channel_id=1, source_target_pairs={{0,24},{8,16},{16,8},{24,0},{32,56},{40,48},{48,40},{56,32},{64,88... | collective-permute-start | bytes 12296 | tf_op jit(solution)/shard_map/ppermute | solution.py:547
  42.0 1.9 %collective-permute-done.4 = f32[8,128]{1,0:T(8,128)S(1)} collective-permute-done((f32[8,128]{1,0:T(8,128)S(1)}, f32[8,128]{1,0:T(8,128)S(1)}, u32[]{:S(2)}, u32[]{:S(2)}) %collective-permute-start.4) | collective-permute-done | bytes 4128 | tf_op jit(solution)/shard_map/ppermute | solution.py:547
  44.0 4.7 %collective-permute-start.8 = (f32[8,128]{1,0:T(8,128)S(1)}, f32[8,128]{1,0:T(8,128)S(1)}, u32[]{:S(2)}, u32[]{:S(2)}) collective-permute-start(f32[8,128]{1,0:T(8,128)S(1)} %add.28), channel_id=1, source_target_pairs={{96,0},{225,1},{98,2},{227,3},{100,4},{229,5},{102,6},{231,7},{104... | collective-permute-start | bytes 12296 | tf_op jit(solution)/shard_map/ppermute | solution.py:567
  48.7 1.5 %collective-permute-start.7 = (f32[8,128]{1,0:T(8,128)S(1)}, f32[8,128]{1,0:T(8,128)S(1)}, u32[]{:S(2)}, u32[]{:S(2)}) collective-permute-start(f32[8,128]{1,0:T(8,128)S(1)} %add.28), channel_id=1, source_target_pairs={{64,0},{193,1},{66,2},{195,3},{68,4},{197,5},{70,6},{199,7},{72,8}... | collective-permute-start | bytes 12296 | tf_op jit(solution)/shard_map/ppermute | solution.py:567
  50.2 0.5 collective-permute-start.6
  50.7 0.6 collective-permute-start.5
  51.4 13.2 %collective-permute-done.8 = f32[8,128]{1,0:T(8,128)S(1)} collective-permute-done((f32[8,128]{1,0:T(8,128)S(1)}, f32[8,128]{1,0:T(8,128)S(1)}, u32[]{:S(2)}, u32[]{:S(2)}) %collective-permute-start.8) | collective-permute-done | bytes 4128 | tf_op jit(solution)/shard_map/ppermute | solution.py:567
  64.6 0.0 collective-permute-done.7
  64.6 0.3 collective-permute-done.6
  64.8 0.0 collective-permute-done.5
  64.8 0.0 copy-start.5
  64.9 1.8 %collective-permute-start.9 = (f32[8,128]{1,0:T(8,128)S(1)}, f32[8,128]{1,0:T(8,128)S(1)}, u32[]{:S(2)}, u32[]{:S(2)}) collective-permute-start(f32[8,128]{1,0:T(8,128)S(1)} %add_add_fusion.half_ref), channel_id=1, source_target_pairs={{0,1},{1,0},{2,3},{3,2},{4,5},{5,4},{6,7},{7,6},{8,9},{9,8},{10,11... | collective-permute-start | bytes 12296 | tf_op jit(solution)/shard_map/ppermute | solution.py:547
  66.7 0.8 collective-permute-done.9.other_ref
  67.5 0.5 all-to-all-done.arrived_hbm
  68.0 0.0 copy-done.5
  68.0 0.1 copy-done.7
  68.1 6.8 %owner.1 = (bf16[2,2,512,512]{3,2,1,0:T(8,128)(2,1)}, bf16[32,152,128]{2,1,0:T(8,128)(2,1)}, f32[2,16,6144]{2,1,0:T(8,128)}) custom-call(s32[4]{0:T(128)} %get-tuple-element.19.role_ref, f32[8,128]{1,0:T(8,128)} %copy-done.5, f32[8,128]{1,0:T(8,128)} %copy-done.7, bf16[2,16,6144]{2,1,0:T(8,128)(2,1)} %grads_hbm.3, f32[2,16,6144]{2,1,0:T(8,128)} %second_hbm.1, ...), custom_call_target="tpu_custom_call" | custom-call | flops 4294967296 | bytes 12582912 | tf_op jit(solution)/shard_map/owner/pallas_call | solution.py:644
  75.0 0.0 copy-start.1
  75.0 0.0 copy-start.2
  75.0 0.0 copy-start.6
  75.0 0.0 copy-start.8
  75.0 0.0 copy-start.9
  75.0 42.6 %all_to_all.10.back_ref = bf16[32,152,128]{2,1,0:T(8,128)(2,1)S(1)} all-to-all(bf16[32,152,128]{2,1,0:T(8,128)(2,1)} %get-tuple-element.21), channel_id=1, replica_groups=mesh['blk'=32,'zero'=8] {'blk'}, dimensions={0} | all-to-all | bytes 2490368 | tf_op jit(solution)/shard_map/all_to_all | solution.py:573
  117.7 0.0 copy-done.1
  117.7 0.0 copy-done.2
  117.7 0.0 copy-done.8
  117.7 0.0 copy-done.9
  117.7 2.1 %finish.1 = (bf16[2,16,6144]{2,1,0:T(8,128)(2,1)}, f32[24,16,512]{2,1,0:T(8,128)}, f32[24,16,512]{2,1,0:T(8,128)}) custom-call(s32[172]{0:T(256)S(1)} %copy-done.9, f32[8,128]{1,0:T(8,128)S(1)} %copy-done.6, f32[8,128]{1,0:T(8,128)S(1)} %copy-done.8, f32[24,16,512]{2,1,0:T(8,128)S(1)} %bitcast.12, f32[24,16,512]{2,1,0:T(8,128)S(1)} %bitcast.14, ...), custom_call_target="tpu_custom_call" | custom-call | tf_op jit(solution)/shard_map/finish/pallas_call | solution.py:672
  (10 shorter events, 0.0 us)
Async XLA Ops:
  4.6 63.4 %all-to-all-start = ((bf16[32,264,128]{2,1,0:T(8,128)(2,1)}), bf16[32,264,128]{2,1,0:T(8,128)(2,1)}, u32[]{:S(2)}, u32[]{:S(2)}) async-start(bf16[32,264,128]{2,1,0:T(8,128)(2,1)} %get-tuple-element.18.__), calls=%async_computation | async-start | bytes 4325376 | tf_op jit(solution)/shard_map/all_to_all | solution.py:573
  16.2 1.6 %copy-start.10 = (bf16[1,2,2,512,512]{4,3,2,1,0:T(8,128)(2,1)S(1)}, bf16[1,2,2,512,512]{4,3,2,1,0:T(8,128)(2,1)}, u32[]{:S(2)}) copy-start(bf16[1,2,2,512,512]{4,3,2,1,0:T(8,128)(2,1)} %param.11) | copy-start | bytes 6291460
  17.8 7.6 %copy-start = (bf16[32,264,128]{2,1,0:T(8,128)(2,1)S(1)}, bf16[32,264,128]{2,1,0:T(8,128)(2,1)}, u32[]{:S(2)}) copy-start(bf16[32,264,128]{2,1,0:T(8,128)(2,1)} %get-tuple-element.18.__) | copy-start | bytes 6488068
  17.8 7.6 %copy-start.4 = (bf16[2,16,6144]{2,1,0:T(8,128)(2,1)S(1)}, bf16[2,16,6144]{2,1,0:T(8,128)(2,1)}, u32[]{:S(2)}) copy-start(bf16[2,16,6144]{2,1,0:T(8,128)(2,1)} %grads_hbm.3) | copy-start | bytes 1179652
  25.4 1.4 %copy-start.3 = (bf16[4,512,512]{2,1,0:T(8,128)(2,1)}, bf16[4,512,512]{2,1,0:T(8,128)(2,1)S(1)}, u32[]{:S(2)}) copy-start(bf16[4,512,512]{2,1,0:T(8,128)(2,1)S(1)} %get-tuple-element.17._) | copy-start | bytes 6291460
  25.4 1.7 %copy-start.11 = (f32[4,512,128]{2,1,0:T(8,128)}, f32[4,512,128]{2,1,0:T(8,128)S(1)}, u32[]{:S(2)}) copy-start(f32[4,512,128]{2,1,0:T(8,128)S(1)} %get-tuple-element.20) | copy-start | bytes 3145732
  27.1 1.2 collective-permute-start
  28.3 3.6 %collective-permute-start.1 = (f32[8,128]{1,0:T(8,128)S(1)}, f32[8,128]{1,0:T(8,128)S(1)}, u32[]{:S(2)}, u32[]{:S(2)}) collective-permute-start(f32[8,128]{1,0:T(8,128)S(1)} %add.24), channel_id=1, source_target_pairs={{0,2},{1,3},{2,0},{3,1},{4,6},{5,7},{6,4},{7,5},{8,10},{9,11},{10,... | collective-permute-start | bytes 12296 | tf_op jit(solution)/shard_map/ppermute | solution.py:547
  31.9 3.6 %collective-permute-start.2 = (f32[8,128]{1,0:T(8,128)S(1)}, f32[8,128]{1,0:T(8,128)S(1)}, u32[]{:S(2)}, u32[]{:S(2)}) collective-permute-start(f32[8,128]{1,0:T(8,128)S(1)} %add.25), channel_id=1, source_target_pairs={{0,6},{1,7},{2,4},{3,5},{4,2},{5,3},{6,0},{7,1},{8,14},{9,15},{10,... | collective-permute-start | bytes 12296 | tf_op jit(solution)/shard_map/ppermute | solution.py:547
  35.5 3.6 %collective-permute-start.3 = (f32[8,128]{1,0:T(8,128)S(1)}, f32[8,128]{1,0:T(8,128)S(1)}, u32[]{:S(2)}, u32[]{:S(2)}) collective-permute-start(f32[8,128]{1,0:T(8,128)S(1)} %add.26), channel_id=1, source_target_pairs={{0,8},{8,0},{16,24},{24,16},{32,40},{40,32},{48,56},{56,48},{64,72... | collective-permute-start | bytes 12296 | tf_op jit(solution)/shard_map/ppermute | solution.py:547
  39.1 4.9 %collective-permute-start.4 = (f32[8,128]{1,0:T(8,128)S(1)}, f32[8,128]{1,0:T(8,128)S(1)}, u32[]{:S(2)}, u32[]{:S(2)}) collective-permute-start(f32[8,128]{1,0:T(8,128)S(1)} %add.27), channel_id=1, source_target_pairs={{0,24},{8,16},{16,8},{24,0},{32,56},{40,48},{48,40},{56,32},{64,88... | collective-permute-start | bytes 12296 | tf_op jit(solution)/shard_map/ppermute | solution.py:547
  44.0 20.6 %collective-permute-start.8 = (f32[8,128]{1,0:T(8,128)S(1)}, f32[8,128]{1,0:T(8,128)S(1)}, u32[]{:S(2)}, u32[]{:S(2)}) collective-permute-start(f32[8,128]{1,0:T(8,128)S(1)} %add.28), channel_id=1, source_target_pairs={{96,0},{225,1},{98,2},{227,3},{100,4},{229,5},{102,6},{231,7},{104... | collective-permute-start | bytes 12296 | tf_op jit(solution)/shard_map/ppermute | solution.py:567
  48.7 15.9 %collective-permute-start.7 = (f32[8,128]{1,0:T(8,128)S(1)}, f32[8,128]{1,0:T(8,128)S(1)}, u32[]{:S(2)}, u32[]{:S(2)}) collective-permute-start(f32[8,128]{1,0:T(8,128)S(1)} %add.28), channel_id=1, source_target_pairs={{64,0},{193,1},{66,2},{195,3},{68,4},{197,5},{70,6},{199,7},{72,8}... | collective-permute-start | bytes 12296 | tf_op jit(solution)/shard_map/ppermute | solution.py:567
  50.2 14.7 %collective-permute-start.6 = (f32[8,128]{1,0:T(8,128)S(1)}, f32[8,128]{1,0:T(8,128)S(1)}, u32[]{:S(2)}, u32[]{:S(2)}) collective-permute-start(f32[8,128]{1,0:T(8,128)S(1)} %add.28), channel_id=1, source_target_pairs={{32,0},{161,1},{34,2},{163,3},{36,4},{165,5},{38,6},{167,7},{40,8}... | collective-permute-start | bytes 12296 | tf_op jit(solution)/shard_map/ppermute | solution.py:567
  50.7 14.1 %collective-permute-start.5 = (f32[8,128]{1,0:T(8,128)S(1)}, f32[8,128]{1,0:T(8,128)S(1)}, u32[]{:S(2)}, u32[]{:S(2)}) collective-permute-start(f32[8,128]{1,0:T(8,128)S(1)} %add.28), channel_id=1, source_target_pairs={{0,0},{129,1},{2,2},{131,3},{4,4},{133,5},{6,6},{135,7},{8,8},{137... | collective-permute-start | bytes 12296 | tf_op jit(solution)/shard_map/ppermute | solution.py:567
  64.8 3.2 %copy-start.5 = (f32[8,128]{1,0:T(8,128)}, f32[8,128]{1,0:T(8,128)S(1)}, u32[]{:S(2)}) copy-start(f32[8,128]{1,0:T(8,128)S(1)} %add_add_fusion.half_ref) | copy-start | bytes 12292
  64.9 2.7 %collective-permute-start.9 = (f32[8,128]{1,0:T(8,128)S(1)}, f32[8,128]{1,0:T(8,128)S(1)}, u32[]{:S(2)}, u32[]{:S(2)}) collective-permute-start(f32[8,128]{1,0:T(8,128)S(1)} %add_add_fusion.half_ref), channel_id=1, source_target_pairs={{0,1},{1,0},{2,3},{3,2},{4,5},{5,4},{6,7},{7,6},{8,9},{9,8},{10,11... | collective-permute-start | bytes 12296 | tf_op jit(solution)/shard_map/ppermute | solution.py:547
  67.5 0.6 copy-start.7
  75.0 42.7 %copy-start.1 = (f32[1,24,16,512]{3,2,1,0:T(8,128)S(1)}, f32[1,24,16,512]{3,2,1,0:T(8,128)}, u32[]{:S(2)}) copy-start(f32[1,24,16,512]{3,2,1,0:T(8,128)} %param.8) | copy-start | bytes 2359300
  75.0 42.7 %copy-start.2 = (f32[1,24,16,512]{3,2,1,0:T(8,128)S(1)}, f32[1,24,16,512]{3,2,1,0:T(8,128)}, u32[]{:S(2)}) copy-start(f32[1,24,16,512]{3,2,1,0:T(8,128)} %param.9) | copy-start | bytes 2359300
  75.0 42.7 %copy-start.6 = (f32[8,128]{1,0:T(8,128)S(1)}, f32[8,128]{1,0:T(8,128)}, u32[]{:S(2)}) copy-start(f32[8,128]{1,0:T(8,128)} %copy-done.5) | copy-start | bytes 12292
  75.0 42.7 %copy-start.8 = (f32[8,128]{1,0:T(8,128)S(1)}, f32[8,128]{1,0:T(8,128)}, u32[]{:S(2)}) copy-start(f32[8,128]{1,0:T(8,128)} %copy-done.7) | copy-start | bytes 12292
  75.0 42.7 %copy-start.9 = (s32[172]{0:T(256)S(1)}, s32[172]{0:T(256)}, u32[]{:S(2)}) copy-start(s32[172]{0:T(256)} %get-tuple-element.16.plan_ref) | copy-start | bytes 2068
